TPU v7x, 32 devices: a whole 2x2x4 slice. The times are simulated.
32 devices in a mesh: dp: 4 (over y, core), fsdp: 8 (over z, x).
Axes of the slice: x: 2, y: 2, z: 4, core: 2. Of those that a mesh axis runs over, the one named last changes fastest.
Arguments:
- tokens: bfloat16 [12608, 768], P(('dp', 'fsdp')), may hold values from -6 to 6
- masked_rows: int32 [64, 196], P(('dp', 'fsdp')), may hold values from -1 to 196, as said below
- cotangent: bfloat16 [12608, 768], P(('dp', 'fsdp')), may hold values from -6 to 6
- norm1_gain: bfloat16 [2, 768], P(None, ('dp', 'fsdp')), may hold values from 0.099609375 to 1.8984375
- norm1_bias: bfloat16 [2, 768], P(None, ('dp', 'fsdp')), may hold values from -3 to 3
- qkv_weight: bfloat16 [2, 768, 2304], P(None, ('dp', 'fsdp')), may hold values from -0.21875 to 0.21875
- q_bias: bfloat16 [2, 768], P(None, ('dp', 'fsdp')), may hold values from -3 to 3
- v_bias: bfloat16 [2, 768], P(None, ('dp', 'fsdp')), may hold values from -3 to 3
- proj_weight: bfloat16 [2, 768, 768], P(None, ('dp', 'fsdp')), may hold values from -0.625 to 0.625
- proj_bias: bfloat16 [2, 768], P(None, ('dp', 'fsdp')), may hold values from -2 to 2
- gamma_attn: bfloat16 [2, 768], P(None, ('dp', 'fsdp')), may hold values from 0.5 to 1.5
- norm2_gain: bfloat16 [2, 768], P(None, ('dp', 'fsdp')), may hold values from 0.099609375 to 1.8984375
- norm2_bias: bfloat16 [2, 768], P(None, ('dp', 'fsdp')), may hold values from -3 to 3
- fc1_weight: bfloat16 [2, 768, 3072], P(None, ('dp', 'fsdp')), may hold values from -0.21875 to 0.21875
- fc1_bias: bfloat16 [2, 3072], P(None, ('dp', 'fsdp')), may hold values from -3 to 3
- fc2_weight: bfloat16 [2, 3072, 768], P(None, ('dp', 'fsdp')), may hold values from -0.109375 to 0.109375
- fc2_bias: bfloat16 [2, 768], P(None, ('dp', 'fsdp')), may hold values from -2 to 2
- gamma_mlp: bfloat16 [2, 768], P(None, ('dp', 'fsdp')), may hold values from 0.5 to 1.5
- rel_table: bfloat16 [2, 12, 736], P(None, None, ('dp', 'fsdp')), may hold values from -5 to 5
Outputs:
- encoded: bfloat16 [12608, 768], P(('dp', 'fsdp'))
- tokens_grad: float32 [12608, 768], P(('dp', 'fsdp'))
- grad_norm1_gain: float32 [2, 768], P(None, ('dp', 'fsdp'))
- grad_norm1_bias: float32 [2, 768], P(None, ('dp', 'fsdp'))
- grad_qkv_weight: float32 [2, 768, 2304], P(None, ('dp', 'fsdp'))
- grad_q_bias: float32 [2, 768], P(None, ('dp', 'fsdp'))
- grad_v_bias: float32 [2, 768], P(None, ('dp', 'fsdp'))
- grad_proj_weight: float32 [2, 768, 768], P(None, ('dp', 'fsdp'))
- grad_proj_bias: float32 [2, 768], P(None, ('dp', 'fsdp'))
- grad_gamma_attn: float32 [2, 768], P(None, ('dp', 'fsdp'))
- grad_norm2_gain: float32 [2, 768], P(None, ('dp', 'fsdp'))
- grad_norm2_bias: float32 [2, 768], P(None, ('dp', 'fsdp'))
- grad_fc1_weight: float32 [2, 768, 3072], P(None, ('dp', 'fsdp'))
- grad_fc1_bias: float32 [2, 3072], P(None, ('dp', 'fsdp'))
- grad_fc2_weight: float32 [2, 3072, 768], P(None, ('dp', 'fsdp'))
- grad_fc2_bias: float32 [2, 768], P(None, ('dp', 'fsdp'))
- grad_gamma_mlp: float32 [2, 768], P(None, ('dp', 'fsdp'))
- grad_rel_table: float32 [2, 12, 736], P(None, None, ('dp', 'fsdp'))
Inputs may be any that keep to these rules, and one draw needn't show every extreme that they name: `masked_rows`: each image lists its masked patches first, distinct, then -1 to the end; some image has all 196 patches masked, and row 0 is never listed.
All inputs are finite; a program needn't handle non-finite values.
Results may differ from a plain program's by a relative error of at most 0.015.
Values may be sent and summed in bfloat16 or wider, within the bound.
No kernel may reach another device: no remote copies, remote signals or barrier semaphores. Data moves between devices by JAX's collectives and lax.ppermute only.
A program may use at most 256 MiB of HBM per device.

v0:
```python
import jax
import jax.numpy as jnp
import numpy as np
from jax import lax
from jax.sharding import PartitionSpec as P

GRID = 14
LAYERS = 2


F32 = jnp.float32
B16 = jnp.bfloat16


def rel_index(grid):
    rows = np.arange(grid)
    coords = np.stack(np.meshgrid(rows, rows, indexing="ij")).reshape(2, -1)
    offsets = coords[:, :, None] - coords[:, None, :] + grid - 1
    count = (2 * grid - 1) * (2 * grid - 1) + 3
    table_idx = np.zeros((grid * grid + 1, grid * grid + 1), np.int32)
    table_idx[1:, 1:] = offsets[0] * (2 * grid - 1) + offsets[1]
    table_idx[0, :] = count - 3
    table_idx[:, 0] = count - 2
    table_idx[0, 0] = count - 1
    return table_idx


def layer_norm(values, gain, shift):
    centered = values - jnp.mean(values, -1, keepdims=True)
    variance = jnp.mean(centered * centered, -1, keepdims=True)
    return centered * lax.rsqrt(variance + 1e-06) * gain + shift


def softmax_rows(scores):
    return jax.nn.softmax(scores, -1)


def gelu_exact(pre):
    return jax.nn.gelu(pre, approximate=False)


def layer_forward(inputs, weights, index):
    (
        n1_gain,
        n1_shift,
        w_qkv,
        query_bias,
        value_bias,
        w_proj,
        b_proj,
        g_attn,
        n2_gain,
        n2_shift,
        w_one,
        b_one,
        w_two,
        b_two,
        g_mlp,
        table,
    ) = weights
    batch, length, width = inputs.shape
    heads = table.shape[0]
    size = width // heads
    hidden = layer_norm(inputs, n1_gain.astype(F32), n1_shift.astype(F32)).astype(B16)
    qkv_bias = jnp.concatenate(
        [query_bias.astype(F32), jnp.zeros((width,), F32), value_bias.astype(F32)]
    )
    qkv = (jnp.einsum("bnd,de->bne", hidden, w_qkv, preferred_element_type=F32) + qkv_bias).astype(
        B16
    )
    qkv = qkv.reshape(batch, length, 3, heads, size)
    query, keys, values = (qkv[:, :, 0], qkv[:, :, 1], qkv[:, :, 2])
    bias = table.astype(F32)[:, index]
    scores = (
        jnp.einsum("bqhe,bkhe->bhqk", query, keys, preferred_element_type=F32) * size ** (-0.5)
        + bias[None]
    )
    probs_full = softmax_rows(scores)
    probs = probs_full.astype(B16)
    attended = (
        jnp.einsum("bhqk,bkhe->bqhe", probs, values, preferred_element_type=F32)
        .reshape(batch, length, width)
        .astype(B16)
    )
    branch = jnp.einsum(
        "bnd,de->bne", attended, w_proj, preferred_element_type=F32
    ) + b_proj.astype(F32)
    middle = inputs + g_attn.astype(F32) * branch
    hidden_two = layer_norm(middle, n2_gain.astype(F32), n2_shift.astype(F32)).astype(B16)
    pre = jnp.einsum("bnd,df->bnf", hidden_two, w_one, preferred_element_type=F32) + b_one.astype(
        F32
    )
    active = gelu_exact(pre).astype(B16)
    mlp_out = jnp.einsum("bnf,fd->bnd", active, w_two, preferred_element_type=F32) + b_two.astype(
        F32
    )
    output = middle + g_mlp.astype(F32) * mlp_out
    saved = (
        hidden,
        query,
        keys,
        values,
        scores,
        probs,
        attended,
        branch,
        middle,
        hidden_two,
        pre,
        active,
        mlp_out,
    )
    return (output, saved)


def layer_backward(inputs, weights, index, grad_out):
    (
        n1_gain,
        n1_shift,
        w_qkv,
        query_bias,
        value_bias,
        w_proj,
        b_proj,
        g_attn,
        n2_gain,
        n2_shift,
        w_one,
        b_one,
        w_two,
        b_two,
        g_mlp,
        table,
    ) = weights
    batch, length, width = inputs.shape
    heads = table.shape[0]
    size = width // heads
    _, saved = layer_forward(inputs, weights, index)
    (
        hidden,
        query,
        keys,
        values,
        scores,
        probs,
        attended,
        branch,
        middle,
        hidden_two,
        pre,
        active,
        mlp_out,
    ) = saved
    over_rows = (0, 1)
    grad_g_mlp = jnp.sum(grad_out * mlp_out, over_rows)
    grad_mlp = (grad_out * g_mlp.astype(F32)).astype(B16)
    grad_b_two = jnp.sum(grad_mlp.astype(F32), over_rows)
    grad_w_two = jnp.einsum("bnf,bnd->fd", active, grad_mlp, preferred_element_type=F32)
    grad_active = jnp.einsum("bnd,fd->bnf", grad_mlp, w_two, preferred_element_type=F32)
    _, gelu_pull = jax.vjp(gelu_exact, pre)
    grad_pre = gelu_pull(grad_active)[0].astype(B16)
    grad_b_one = jnp.sum(grad_pre.astype(F32), over_rows)
    grad_w_one = jnp.einsum("bnd,bnf->df", hidden_two, grad_pre, preferred_element_type=F32)
    grad_hidden_two = jnp.einsum("bnf,df->bnd", grad_pre, w_one, preferred_element_type=F32)
    _, norm_two_pull = jax.vjp(layer_norm, middle, n2_gain.astype(F32), n2_shift.astype(F32))
    grad_middle_norm, grad_n2_gain, grad_n2_shift = norm_two_pull(grad_hidden_two)
    grad_middle = grad_out + grad_middle_norm
    grad_g_attn = jnp.sum(grad_middle * branch, over_rows)
    grad_branch = (grad_middle * g_attn.astype(F32)).astype(B16)
    grad_b_proj = jnp.sum(grad_branch.astype(F32), over_rows)
    grad_w_proj = jnp.einsum("bnd,bne->de", attended, grad_branch, preferred_element_type=F32)
    grad_attended = jnp.einsum(
        "bne,de->bnd", grad_branch, w_proj, preferred_element_type=F32
    ).astype(B16)
    grad_attended = grad_attended.reshape(batch, length, heads, size)
    grad_probs = jnp.einsum("bqhe,bkhe->bhqk", grad_attended, values, preferred_element_type=F32)
    grad_values = jnp.einsum("bhqk,bqhe->bkhe", probs, grad_attended, preferred_element_type=F32)
    _, soft_pull = jax.vjp(softmax_rows, scores)
    grad_scores = soft_pull(grad_probs)[0].astype(B16)
    score_sum = jnp.sum(grad_scores.astype(F32), 0).reshape(heads, length * length)
    grad_table = jax.ops.segment_sum(
        jnp.transpose(score_sum), index.reshape(-1), num_segments=table.shape[1]
    )
    grad_table = jnp.transpose(grad_table)
    grad_query = jnp.einsum(
        "bhqk,bkhe->bqhe", grad_scores, keys, preferred_element_type=F32
    ) * size ** (-0.5)
    grad_keys = jnp.einsum(
        "bhqk,bqhe->bkhe", grad_scores, query, preferred_element_type=F32
    ) * size ** (-0.5)
    grad_qkv = (
        jnp.stack([grad_query, grad_keys, grad_values], axis=2)
        .reshape(batch, length, 3 * width)
        .astype(B16)
    )
    qkv_sums = jnp.sum(grad_qkv.astype(F32), over_rows)
    grad_query_bias = qkv_sums[:width]
    grad_value_bias = qkv_sums[2 * width :]
    grad_w_qkv = jnp.einsum("bnd,bne->de", hidden, grad_qkv, preferred_element_type=F32)
    grad_hidden = jnp.einsum("bne,de->bnd", grad_qkv, w_qkv, preferred_element_type=F32)
    _, norm_one_pull = jax.vjp(layer_norm, inputs, n1_gain.astype(F32), n1_shift.astype(F32))
    grad_inputs_norm, grad_n1_gain, grad_n1_shift = norm_one_pull(grad_hidden)
    grad_inputs = grad_middle + grad_inputs_norm
    grads = (
        grad_n1_gain,
        grad_n1_shift,
        grad_w_qkv,
        grad_query_bias,
        grad_value_bias,
        grad_w_proj,
        grad_b_proj,
        grad_g_attn,
        grad_n2_gain,
        grad_n2_shift,
        grad_w_one,
        grad_b_one,
        grad_w_two,
        grad_b_two,
        grad_g_mlp,
        grad_table,
    )
    return (grad_inputs, grads)


def fetch_forward(parts):
    return (
        lax.all_gather(parts[0], ("dp", "fsdp"), axis=0, tiled=True),
        lax.all_gather(parts[1], ("dp", "fsdp"), axis=0, tiled=True),
        lax.all_gather(parts[2], ("dp", "fsdp"), axis=0, tiled=True),
        lax.all_gather(parts[3], ("dp", "fsdp"), axis=0, tiled=True),
        lax.all_gather(parts[4], ("dp", "fsdp"), axis=0, tiled=True),
        lax.all_gather(parts[5], ("dp", "fsdp"), axis=0, tiled=True),
        lax.all_gather(parts[6], ("dp", "fsdp"), axis=0, tiled=True),
        lax.all_gather(parts[7], ("dp", "fsdp"), axis=0, tiled=True),
        lax.all_gather(parts[8], ("dp", "fsdp"), axis=0, tiled=True),
        lax.all_gather(parts[9], ("dp", "fsdp"), axis=0, tiled=True),
        lax.all_gather(parts[10], ("dp", "fsdp"), axis=0, tiled=True),
        lax.all_gather(parts[11], ("dp", "fsdp"), axis=0, tiled=True),
        lax.all_gather(parts[12], ("dp", "fsdp"), axis=0, tiled=True),
        lax.all_gather(parts[13], ("dp", "fsdp"), axis=0, tiled=True),
        lax.all_gather(parts[14], ("dp", "fsdp"), axis=0, tiled=True),
        lax.all_gather(parts[15], ("dp", "fsdp"), axis=1, tiled=True),
    )


def fetch_backward(parts):
    return (
        lax.all_gather(parts[0], ("dp", "fsdp"), axis=0, tiled=True),
        lax.all_gather(parts[1], ("dp", "fsdp"), axis=0, tiled=True),
        lax.all_gather(parts[2], ("dp", "fsdp"), axis=0, tiled=True),
        lax.all_gather(parts[3], ("dp", "fsdp"), axis=0, tiled=True),
        lax.all_gather(parts[4], ("dp", "fsdp"), axis=0, tiled=True),
        lax.all_gather(parts[5], ("dp", "fsdp"), axis=0, tiled=True),
        lax.all_gather(parts[6], ("dp", "fsdp"), axis=0, tiled=True),
        lax.all_gather(parts[7], ("dp", "fsdp"), axis=0, tiled=True),
        lax.all_gather(parts[8], ("dp", "fsdp"), axis=0, tiled=True),
        lax.all_gather(parts[9], ("dp", "fsdp"), axis=0, tiled=True),
        lax.all_gather(parts[10], ("dp", "fsdp"), axis=0, tiled=True),
        lax.all_gather(parts[11], ("dp", "fsdp"), axis=0, tiled=True),
        lax.all_gather(parts[12], ("dp", "fsdp"), axis=0, tiled=True),
        lax.all_gather(parts[13], ("dp", "fsdp"), axis=0, tiled=True),
        lax.all_gather(parts[14], ("dp", "fsdp"), axis=0, tiled=True),
        lax.all_gather(parts[15], ("dp", "fsdp"), axis=1, tiled=True),
    )


def reduce_grads(terms):
    return (
        lax.psum_scatter(terms[0], ("dp", "fsdp"), scatter_dimension=0, tiled=True),
        lax.psum_scatter(terms[1], ("dp", "fsdp"), scatter_dimension=0, tiled=True),
        lax.psum_scatter(terms[2], ("dp", "fsdp"), scatter_dimension=0, tiled=True),
        lax.psum_scatter(terms[3], ("dp", "fsdp"), scatter_dimension=0, tiled=True),
        lax.psum_scatter(terms[4], ("dp", "fsdp"), scatter_dimension=0, tiled=True),
        lax.psum_scatter(terms[5], ("dp", "fsdp"), scatter_dimension=0, tiled=True),
        lax.psum_scatter(terms[6], ("dp", "fsdp"), scatter_dimension=0, tiled=True),
        lax.psum_scatter(terms[7], ("dp", "fsdp"), scatter_dimension=0, tiled=True),
        lax.psum_scatter(terms[8], ("dp", "fsdp"), scatter_dimension=0, tiled=True),
        lax.psum_scatter(terms[9], ("dp", "fsdp"), scatter_dimension=0, tiled=True),
        lax.psum_scatter(terms[10], ("dp", "fsdp"), scatter_dimension=0, tiled=True),
        lax.psum_scatter(terms[11], ("dp", "fsdp"), scatter_dimension=0, tiled=True),
        lax.psum_scatter(terms[12], ("dp", "fsdp"), scatter_dimension=0, tiled=True),
        lax.psum_scatter(terms[13], ("dp", "fsdp"), scatter_dimension=0, tiled=True),
        lax.psum_scatter(terms[14], ("dp", "fsdp"), scatter_dimension=0, tiled=True),
        lax.psum_scatter(terms[15], ("dp", "fsdp"), scatter_dimension=1, tiled=True),
    )


def per_device(
    tokens,
    masked_rows,
    cotangent,
    norm1_gain,
    norm1_bias,
    qkv_weight,
    q_bias,
    v_bias,
    proj_weight,
    proj_bias,
    gamma_attn,
    norm2_gain,
    norm2_bias,
    fc1_weight,
    fc1_bias,
    fc2_weight,
    fc2_bias,
    gamma_mlp,
    rel_table,
):
    shards = (
        norm1_gain,
        norm1_bias,
        qkv_weight,
        q_bias,
        v_bias,
        proj_weight,
        proj_bias,
        gamma_attn,
        norm2_gain,
        norm2_bias,
        fc1_weight,
        fc1_bias,
        fc2_weight,
        fc2_bias,
        gamma_mlp,
        rel_table,
    )
    row_count = tokens.shape[0]
    width = tokens.shape[1]
    images = masked_rows.shape[0]
    length = row_count // images
    index = jnp.asarray(rel_index(GRID))
    values = tokens.astype(F32).reshape(images, length, width)
    stored = []
    for layer_idx in range(LAYERS):
        weights = fetch_forward(tuple((s[layer_idx] for s in shards)))
        stored.append(values)
        values, _ = layer_forward(values, weights, index)
    encoded = values.reshape(row_count, width).astype(B16)
    positions = jnp.arange(length, dtype=jnp.int32)
    mask = jnp.any(masked_rows[:, :, None] == positions[None, None, :], axis=1).astype(F32)
    grad_rows = cotangent.astype(F32).reshape(images, length, width) * mask[:, :, None]
    owned = [None] * LAYERS
    for layer_idx in reversed(range(LAYERS)):
        weights = fetch_backward(tuple((s[layer_idx] for s in shards)))
        grad_rows, weight_grads = layer_backward(stored[layer_idx], weights, index, grad_rows)
        owned[layer_idx] = reduce_grads(weight_grads)
    stacked = tuple(
        (
            jnp.stack([owned[layer_idx][member] for layer_idx in range(LAYERS)])
            for member in range(16)
        )
    )
    return (encoded, grad_rows.reshape(row_count, width)) + stacked


def solution(mesh):
    return jax.shard_map(
        per_device,
        mesh=mesh,
        in_specs=(
            P(("dp", "fsdp"), None),
            P(("dp", "fsdp"), None),
            P(("dp", "fsdp"), None),
            P(None, ("dp", "fsdp")),
            P(None, ("dp", "fsdp")),
            P(None, ("dp", "fsdp"), None),
            P(None, ("dp", "fsdp")),
            P(None, ("dp", "fsdp")),
            P(None, ("dp", "fsdp"), None),
            P(None, ("dp", "fsdp")),
            P(None, ("dp", "fsdp")),
            P(None, ("dp", "fsdp")),
            P(None, ("dp", "fsdp")),
            P(None, ("dp", "fsdp"), None),
            P(None, ("dp", "fsdp")),
            P(None, ("dp", "fsdp"), None),
            P(None, ("dp", "fsdp")),
            P(None, ("dp", "fsdp")),
            P(None, None, ("dp", "fsdp")),
        ),
        out_specs=(
            P(("dp", "fsdp"), None),
            P(("dp", "fsdp"), None),
            P(None, ("dp", "fsdp")),
            P(None, ("dp", "fsdp")),
            P(None, ("dp", "fsdp"), None),
            P(None, ("dp", "fsdp")),
            P(None, ("dp", "fsdp")),
            P(None, ("dp", "fsdp"), None),
            P(None, ("dp", "fsdp")),
            P(None, ("dp", "fsdp")),
            P(None, ("dp", "fsdp")),
            P(None, ("dp", "fsdp")),
            P(None, ("dp", "fsdp"), None),
            P(None, ("dp", "fsdp")),
            P(None, ("dp", "fsdp"), None),
            P(None, ("dp", "fsdp")),
            P(None, ("dp", "fsdp")),
            P(None, None, ("dp", "fsdp")),
        ),
        check_vma=False,
    )
```

profile of v0, /device:TPU:0, one launch (start us, length us, event | category | flops | bytes accessed | tf_op | source)
XLA Modules:
  0.0 1878.3 jit_solution(2177916772215576036)
XLA Ops:
  22.5 43.6 %all-reduce.49 = (bf16[768]{0:T(1024)(128)(2,1)S(1)}, bf16[768]{0:T(1024)(128)(2,1)S(1)}, bf16[768]{0:T(1024)(128)(2,1)S(1)}, bf16[768]{0:T(1024)(128)(2,1)S(1)}...) all-reduce(bf16[768]{0:T(1024)(128)(2,1)S(1)} %dynamic-update-slice, ...), channel_id=7, replica_groups=mesh['dp'=4,'fsdp'=8] {'dp','fsdp'}, use_global_device_ids=true, to_apply=%add.4 | all-reduce | flops 21504 | bytes 86016
  67.0 68.0 %all-gather.6 = bf16[1,12,736]{1,0,2:T(2,128)(2,1)S(1)} all-gather(bf16[1,12,23]{1,0,2:T(2,128)(2,1)S(1)} %copy.203), channel_id=8, replica_groups=mesh['dp'=4,'fsdp'=8] {'dp','fsdp'}, dimensions={2}, use_global_device_ids=true | all-gather | bytes 18216 | tf_op jit(solution)/shard_map/all_gather | solution.py:242
  135.0 129.4 %gather_fusion = f32[38809,12]{1,0:T(8,128)} fusion(f32[12,736]{0,1:T(8,128)S(1)} %bitcast_convert_fusion.1, s32[38912]{0:T(1024)S(1)} %pad_clamp_fusion), kind=kCustom, calls=%fused_computation | custom fusion | bytes 3880900 | tf_op jit(solution)/shard_map/gather | solution.py:73
  264.5 12.2 copy.149
  276.7 4.1 reshape.301
  284.3 66.6 %all-gather.22 = bf16[1,12,736]{1,0,2:T(2,128)(2,1)S(1)} all-gather(bf16[1,12,23]{1,0,2:T(2,128)(2,1)S(1)} %copy.207), channel_id=24, replica_groups=mesh['dp'=4,'fsdp'=8] {'dp','fsdp'}, dimensions={2}, use_global_device_ids=true | all-gather | bytes 18216 | tf_op jit(solution)/shard_map/all_gather | solution.py:242
  350.9 129.4 %gather_fusion.1 = f32[38809,12]{1,0:T(8,128)} fusion(f32[12,736]{0,1:T(8,128)S(1)} %bitcast_convert_fusion, s32[38912]{0:T(1024)S(1)} %pad_clamp_fusion), kind=kCustom, calls=%fused_computation.1 | custom fusion | bytes 3880900 | tf_op jit(solution)/shard_map/gather | solution.py:73
  480.4 12.2 copy.159
  492.5 4.1 reshape.309
  502.2 5.0 fusion.32
  518.9 3.5 fusion.98
  523.7 6.4 fusion.58
  532.4 12.8 multiply_convert_fusion.3
  545.2 6.6 fusion.96
  553.2 5.4 fusion.33
  558.5 4.1 copy.153
  573.6 3.7 fusion.95
  578.7 6.4 fusion.59
  587.4 12.6 multiply_convert_fusion.2
  600.0 9.6 convert_reduce_fusion.2
  609.6 6.2 fusion.90
  617.4 3.8 multiply_reduce_fusion.6
  630.6 3.6 multiply_reduce_fusion.1
  648.6 7.4 convert_reduce_fusion.3
  669.9 3.6 multiply_reduce_fusion
  681.3 3.8 fusion.91
  693.8 3.5 convolution_bitcast_fusion.7
  697.4 7.0 convolution_bitcast_fusion.4
  705.9 6.7 convolution_bitcast_fusion.5
  713.8 7.0 convolution_bitcast_fusion.2
  722.1 7.0 convolution_bitcast_fusion.3
  730.3 8.1 convolution_bitcast_fusion
  739.4 7.9 convolution_bitcast_fusion.1
  750.6 3.8 reshape.294
  754.4 10.9 copy.182
  765.3 207.7 %scatter_custom_fusion.1 = f32[736,12]{1,0:T(8,128)S(1)} fusion(s32[38809]{0:T(1024)} %constant.125, f32[38809,12]{1,0:T(8,128)} %copy.182, f32[]{:T(128)} %constant.40.clone.1), kind=kCustom, calls=%fused_computation.191 | custom fusion | flops 465708 | bytes 35840 | tf_op jit(solution)/shard_map/scatter-add | solution.py:181
  976.2 3.8 reshape.293
  980.1 11.0 copy.180
  991.1 207.7 %scatter_custom_fusion = f32[736,12]{1,0:T(8,128)S(1)} fusion(s32[38809]{0:T(1024)} %constant.125, f32[38809,12]{1,0:T(8,128)} %copy.180, f32[]{:T(128)} %constant.40.clone.1), kind=kCustom, calls=%fused_computation.193 | custom fusion | flops 465708 | bytes 35840 | tf_op jit(solution)/shard_map/scatter-add | solution.py:181
  1198.8 75.5 %fusion.93 = (f32[12,32]{0,1:T(8,128)S(1)}, f32[12,32]{0,1:T(8,128)S(1)}) fusion(f32[12,736]{0,1:T(8,128)S(1)} %bitcast.357, f32[12,736]{0,1:T(8,128)S(1)} %bitcast.358), kind=kCustom, calls=%all-reduce-scatter.2 | all-reduce-scatter fusion | flops 24577 | bytes 73728
  1275.6 5.2 collective-permute-start.17
  1282.7 4.8 collective-permute-start.15
  1298.2 3.4 collective-permute-start.9
  1302.9 3.7 collective-permute-start.6
  1348.6 97.8 %reduce-scatter.23.cloned.1.call-done = f32[24,3072]{1,0:T(8,128)} async-done(((f32[768,3072]{1,0:T(8,128)}), f32[24,3072]{1,0:T(8,128)}) %reduce-scatter.23.cloned.1.call-update) | async-done | bytes 294928 | tf_op jit(solution)/shard_map/reduce_scatter | solution.py:279
  1446.4 141.3 %reduce-scatter.21.cloned.1.call-done = f32[24,3072]{1,0:T(8,128)} async-done(((f32[768,3072]{1,0:T(8,128)}), f32[24,3072]{1,0:T(8,128)}) %reduce-scatter.21.cloned.1.call-update) | async-done | bytes 294928 | tf_op jit(solution)/shard_map/reduce_scatter | solution.py:279
  1589.7 138.5 %reduce-scatter.27.cloned.1.call-done = f32[96,768]{1,0:T(8,128)} async-done(((f32[3072,768]{1,0:T(8,128)}), f32[96,768]{1,0:T(8,128)}) %reduce-scatter.27.cloned.1.call-update) | async-done | bytes 294928 | tf_op jit(solution)/shard_map/reduce_scatter | solution.py:281
  1728.1 141.4 %reduce-scatter.25.cloned.1.call-done = f32[96,768]{1,0:T(8,128)} async-done(((f32[3072,768]{1,0:T(8,128)}), f32[96,768]{1,0:T(8,128)}) %reduce-scatter.25.cloned.1.call-update) | async-done | bytes 294928 | tf_op jit(solution)/shard_map/reduce_scatter | solution.py:281
  (456 shorter events, 185.1 us)
Async XLA Ops:
  7.2 9.7 copy-start.19
  7.2 495.0 %all-gather.41.cloned.1.call-start = ((), (), s32[]{:S(2)}) async-start(), calls=%async_computation.16 | async-start | bytes 3649536 | tf_op jit(solution)/shard_map/all_gather | solution.py:229
  9.0 509.9 %all-gather.43.cloned.1.call-start = ((), (), s32[]{:S(2)}) async-start(), calls=%async_computation.17 | async-start | bytes 1216512 | tf_op jit(solution)/shard_map/all_gather | solution.py:232
  10.6 513.1 %all-gather.45.cloned.1.call-start = ((), (), s32[]{:S(2)}) async-start(), calls=%async_computation.18 | async-start | bytes 4866048 | tf_op jit(solution)/shard_map/all_gather | solution.py:237
  12.4 54.5 %copy-start.49 = (bf16[2,12,23]{2,0,1:T(2,128)(2,1)S(1)}, bf16[2,12,23]{2,0,1:T(2,128)(2,1)}, u32[]{:S(2)}) copy-start(bf16[2,12,23]{2,0,1:T(2,128)(2,1)} %param.38) | copy-start | bytes 3316
  12.4 532.8 %all-gather.47.cloned.1.call-start = ((), (), s32[]{:S(2)}) async-start(), calls=%async_computation.19 | async-start | bytes 4866048 | tf_op jit(solution)/shard_map/all_gather | solution.py:239
  14.2 539.0 %all-gather.49.cloned.1.call-start = ((), (), s32[]{:S(2)}) async-start(), calls=%async_computation.20 | async-start | bytes 3649536 | tf_op jit(solution)/shard_map/all_gather | solution.py:229
  14.8 558.8 %all-gather.51.cloned.1.call-start = ((), (), s32[]{:S(2)}) async-start(), calls=%async_computation.21 | async-start | bytes 1216512 | tf_op jit(solution)/shard_map/all_gather | solution.py:232
  15.3 119.7 %copy-start.46 = (s32[38809]{0:T(1024)S(1)}, s32[38809]{0:T(1024)}, u32[]{:S(2)}) copy-start(s32[38809]{0:T(1024)} %constant.125) | copy-start | bytes 465712
  15.4 563.3 %all-gather.53.cloned.1.call-start = ((), (), s32[]{:S(2)}) async-start(), calls=%async_computation.22 | async-start | bytes 4866048 | tf_op jit(solution)/shard_map/all_gather | solution.py:237
  16.1 583.9 %all-gather.55.cloned.1.call-start = ((), (), s32[]{:S(2)}) async-start(), calls=%async_computation.23 | async-start | bytes 4866048 | tf_op jit(solution)/shard_map/all_gather | solution.py:239
  16.9 1313.6 %all-reduce.53.cloned.1.call-start = ((), (), s32[]{:S(2)}) async-start(), calls=%async_computation.24 | async-start | bytes 212992
  17.0 485.2 %copy-start.6 = (f32[2,197,768]{2,1,0:T(8,128)}, f32[2,197,768]{2,1,0:T(8,128)S(1)}, u32[]{:S(2)}) copy-start(f32[2,197,768]{2,1,0:T(8,128)S(1)} %reshape.286) | copy-start | bytes 3631108
  17.2 49.6 %copy-start.47 = (f32[394]{0:T(512)}, f32[394]{0:T(512)S(1)}, u32[]{:S(2)}) copy-start(f32[394]{0:T(512)S(1)} %broadcast_multiply_fusion.3) | copy-start | bytes 4732
  66.8 197.7 %copy-start.50 = (f32[2,197]{1,0:T(2,128)}, f32[2,197]{1,0:T(2,128)S(1)}, u32[]{:S(2)}) copy-start(f32[2,197]{1,0:T(2,128)S(1)} %add.172) | copy-start | bytes 4732
  600.0 9.6 copy-start.15
  639.5 9.1 slice-start.6
  646.7 9.3 slice-start.8
  648.5 7.4 copy-start.43
  648.6 7.4 copy-start.9
  690.2 654.9 %reduce-scatter.19.cloned.1.call-start = ((), (), s32[]{:S(2)}) async-start(), calls=%async_computation.11 | async-start | bytes 2433024 | tf_op jit(solution)/shard_map/reduce_scatter | solution.py:274
  693.6 651.5 %reduce-scatter.17.cloned.1.call-start = ((), (), s32[]{:S(2)}) async-start(), calls=%async_computation.10 | async-start | bytes 2433024 | tf_op jit(solution)/shard_map/reduce_scatter | solution.py:274
  697.3 649.4 %reduce-scatter.15.cloned.1.call-start = ((), (), s32[]{:S(2)}) async-start(), calls=%async_computation.9 | async-start | bytes 7299072 | tf_op jit(solution)/shard_map/reduce_scatter | solution.py:271
  704.4 642.4 %reduce-scatter.13.cloned.1.call-start = ((), (), s32[]{:S(2)}) async-start(), calls=%async_computation.8 | async-start | bytes 7299072 | tf_op jit(solution)/shard_map/reduce_scatter | solution.py:271
  712.5 733.9 %reduce-scatter.23.cloned.1.call-start = ((), (), s32[]{:S(2)}) async-start(), calls=%async_computation.13 | async-start | bytes 9732096 | tf_op jit(solution)/shard_map/reduce_scatter | solution.py:279
  720.8 867.0 %reduce-scatter.21.cloned.1.call-start = ((), (), s32[]{:S(2)}) async-start(), calls=%async_computation.12 | async-start | bytes 9732096 | tf_op jit(solution)/shard_map/reduce_scatter | solution.py:279
  729.1 999.1 %reduce-scatter.27.cloned.1.call-start = ((), (), s32[]{:S(2)}) async-start(), calls=%async_computation.15 | async-start | bytes 9732096 | tf_op jit(solution)/shard_map/reduce_scatter | solution.py:281
  738.4 1131.1 %reduce-scatter.25.cloned.1.call-start = ((), (), s32[]{:S(2)}) async-start(), calls=%async_computation.14 | async-start | bytes 9732096 | tf_op jit(solution)/shard_map/reduce_scatter | solution.py:281
  980.1 341.0 %copy-start.18 = (f32[2,197,768]{2,1,0:T(8,128)S(1)}, f32[2,197,768]{2,1,0:T(8,128)}, u32[]{:S(2)}) copy-start(f32[2,197,768]{2,1,0:T(8,128)} %copy-done.17) | copy-start | bytes 3631108
  1274.3 18.5 collective-permute-start.16
  1275.6 13.3 collective-permute-start.17
  1280.8 9.4 collective-permute-start.8
  1282.7 13.2 collective-permute-start.15
  1287.6 10.6 collective-permute-start.14
  1288.9 12.6 collective-permute-start.13
  1290.2 12.6 collective-permute-start.12
  1292.8 13.8 collective-permute-start.11
  1295.9 12.6 collective-permute-start.10
  1298.2 11.8 collective-permute-start.9
  1301.6 11.6 collective-permute-start.7
  1302.9 12.2 collective-permute-start.6
  1306.6 11.0 collective-permute-start.5
  1308.5 15.4 copy-start.45
  1308.5 19.9 %collective-permute-start.4 = (f32[12,32]{0,1:T(8,128)S(1)}, f32[12,32]{0,1:T(8,128)S(1)}, u32[]{:S(2)}, u32[]{:S(2)}) collective-permute-start(f32[12,32]{0,1:T(8,128)S(1)} %get-tuple-element.157), channel_id=1, source_target_pairs={{0,5},{1,6},{2,7},{3,8},{4,9},{5,10},{6,11},{7,12},{8,13},{9,14},{... | collective-permute-start | bytes 4616
  1309.9 18.5 collective-permute-start.3
  1313.2 15.2 collective-permute-start.2
  1315.1 13.4 collective-permute-start.1
  1317.6 10.8 collective-permute-start
  (68 other events, 257.9 us)
Sparse Core Ops, SparseCore 0:
  11.0 63.4 all-gather.40
  77.5 53.4 all-gather.42
  134.6 62.3 all-gather.44
  200.5 62.4 all-gather.46
  266.4 60.4 all-gather.48
  329.7 52.3 all-gather.50
  385.7 62.6 all-gather.52
  451.9 63.1 all-gather.54
  690.3 150.5 all-reduce.52
  846.1 100.5 reduce-scatter.18
  952.8 98.0 reduce-scatter.16
  1056.4 118.0 reduce-scatter.14
  1181.1 124.7 reduce-scatter.12
  1311.7 134.6 reduce-scatter.22
  1453.2 134.5 reduce-scatter.20
  1593.5 134.5 reduce-scatter.26
  1734.9 134.5 reduce-scatter.24
where the time goes:
time: 1890 us; the launch traced here: 1880 us
  waiting for transfers between devices  522 us (28%)
  other arithmetic  484 us (26%)
  local copies, waits for them, and re-layouts  406 us (21%)
  blocking collectives  254 us (13%)
  matrix products  150 us (8%)
  starting transfers between devices  47.5 us (3%)
    scatter-add x2, other arithmetic, layer_backward(): jax.ops.segment_sum(jnp.transpose(score_sum), index.reshape(-1), num_segm...  415 us
    gather x8, local copies, waits for them, and re-layouts, layer_forward(): bias = table.astype(F32)[:, index]  298 us
    reduce_scatter x2, waiting for transfers between devices, reduce_grads(): lax.psum_scatter(terms[12], ('dp', 'fsdp'), scatter_dimension=0, tiled=True)  280 us
    reduce_scatter x2, waiting for transfers between devices, reduce_grads(): lax.psum_scatter(terms[10], ('dp', 'fsdp'), scatter_dimension=0, tiled=True)  239 us
    all_gather x2, blocking collectives, fetch_forward(): lax.all_gather(parts[15], ('dp', 'fsdp'), axis=1, tiled=True)  135 us
    unnamed x2, blocking collectives  119 us
    unnamed x19, starting transfers between devices  46.4 us
  transfers between devices with their start and end apart: 35, of which 4 were waited for; matrix products, arithmetic and copies ran while one was open for 53% of the time, Pallas kernels for 0%

commit v1 on v0

v1 whole, which is shorter than its diff:
```python
import functools
import math

import jax
import jax.numpy as jnp
import numpy as np
from jax import lax
from jax.experimental import pallas as pl
from jax.experimental.pallas import tpu as pltpu
from jax.sharding import PartitionSpec as P

GRID = 14
SPAN = 2 * GRID - 1
LAYERS = 2
IMG_ROWS = GRID * GRID + 1
PAD_ROWS = 208
LANES = 256
E_LANES = 512
HEAD = 64
PAIR = 2 * HEAD
NEG = -1e30
SMALL = 128
F32 = jnp.float32
B16 = jnp.bfloat16
AXES = ("dp", "fsdp")
VMEM = pltpu.CompilerParams(vmem_limit_bytes=56 * 1024 * 1024)


def dot(a, b, dims):
    return lax.dot_general(a, b, (dims, ((), ())), preferred_element_type=F32)


NN = ((1,), (0,))
NT = ((1,), (1,))
TN = ((0,), (0,))


def shift_onehot():
    v, d, b = np.meshgrid(np.arange(SPAN), np.arange(GRID), np.arange(GRID), indexing="ij")
    return (v == b - d + GRID - 1).astype(np.float32)


def bias_kernel(cls_ref, e_ref, out_ref, tmp_ref):
    head = pl.program_id(0)
    tmp_ref[...] = jnp.zeros_like(tmp_ref)
    for c in range(GRID):
        start = (GRID - 1 - c) * GRID
        tmp_ref[1 + c * GRID : 1 + (c + 1) * GRID, 0:IMG_ROWS] = e_ref[
            0, 0:GRID, start : start + IMG_ROWS
        ]
    row = lax.broadcasted_iota(jnp.int32, (PAD_ROWS, LANES), 0)
    lane = lax.broadcasted_iota(jnp.int32, (PAD_ROWS, LANES), 1)
    to_patch = cls_ref[head, 0]
    from_patch = cls_ref[head, 1]
    to_self = cls_ref[head, 2]
    val = jnp.where(lane == 0, to_patch, tmp_ref[...])
    first = jnp.where(lane == 0, to_self, from_patch)
    val = jnp.where(row == 0, first, val)
    out_ref[0] = jnp.where(row >= IMG_ROWS, NEG, val)


def build_bias(table):
    heads = table.shape[0]
    grid_part = table[:, : SPAN * SPAN].reshape(heads, SPAN, SPAN).astype(B16)
    onehot = jnp.asarray(shift_onehot(), B16)
    e = jnp.einsum("huv,vdb->hdub", grid_part, onehot, preferred_element_type=F32)
    e = e.reshape(heads, GRID, SPAN * GRID)
    e = jnp.pad(e, ((0, 0), (0, 16 - GRID), (1, E_LANES - 1 - SPAN * GRID)))
    cls = table[:, SPAN * SPAN : SPAN * SPAN + 3]
    return pl.pallas_call(
        bias_kernel,
        grid=(heads,),
        out_shape=jax.ShapeDtypeStruct((heads, PAD_ROWS, LANES), F32),
        in_specs=[
            pl.BlockSpec(memory_space=pltpu.SMEM),
            pl.BlockSpec((1, 16, E_LANES), lambda h: (h, 0, 0)),
        ],
        out_specs=pl.BlockSpec((1, PAD_ROWS, LANES), lambda h: (h, 0, 0)),
        scratch_shapes=[pltpu.VMEM((PAD_ROWS, LANES), F32)],
        compiler_params=VMEM,
        name="bias_expand",
    )(cls, e)


def bias_grad_kernel(g_ref, e_ref, cls_ref):
    lane = lax.broadcasted_iota(jnp.int32, (PAD_ROWS, LANES), 1)
    row = lax.broadcasted_iota(jnp.int32, (PAD_ROWS, LANES), 0)
    g = g_ref[0]
    g = jnp.where((lane < IMG_ROWS) & (row < IMG_ROWS), g, 0.0)
    e_ref[...] = jnp.zeros_like(e_ref)
    for c in range(GRID):
        start = (GRID - 1 - c) * GRID
        rows = g_ref[0, 1 + c * GRID : 1 + (c + 1) * GRID, 1:IMG_ROWS]
        e_ref[0, 0:GRID, start + 1 : start + IMG_ROWS] += rows
    to_patch = jnp.sum(jnp.where((lane == 0) & (row > 0), g, 0.0))
    from_patch = jnp.sum(jnp.where((lane > 0) & (row == 0), g, 0.0))
    to_self = jnp.sum(jnp.where((lane == 0) & (row == 0), g, 0.0))
    spot = lax.broadcasted_iota(jnp.int32, (8, 128), 1)
    cls_ref[0] = jnp.where(
        spot == 0, to_patch, jnp.where(spot == 1, from_patch, jnp.where(spot == 2, to_self, 0.0))
    )


def reduce_bias(grad, entries):
    heads = grad.shape[0]
    e, cls = pl.pallas_call(
        bias_grad_kernel,
        grid=(heads,),
        out_shape=(
            jax.ShapeDtypeStruct((heads, 16, E_LANES), F32),
            jax.ShapeDtypeStruct((heads, 8, 128), F32),
        ),
        in_specs=[pl.BlockSpec((1, PAD_ROWS, LANES), lambda h: (h, 0, 0))],
        out_specs=(
            pl.BlockSpec((1, 16, E_LANES), lambda h: (h, 0, 0)),
            pl.BlockSpec((1, 8, 128), lambda h: (h, 0, 0)),
        ),
        compiler_params=VMEM,
        name="bias_reduce",
    )(grad)
    e = e[:, :GRID, 1 : 1 + SPAN * GRID].reshape(heads, GRID, SPAN, GRID)
    onehot = jnp.asarray(shift_onehot(), F32)
    grid_part = jnp.einsum("hdub,vdb->huv", e, onehot, precision=lax.Precision.HIGHEST)
    flat = jnp.concatenate([grid_part.reshape(heads, SPAN * SPAN), cls[:, 0, :3]], axis=1)
    return jnp.pad(flat, ((0, 0), (0, entries - flat.shape[1])))


def head_mask(which):
    lane = lax.broadcasted_iota(jnp.int32, (PAD_ROWS, PAIR), 1)
    return (lane < HEAD) if which == 0 else (lane >= HEAD)


def attention_kernel(width, qkv_ref, bias_ref, out_ref, lse_ref):
    heads = width // HEAD
    for pair in range(heads // 2):
        at = pair * PAIR
        q = qkv_ref[0, :, at : at + PAIR]
        k = qkv_ref[0, :, width + at : width + at + PAIR]
        v = qkv_ref[0, :, 2 * width + at : 2 * width + at + PAIR]
        q = q * jnp.asarray(HEAD ** (-0.5), B16)
        v_t = v.T
        parts = []
        for t in range(2):
            head = 2 * pair + t
            q_t = jnp.where(head_mask(t), q, jnp.zeros_like(q))
            scores = dot(k, q_t, NT) + bias_ref[head, :, 0:PAD_ROWS]
            top = jnp.max(scores, axis=0, keepdims=True)
            weights = jnp.exp(scores - top)
            total = jnp.sum(weights, axis=0, keepdims=True)
            probs = (weights * (1.0 / total)).astype(B16)
            lse_ref[0, head : head + 1, 0:PAD_ROWS] = top + jnp.log(total)
            parts.append(dot(v_t[t * HEAD : (t + 1) * HEAD], probs, NN))
        out_ref[0, :, at : at + PAIR] = jnp.concatenate(parts, axis=0).T.astype(B16)


def attention_forward(qkv, bias):
    images = qkv.shape[0]
    width = qkv.shape[2] // 3
    heads = width // HEAD
    return pl.pallas_call(
        functools.partial(attention_kernel, width),
        grid=(images,),
        out_shape=(
            jax.ShapeDtypeStruct((images, PAD_ROWS, width), B16),
            jax.ShapeDtypeStruct((images, 16, LANES), F32),
        ),
        in_specs=[
            pl.BlockSpec((1, PAD_ROWS, 3 * width), lambda i: (i, 0, 0)),
            pl.BlockSpec((heads, PAD_ROWS, LANES), lambda i: (0, 0, 0)),
        ],
        out_specs=(
            pl.BlockSpec((1, PAD_ROWS, width), lambda i: (i, 0, 0)),
            pl.BlockSpec((1, 16, LANES), lambda i: (i, 0, 0)),
        ),
        compiler_params=VMEM,
        name="attention",
    )(qkv, bias)


def attention_grad_kernel(width, qkv_ref, bias_ref, lse_ref, g_ref, out_ref, dbias_ref):
    heads = width // HEAD
    scale = HEAD ** (-0.5)

    @pl.when(pl.program_id(0) == 0)
    def _():
        dbias_ref[...] = jnp.zeros_like(dbias_ref)

    for pair in range(heads // 2):
        at = pair * PAIR
        q = qkv_ref[0, :, at : at + PAIR]
        k = qkv_ref[0, :, width + at : width + at + PAIR]
        v = qkv_ref[0, :, 2 * width + at : 2 * width + at + PAIR]
        g = g_ref[0, :, at : at + PAIR]
        q = q * jnp.asarray(scale, B16)
        k_t = k.T
        dq_parts = []
        dk = None
        dv = None
        for t in range(2):
            head = 2 * pair + t
            q_t = jnp.where(head_mask(t), q, jnp.zeros_like(q))
            g_t = jnp.where(head_mask(t), g, jnp.zeros_like(g))
            scores = dot(k, q_t, NT) + bias_ref[head, :, 0:PAD_ROWS]
            probs = jnp.exp(scores - lse_ref[0, head : head + 1, 0:PAD_ROWS])
            dprobs = dot(v, g_t, NT)
            dv_t = dot(probs.astype(B16), g_t, NN)
            mean = jnp.sum(probs * dprobs, axis=0, keepdims=True)
            dscores = (probs * (dprobs - mean)).astype(B16)
            dbias_ref[head, :, 0:PAD_ROWS] += dscores.astype(F32)
            dk_t = dot(dscores, q_t, NN)
            dq_parts.append(dot(k_t[t * HEAD : (t + 1) * HEAD], dscores, NN))
            dk = dk_t if dk is None else dk + dk_t
            dv = dv_t if dv is None else dv + dv_t
        dq = jnp.concatenate(dq_parts, axis=0).T * scale
        out_ref[0, :, at : at + PAIR] = dq.astype(B16)
        out_ref[0, :, width + at : width + at + PAIR] = dk.astype(B16)
        out_ref[0, :, 2 * width + at : 2 * width + at + PAIR] = dv.astype(B16)


def attention_backward(qkv, bias, lse, grad):
    images = qkv.shape[0]
    width = qkv.shape[2] // 3
    heads = width // HEAD
    return pl.pallas_call(
        functools.partial(attention_grad_kernel, width),
        grid=(images,),
        out_shape=(
            jax.ShapeDtypeStruct((images, PAD_ROWS, 3 * width), B16),
            jax.ShapeDtypeStruct((heads, PAD_ROWS, LANES), F32),
        ),
        in_specs=[
            pl.BlockSpec((1, PAD_ROWS, 3 * width), lambda i: (i, 0, 0)),
            pl.BlockSpec((heads, PAD_ROWS, LANES), lambda i: (0, 0, 0)),
            pl.BlockSpec((1, 16, LANES), lambda i: (i, 0, 0)),
            pl.BlockSpec((1, PAD_ROWS, width), lambda i: (i, 0, 0)),
        ],
        out_specs=(
            pl.BlockSpec((1, PAD_ROWS, 3 * width), lambda i: (i, 0, 0)),
            pl.BlockSpec((heads, PAD_ROWS, LANES), lambda i: (0, 0, 0)),
        ),
        compiler_params=VMEM,
        name="attention_grad",
    )(qkv, bias, lse, grad)


def normalize(x):
    centered = x - jnp.mean(x, -1, keepdims=True)
    scale = lax.rsqrt(jnp.mean(centered * centered, -1, keepdims=True) + 1e-06)
    return centered * scale, scale


def normalize_grad(x_hat, scale, dy):
    return scale * (
        dy - jnp.mean(dy, -1, keepdims=True) - x_hat * jnp.mean(dy * x_hat, -1, keepdims=True)
    )


def gelu_and_slope(x):
    t = 1.0 / (1.0 + (0.3275911 / math.sqrt(2.0)) * jnp.abs(x))
    bell = jnp.exp(-0.5 * x * x)
    poly = 0.5 * 1.061405429
    for coef in (-1.453152027, 1.421413741, -0.284496736, 0.254829592):
        poly = poly * t + 0.5 * coef
    tail = poly * t * bell
    phi = jnp.where(x >= 0, 1.0 - tail, tail)
    return x * phi, phi + x * bell * (1.0 / math.sqrt(2.0 * math.pi))


def mlp_kernel(mid_ref, vec_ref, b1_ref, w1_ref, w2_ref, out_ref, mlp_ref, h2_ref, act_ref, slope_ref):
    step = pl.program_id(0)

    @pl.when(step == 0)
    def _():
        x_hat, _ = normalize(mid_ref[...])
        h2_ref[...] = (x_hat * vec_ref[0:1] + vec_ref[1:2]).astype(B16)

    pre = dot(h2_ref[...], w1_ref[...], NN) + b1_ref[...]
    act, slope = gelu_and_slope(pre)
    act = act.astype(B16)
    act_ref[...] = act
    slope_ref[...] = slope.astype(slope_ref.dtype)
    part = dot(act, w2_ref[...], NN)

    @pl.when(step == 0)
    def _():
        mlp_ref[...] = part + vec_ref[2:3]

    @pl.when(step > 0)
    def _():
        mlp_ref[...] += part

    @pl.when(step == pl.num_programs(0) - 1)
    def _():
        out_ref[...] = mid_ref[...] + vec_ref[3:4] * mlp_ref[...]


def mlp_forward(mid, vecs, b1, w1, w2, tile=768):
    rows, width = mid.shape
    hidden = w1.shape[1]
    whole = pl.BlockSpec((rows, width), lambda i: (0, 0))
    cols = pl.BlockSpec((rows, tile), lambda i: (0, i))
    return pl.pallas_call(
        mlp_kernel,
        grid=(hidden // tile,),
        out_shape=(
            jax.ShapeDtypeStruct((rows, width), F32),
            jax.ShapeDtypeStruct((rows, width), F32),
            jax.ShapeDtypeStruct((rows, width), B16),
            jax.ShapeDtypeStruct((rows, hidden), B16),
            jax.ShapeDtypeStruct((rows, hidden), F32),
        ),
        in_specs=[
            whole,
            pl.BlockSpec((8, width), lambda i: (0, 0)),
            pl.BlockSpec((1, tile), lambda i: (0, i)),
            pl.BlockSpec((width, tile), lambda i: (0, i)),
            pl.BlockSpec((tile, width), lambda i: (i, 0)),
        ],
        out_specs=(whole, whole, whole, cols, cols),
        compiler_params=VMEM,
        name="mlp",
    )(mid, vecs, b1, w1, w2)


def mlp_grad_kernel(
    g_ref, mid_ref, mlp_ref, branch_ref, vec_ref, h2_ref, act_ref, slope_ref, w1_ref, w2_ref,
    dw1_ref, dw2_ref, db1_ref, dmid_ref, dbranch_ref, sums_ref, dmlp_ref, h2t_ref, dh2_ref,
):
    step = pl.program_id(0)

    @pl.when(step == 0)
    def _():
        g = g_ref[...]
        dmlp = (g * vec_ref[3:4]).astype(B16)
        dmlp_ref[...] = dmlp
        h2t_ref[...] = h2_ref[...].T
        sums_ref[...] = jnp.zeros_like(sums_ref)
        sums_ref[0:1] = jnp.sum(g * mlp_ref[...], axis=0, keepdims=True)
        sums_ref[1:2] = jnp.sum(dmlp.astype(F32), axis=0, keepdims=True)

    dmlp = dmlp_ref[...]
    dact = dot(dmlp, w2_ref[...], NT)
    dpre = (dact * slope_ref[...].astype(F32)).astype(B16)
    dw2_ref[...] = dot(act_ref[...].T, dmlp, NN).astype(dw2_ref.dtype)
    dw1_ref[...] = dot(h2t_ref[...], dpre, NN).astype(dw1_ref.dtype)
    db1_ref[...] = jnp.sum(dpre.astype(F32), axis=0, keepdims=True)
    part = dot(dpre, w1_ref[...], NT)

    @pl.when(step == 0)
    def _():
        dh2_ref[...] = part

    @pl.when(step > 0)
    def _():
        dh2_ref[...] += part

    @pl.when(step == pl.num_programs(0) - 1)
    def _():
        x_hat, scale = normalize(mid_ref[...])
        dh2 = dh2_ref[...]
        sums_ref[2:3] = jnp.sum(dh2 * x_hat, axis=0, keepdims=True)
        sums_ref[3:4] = jnp.sum(dh2, axis=0, keepdims=True)
        dmid = g_ref[...] + normalize_grad(x_hat, scale, dh2 * vec_ref[0:1])
        dmid_ref[...] = dmid
        dbranch = (dmid * vec_ref[4:5]).astype(B16)
        dbranch_ref[...] = dbranch
        sums_ref[4:5] = jnp.sum(dmid * branch_ref[...], axis=0, keepdims=True)
        sums_ref[5:6] = jnp.sum(dbranch.astype(F32), axis=0, keepdims=True)


def mlp_backward(grad, mid, mlp_out, branch, vecs, h2, act, slope, w1, w2, tile=768):
    rows, width = mid.shape
    hidden = w1.shape[1]
    whole = pl.BlockSpec((rows, width), lambda i: (0, 0))
    cols = pl.BlockSpec((rows, tile), lambda i: (0, i))
    eight = pl.BlockSpec((8, width), lambda i: (0, 0))
    w1_spec = pl.BlockSpec((width, tile), lambda i: (0, i))
    w2_spec = pl.BlockSpec((tile, width), lambda i: (i, 0))
    return pl.pallas_call(
        mlp_grad_kernel,
        grid=(hidden // tile,),
        out_shape=(
            jax.ShapeDtypeStruct((width, hidden), B16),
            jax.ShapeDtypeStruct((hidden, width), B16),
            jax.ShapeDtypeStruct((1, hidden), F32),
            jax.ShapeDtypeStruct((rows, width), F32),
            jax.ShapeDtypeStruct((rows, width), B16),
            jax.ShapeDtypeStruct((8, width), F32),
        ),
        in_specs=[whole, whole, whole, whole, eight, whole, cols, cols, w1_spec, w2_spec],
        out_specs=(
            w1_spec,
            w2_spec,
            pl.BlockSpec((1, tile), lambda i: (0, i)),
            whole,
            whole,
            eight,
        ),
        scratch_shapes=[
            pltpu.VMEM((rows, width), B16),
            pltpu.VMEM((width, rows), B16),
            pltpu.VMEM((rows, width), F32),
        ],
        compiler_params=VMEM,
        name="mlp_grad",
    )(grad, mid, mlp_out, branch, vecs, h2, act, slope, w1, w2)


def layer_forward(x, weights, images):
    small, w_qkv, w_proj, w_one, w_two = weights
    width = x.shape[1]
    vec = small["vec"]
    x_hat, _ = normalize(x)
    h = (x_hat * vec[0] + vec[1]).astype(B16)
    qkv_bias = jnp.concatenate([vec[2], jnp.zeros((width,), F32), vec[3]])
    qkv = (dot(h, w_qkv, NN) + qkv_bias).astype(B16)
    qkv = qkv.reshape(images, PAD_ROWS, 3 * width)
    att, lse = attention_forward(qkv, small["bias"])
    att = att.reshape(images * PAD_ROWS, width)
    branch = dot(att, w_proj, NN) + vec[4]
    mid = x + vec[5] * branch
    mlp_vecs = jnp.concatenate([vec[6:10], vec[5:6], jnp.zeros((3, width), F32)])
    out, mlp_out, h2, act, slope = mlp_forward(mid, mlp_vecs, small["b1"], w_one, w_two)
    return out, (x, h, qkv, lse, att, branch, mid, mlp_vecs, mlp_out, h2, act, slope)


def layer_backward(saved, weights, grad, images):
    x, h, qkv, lse, att, branch, mid, mlp_vecs, mlp_out, h2, act, slope = saved
    small, w_qkv, w_proj, w_one, w_two = weights
    vec = small["vec"]
    width = x.shape[1]
    d_one, d_two, d_b1, d_mid, d_branch, sums = mlp_backward(
        grad, mid, mlp_out, branch, mlp_vecs, h2, act, slope, w_one, w_two
    )
    d_att = dot(d_branch, w_proj, NT).astype(B16)
    d_proj = dot(att, d_branch, TN).astype(B16)
    d_qkv, d_bias = attention_backward(
        qkv, small["bias"], lse, d_att.reshape(images, PAD_ROWS, width)
    )
    d_qkv = d_qkv.reshape(images * PAD_ROWS, 3 * width)
    d_wqkv = dot(h, d_qkv, TN).astype(B16)
    d_h = dot(d_qkv, w_qkv, NT)
    x_hat, scale = normalize(x)
    d_gain = jnp.sum(d_h * x_hat, 0)
    d_shift = jnp.sum(d_h, 0)
    d_x = d_mid + normalize_grad(x_hat, scale, d_h * vec[0])
    sums_qkv = jnp.sum(d_qkv.astype(F32), 0)
    d_table = reduce_bias(d_bias, small["entries"])
    d_vec = jnp.stack(
        [
            d_gain, d_shift, sums_qkv[:width], sums_qkv[2 * width :], sums[5], sums[4],
            sums[2], sums[3], sums[1], sums[0],
        ]
    )
    return d_x, (d_wqkv, d_proj, d_one, d_two), (d_vec, d_b1.reshape(-1), d_table)


def pack_small(vectors, b1, table, dtype):
    rows = vectors[0].shape[0]
    tab = jnp.pad(jnp.transpose(table), ((0, rows - table.shape[1]), (0, 0)))
    cols = jnp.concatenate(
        [jnp.stack(vectors, axis=1), b1.reshape(rows, -1), tab], axis=1
    ).astype(dtype)
    return jnp.pad(cols, ((0, 0), (0, SMALL - cols.shape[1])))


def unpack_small(packed, heads, per_dev, shards):
    count = 10
    ratio = 4
    rows = packed.shape[0]
    turned = jnp.transpose(packed.astype(F32))
    vec = turned[:count]
    b1 = packed[:, count : count + ratio].astype(F32).reshape(1, rows * ratio)
    tab = packed[:, count + ratio : count + ratio + heads].astype(F32)
    tab = tab.reshape(shards, rows // shards, heads)[:, :per_dev].reshape(shards * per_dev, heads)
    table = jnp.transpose(tab)
    return {"vec": vec, "b1": b1, "bias": build_bias(table), "entries": table.shape[1]}


def pack_small_grad(d_vec, d_b1, d_table, shards):
    rows = d_vec.shape[1]
    heads, entries = d_table.shape
    per_dev = entries // shards
    tab = jnp.transpose(d_table).reshape(shards, per_dev, heads)
    tab = jnp.pad(tab, ((0, 0), (0, rows // shards - per_dev), (0, 0))).reshape(rows, heads)
    cols = jnp.concatenate([jnp.transpose(d_vec), d_b1.reshape(rows, -1), tab], axis=1)
    return jnp.pad(cols, ((0, 0), (0, SMALL - cols.shape[1])))


def unpack_small_grad(packed, heads, per_dev):
    vec = [packed[:, i] for i in range(10)]
    b1 = packed[:, 10:14].reshape(-1)
    table = jnp.transpose(packed[:per_dev, 14 : 14 + heads])
    return vec, b1, table


def per_device(
    shards,
    tokens, masked_rows, cotangent, norm1_gain, norm1_bias, qkv_weight, q_bias, v_bias,
    proj_weight, proj_bias, gamma_attn, norm2_gain, norm2_bias, fc1_weight, fc1_bias,
    fc2_weight, fc2_bias, gamma_mlp, rel_table,
):
    vectors = (norm1_gain, norm1_bias, q_bias, v_bias, proj_bias, gamma_attn, norm2_gain,
               norm2_bias, fc2_bias, gamma_mlp)
    width = tokens.shape[1]
    images = masked_rows.shape[0]
    heads, per_dev = rel_table.shape[1:]
    own_rows = qkv_weight.shape[1]
    ratio = fc2_weight.shape[1] // own_rows
    hidden = fc1_weight.shape[2]
    ends = np.cumsum([3 * width, width, hidden, ratio * width, SMALL])

    def pad_rows(v):
        v = v.astype(F32).reshape(images, IMG_ROWS, width)
        v = jnp.pad(v, ((0, 0), (0, PAD_ROWS - IMG_ROWS), (0, 0)))
        return v.reshape(images * PAD_ROWS, width)

    def cut_rows(v):
        return v.reshape(images, PAD_ROWS, width)[:, :IMG_ROWS].reshape(images * IMG_ROWS, width)

    def fetch(layer):
        two = fc2_weight[layer].reshape(ratio, own_rows, width)
        small = pack_small([v[layer] for v in vectors], fc1_bias[layer], rel_table[layer], B16)
        block = jnp.concatenate(
            [qkv_weight[layer], proj_weight[layer], fc1_weight[layer]]
            + [two[i] for i in range(ratio)]
            + [small],
            axis=1,
        )
        full = lax.all_gather(block, AXES, axis=0, tiled=True)
        w_qkv, w_proj, w_one, w_two, small = jnp.split(full, ends[:-1], axis=1)
        w_two = w_two.reshape(shards, own_rows, ratio, width).transpose(0, 2, 1, 3)
        w_two = w_two.reshape(hidden, width)
        return unpack_small(small, heads, per_dev, shards), w_qkv, w_proj, w_one, w_two

    def reduce(big, small):
        d_wqkv, d_proj, d_one, d_two = big
        packed = pack_small_grad(*small, shards).astype(B16)
        d_two = d_two.reshape(shards, ratio, own_rows, width).transpose(0, 2, 1, 3)
        d_two = d_two.reshape(width, ratio * width)
        block = jnp.concatenate([d_wqkv, d_proj, d_one, d_two, packed], axis=1)
        own = lax.psum_scatter(block, AXES, scatter_dimension=0, tiled=True).astype(F32)
        o_qkv, o_proj, o_one, o_two, o_small = jnp.split(own, ends[:-1], axis=1)
        o_two = o_two.reshape(own_rows, ratio, width).transpose(1, 0, 2)
        o_two = o_two.reshape(ratio * own_rows, width)
        return o_qkv, o_proj, o_one, o_two, unpack_small_grad(o_small, heads, per_dev)

    x = pad_rows(tokens)
    weights = []
    saved = []
    for layer in range(LAYERS):
        weights.append(fetch(layer))
        x, keep = layer_forward(x, weights[layer], images)
        saved.append(keep)
    encoded = cut_rows(x.astype(B16))

    positions = jnp.arange(IMG_ROWS, dtype=jnp.int32)
    mask = jnp.any(masked_rows[:, :, None] == positions[None, None, :], axis=1)
    mask = jnp.pad(mask, ((0, 0), (0, PAD_ROWS - IMG_ROWS))).reshape(-1, 1)
    grad = jnp.where(mask, pad_rows(cotangent), 0.0)
    owned = [None] * LAYERS
    for layer in reversed(range(LAYERS)):
        grad, big, small = layer_backward(saved[layer], weights[layer], grad, images)
        owned[layer] = reduce(big, small)

    def both(pick):
        return jnp.stack([pick(o) for o in owned])

    g = [both(lambda o, i=i: o[4][0][i]) for i in range(10)]
    g_qkv, g_proj, g_one, g_two = (both(lambda o, i=i: o[i]) for i in range(4))
    g_b1 = both(lambda o: o[4][1])
    g_table = both(lambda o: o[4][2])
    return (encoded, cut_rows(grad), g[0], g[1], g_qkv, g[2], g[3], g_proj, g[4], g[5], g[6],
            g[7], g_one, g_b1, g_two, g[8], g[9], g_table)


def solution(mesh):
    shards = math.prod(mesh.shape[a] for a in AXES)
    row = P(AXES, None)
    vec = P(None, AXES)
    mat = P(None, AXES, None)
    tab = P(None, None, AXES)
    return jax.shard_map(
        functools.partial(per_device, shards),
        mesh=mesh,
        in_specs=(row, row, row, vec, vec, mat, vec, vec, mat, vec, vec, vec, vec, mat, vec, mat,
                  vec, vec, tab),
        out_specs=(row, row, vec, vec, mat, vec, vec, mat, vec, vec, vec, vec, mat, vec, mat,
                   vec, vec, tab),
        check_vma=False,
    )
```

time: 1890 us -> 838 us (0.44)
  other arithmetic: 484 us -> 33.9 us
  local copies, waits for them, and re-layouts: 406 us -> 146 us
  blocking collectives: 254 us -> 0 us
  Pallas kernels: 0 us -> 140 us
  matrix products: 150 us -> 56.6 us
  waiting for transfers between devices: 522 us -> 438 us
  starting transfers between devices: 47.5 us -> 0.16 us
    reduce_scatter x8 -> x0, waiting for transfers between devices: 519 us -> none  [the longest x2 280 us: reduce_grads(): lax.psum_scatter(terms[12], ('dp', 'fsdp'), scatter_dimension=0, tiled=True)]
    scatter-add x2 -> x0, other arithmetic: 415 us -> none  [layer_backward(): jax.ops.segment_sum(jnp.transpose(score_sum), index.reshape(-1), num_segm...]
    gather x8 -> x0, local copies, waits for them, and re-layouts: 298 us -> none  [layer_forward(): bias = table.astype(F32)[:, index]]
    unnamed x36 -> x6, waiting for transfers between devices: 2.71 us -> 235 us
    all_gather x8 -> x2, waiting for transfers between devices: 0.13 us -> 203 us  [fetch(): full = lax.all_gather(block, AXES, axis=0, tiled=True)]
    pallas_call x0 -> x12, Pallas kernels: none -> 140 us  [the longest x2 39.4 us: mlp_backward(): pl.pallas_call(mlp_grad_kernel, grid=(hidden // tile,), out_shape=(jax.Sh...]
    all_gather x2 -> x0, blocking collectives: 135 us -> none  [fetch_forward(): lax.all_gather(parts[15], ('dp', 'fsdp'), axis=1, tiled=True)]
    unnamed x2 -> x0, blocking collectives: 119 us -> none
  transfers between devices with their start and end apart: 35 -> 4, of which waited for: 4 -> 4; matrix products, arithmetic and copies ran while one was open for 53% -> 7% of each run, Pallas kernels for 0% -> 5%
where the time goes in v1:
time: 838 us; the launch traced here: 830 us
  waiting for transfers between devices  438 us (52%)
  local copies, waits for them, and re-layouts  146 us (17%)
  Pallas kernels  140 us (17%)
  matrix products  56.6 us (7%)
  other arithmetic  33.9 us (4%)
  between operations  15.1 us (2%)
    unnamed x6, waiting for transfers between devices  235 us
    all_gather x2, waiting for transfers between devices, fetch(): full = lax.all_gather(block, AXES, axis=0, tiled=True)  203 us
    dot_general x12, matrix products, dot(): return lax.dot_general(a, b, (dims, ((), ())), preferred_element_type=F32)  47.7 us
    pallas_call x2, Pallas kernels, mlp_backward(): pl.pallas_call(mlp_grad_kernel, grid=(hidden // tile,), out_shape=(jax.Sh...  39.4 us
    unnamed x82, local copies, waits for them, and re-layouts  34.2 us
    reshape x4, local copies, waits for them, and re-layouts, fetch(): w_two = w_two.reshape(shards, own_rows, ratio, width).transpose(0, 2, 1, 3)  30.3 us
    pallas_call x2, Pallas kernels, mlp_forward(): pl.pallas_call(mlp_kernel, grid=(hidden // tile,), out_shape=(jax.ShapeDt...  28.3 us
    pallas_call x2, Pallas kernels, attention_backward(): pl.pallas_call(functools.partial(attention_grad_kernel, width), grid=(ima...  23.7 us
  transfers between devices with their start and end apart: 4, of which 4 were waited for; matrix products, arithmetic and copies ran while one was open for 7% of the time, Pallas kernels for 5%

profile of v1, /device:TPU:0, one launch (start us, length us, event | category | flops | bytes accessed | tf_op | source)
XLA Modules:
  0.0 829.8 jit_solution(15060940620044278106)
XLA Ops:
  27.8 100.4 %all-gather.5.cloned.1.call-done = bf16[768,9344]{1,0:T(8,128)(2,1)} async-done(((bf16[24,9344]{1,0:T(8,128)(2,1)}), bf16[768,9344]{1,0:T(8,128)(2,1)}) %all-gather.5.cloned.1.call-update) | async-done | bytes 14352400 | tf_op jit(solution)/shard_map/all_gather | solution.py:530
  131.7 102.2 %all-gather.3.cloned.1.call-done = bf16[768,9344]{1,0:T(8,128)(2,1)} async-done(((bf16[24,9344]{1,0:T(8,128)(2,1)}), bf16[768,9344]{1,0:T(8,128)(2,1)}) %all-gather.3.cloned.1.call-update) | async-done | bytes 14352400 | tf_op jit(solution)/shard_map/all_gather | solution.py:530
  241.4 2.8 copy.253
  244.3 2.8 reshape.292
  252.6 8.2 fusion.61
  260.7 9.8 %reshape.296 = bf16[32,24,4,768]{3,2,1,0:T(4,128)(2,1)} reshape(bf16[768,3072]{1,0:T(8,128)(2,1)} %get-tuple-element.222) | data formatting | bytes 9437184 | tf_op jit(solution)/shard_map/reshape | solution.py:532
  270.5 5.4 copy.256
  275.9 7.8 bias_expand.2.bias_ref
  283.7 5.0 fusion.2
  288.7 8.3 attention.2
  297.7 3.6 bitcast_add_fusion
  301.3 14.3 %mlp.2 = (f32[416,768]{1,0:T(8,128)}, f32[416,768]{1,0:T(8,128)}, bf16[416,768]{1,0:T(8,128)(2,1)}, bf16[416,3072]{1,0:T(8,128)(2,1)}, f32[416,3072]{1,0:T(8,128)}) custom-call(f32[416,768]{1,0:T(8,128)} %get-tuple-element.278.mid_ref, f32[8,768]{1,0:T(8,128)} %get-tuple-element.257.vec_ref, f32[1,3072]{1,0:T(1,128)} %reshape.333.b1_ref, ...), custom_call_target="tpu_custom_call" | custom-call | tf_op jit(solution)/shard_map/mlp/pallas_call | solution.py:302
  320.4 2.5 copy.269
  322.8 3.4 reshape.301
  329.0 8.3 fusion.60
  337.3 9.8 %reshape.305 = bf16[32,24,4,768]{3,2,1,0:T(4,128)(2,1)} reshape(bf16[768,3072]{1,0:T(8,128)(2,1)} %get-tuple-element.220) | data formatting | bytes 9437184 | tf_op jit(solution)/shard_map/reshape | solution.py:532
  347.1 5.4 copy.272
  352.5 7.8 bias_expand.3.bias_ref
  360.2 5.1 fusion.3
  365.3 8.5 %attention.3 = (bf16[2,208,768]{2,1,0:T(8,128)(2,1)}, f32[2,16,256]{2,1,0:T(8,128)}) custom-call(bf16[2,208,2304]{2,1,0:T(8,128)(2,1)} %bitcast.244, f32[12,208,256]{2,1,0:T(8,128)} %bias_expand.3.bias_ref), custom_call_target="tpu_custom_call" | custom-call | tf_op jit(solution)/shard_map/attention/pallas_call | solution.py:160
  373.8 3.6 multiply_add_fusion.2
  377.4 14.1 %mlp.3 = (f32[416,768]{1,0:T(8,128)}, f32[416,768]{1,0:T(8,128)}, bf16[416,768]{1,0:T(8,128)(2,1)}, bf16[416,3072]{1,0:T(8,128)(2,1)}, f32[416,3072]{1,0:T(8,128)}) custom-call(f32[416,768]{1,0:T(8,128)} %get-tuple-element.280.mid_ref, f32[8,768]{1,0:T(8,128)} %get-tuple-element.256.vec_ref, f32[1,3072]{1,0:T(1,128)} %reshape.335.b1_ref, ...), custom_call_target="tpu_custom_call" | custom-call | tf_op jit(solution)/shard_map/mlp/pallas_call | solution.py:302
  391.4 18.9 %mlp_grad.2 = (bf16[768,3072]{1,0:T(8,128)(2,1)}, bf16[3072,768]{1,0:T(8,128)(2,1)}, f32[1,3072]{1,0:T(1,128)}, f32[416,768]{1,0:T(8,128)}, bf16[416,768]{1,0:T(8,128)(2,1)}, /*index=5*/f32[8,768]{1,0:T(8,128)}) custom-call(f32[416,768]{1,0:T(8,128)} %convert_select_fusion.g_ref, f32[416,768]{1,0:T(8,128)} %get-tuple-element.280.mid_ref, ...), custom_call_target="tpu_custom_call" | custom-call | tf_op jit(solution)/shard_map/mlp_grad/pallas_call | solution.py:379
  411.2 3.0 convolution_convert_fusion.4
  414.2 11.9 %attention_grad.2 = (bf16[2,208,2304]{2,1,0:T(8,128)(2,1)}, f32[12,208,256]{2,1,0:T(8,128)}) custom-call(bf16[2,208,2304]{2,1,0:T(8,128)(2,1)} %bitcast.245, f32[12,208,256]{2,1,0:T(8,128)} %bias_expand.3.bias_ref, f32[2,16,256]{2,1,0:T(8,128)} %get-tuple-element.61.lse_ref, bf16[2,208,768]{2,1,0:T(8,128)(2,1)} %bitcast.266), custom_call_target="tpu_custom_call" | custom-call | tf_op jit(solution)/shard_map/attention_grad/pallas_call | solution.py:224
  428.0 5.7 fusion.1
  438.0 3.2 copy.307
  441.1 8.3 bias_reduce.3
  451.6 4.2 reshape.326
  455.7 4.1 fusion.20
  461.2 5.5 multiply_reduce_fusion
  467.1 4.8 constant_dynamic-update-slice_fusion.15
  471.9 4.8 constant_dynamic-update-slice_fusion.14
  478.9 2.8 multiply_add_fusion.1.g_ref
  481.7 20.5 %mlp_grad.3 = (bf16[768,3072]{1,0:T(8,128)(2,1)}, bf16[3072,768]{1,0:T(8,128)(2,1)}, f32[1,3072]{1,0:T(1,128)}, f32[416,768]{1,0:T(8,128)}, bf16[416,768]{1,0:T(8,128)(2,1)}, /*index=5*/f32[8,768]{1,0:T(8,128)}) custom-call(f32[416,768]{1,0:T(8,128)} %multiply_add_fusion.1.g_ref, f32[416,768]{1,0:T(8,128)} %get-tuple-element.278.mid_ref, ...), custom_call_target="tpu_custom_call" | custom-call | tf_op jit(solution)/shard_map/mlp_grad/pallas_call | solution.py:379
  502.2 5.0 copy.274
  507.3 3.2 copy.306
  510.5 3.0 convolution_convert_fusion.3
  513.5 11.8 %attention_grad.3 = (bf16[2,208,2304]{2,1,0:T(8,128)(2,1)}, f32[12,208,256]{2,1,0:T(8,128)}) custom-call(bf16[2,208,2304]{2,1,0:T(8,128)(2,1)} %bitcast.243, f32[12,208,256]{2,1,0:T(8,128)} %bias_expand.2.bias_ref, f32[2,16,256]{2,1,0:T(8,128)} %get-tuple-element.69.lse_ref, bf16[2,208,768]{2,1,0:T(8,128)(2,1)} %bitcast.267), custom_call_target="tpu_custom_call" | custom-call | tf_op jit(solution)/shard_map/attention_grad/pallas_call | solution.py:224
  525.3 8.3 %bias_reduce.2 = (f32[12,16,512]{2,1,0:T(8,128)}, f32[12,8,128]{2,1,0:T(8,128)}) custom-call(f32[12,208,256]{2,1,0:T(8,128)} %get-tuple-element.76.g_ref), custom_call_target="tpu_custom_call" | custom-call | tf_op jit(solution)/shard_map/bias_reduce/pallas_call | solution.py:106
  536.5 3.8 reshape.320
  540.3 3.0 fusion.19
  547.5 5.3 fusion.59
  553.2 4.0 fusion
  559.1 4.9 constant_dynamic-update-slice_fusion.13
  564.0 2.5 constant_dynamic-update-slice_fusion.12
  573.3 66.5 %reduce-scatter.9.cloned.1.call-done = bf16[24,9344]{1,0:T(8,128)(2,1)} async-done(((bf16[768,9344]{1,0:T(8,128)(2,1)}), bf16[24,9344]{1,0:T(8,128)(2,1)}) %reduce-scatter.9.cloned.1.call-update) | async-done | bytes 448528
  641.3 168.4 %reduce-scatter.7.cloned.1.call-done = bf16[24,9344]{1,0:T(8,128)(2,1)} async-done(((bf16[768,9344]{1,0:T(8,128)(2,1)}), bf16[24,9344]{1,0:T(8,128)(2,1)}) %reduce-scatter.7.cloned.1.call-update) | async-done | bytes 448528
  (269 shorter events, 88.6 us)
Async XLA Ops:
  7.2 13.0 %copy-start.18 = (bf16[2,96,768]{2,1,0:T(8,128)(2,1)S(1)}, bf16[2,96,768]{2,1,0:T(8,128)(2,1)}, u32[]{:S(2)}) copy-start(bf16[2,96,768]{2,1,0:T(8,128)(2,1)} %param.38) | copy-start | bytes 884740
  7.2 121.0 %all-gather.5.cloned.1.call-start = ((), (), s32[]{:S(2)}) async-start(), calls=%async_computation.3 | async-start | bytes 14800896 | tf_op jit(solution)/shard_map/all_gather | solution.py:530
  18.3 5.1 copy-start.15
  20.4 0.8 copy-start.11
  21.2 212.7 %all-gather.3.cloned.1.call-start = ((), (), s32[]{:S(2)}) async-start(), calls=%async_computation.2 | async-start | bytes 14800896 | tf_op jit(solution)/shard_map/all_gather | solution.py:530
  22.6 0.8 copy-start.12
  23.4 1.1 copy-start.16
  23.4 616.4 %reduce-scatter.9.cloned.1.call-start = ((), (), s32[]{:S(2)}) async-start(), calls=%async_computation.5 | async-start | bytes 14800896
  24.2 0.7 copy-start.23
  236.5 3.4 copy-start.19
  247.0 3.1 copy-start.2
  247.0 3.3 copy-start.4
  247.0 3.4 copy-start.3
  275.9 7.8 copy-start.7
  315.5 1.7 copy-start
  428.0 7.6 slice-start.2
  428.0 5.7 copy-start.14
  428.0 5.7 copy-start.26
  428.0 7.6 slice-start.3
  451.6 4.2 copy-start.17
  455.7 5.0 copy-start.21
  477.6 1.3 copy-start.6
  477.7 332.0 %reduce-scatter.7.cloned.1.call-start = ((), (), s32[]{:S(2)}) async-start(), calls=%async_computation.4 | async-start | bytes 14800896
  507.3 3.3 copy-start.24
  540.3 4.8 copy-start.22
  545.0 2.5 copy-start.1
  547.5 5.4 copy-start.20
  553.2 4.0 copy-start.13
  553.2 4.0 copy-start.25
  557.2 6.8 slice-start
  559.1 4.9 slice-start.1
  567.4 1.3 copy-start.8
  568.8 1.5 copy-start.5
  810.8 1.0 copy-start.9
  810.8 1.2 copy-start.10
Sparse Core Ops, SparseCore 0:
  21.4 106.7 all-gather.4
  131.6 102.2 all-gather.2
  477.8 162.0 reduce-scatter.8
  647.0 162.6 reduce-scatter.6

commit v2 on v1

v2 whole, which is shorter than its diff:
```python
import functools
import math

import jax
import jax.numpy as jnp
import numpy as np
from jax import lax
from jax.experimental import pallas as pl
from jax.experimental.pallas import tpu as pltpu
from jax.sharding import PartitionSpec as P

GRID = 14
SPAN = 2 * GRID - 1
LAYERS = 2
IMG_ROWS = GRID * GRID + 1
PAD_ROWS = 208
LANES = 256
HEAD = 64
PAIR = 2 * HEAD
NEG = -1e30
TILE = 768
WIDE = 384
BLOCK = 16
SMALL_ROWS = 32
F32 = jnp.float32
B16 = jnp.bfloat16
AXES = ("dp", "fsdp")


def cost(us):
    return pl.CostEstimate(flops=us * 1_100_000_000, bytes_accessed=us * 3_500_000, transcendentals=0)


ANY = pl.BlockSpec(memory_space=pl.ANY)
SMEM = pl.BlockSpec(memory_space=pltpu.SMEM)

N1_GAIN, N1_SHIFT, Q_BIAS, V_BIAS, B_PROJ, G_ATTN, N2_GAIN, N2_SHIFT, B_TWO, G_MLP = range(10)
B_ONE = 10
TABLE = 14


def params(limit=56):
    return pltpu.CompilerParams(vmem_limit_bytes=limit * 1024 * 1024)


def dot(a, b, dims):
    return lax.dot_general(a, b, (dims, ((), ())), preferred_element_type=F32)


NN = ((1,), (0,))
NT = ((1,), (1,))
TN = ((0,), (0,))


def lane_onehot():
    out = np.zeros((WIDE, LANES), np.float32)
    for a in range(GRID):
        for b in range(GRID):
            out[SPAN * a + b, 1 + GRID * a + b] = 1.0
    return out


def row_onehot(turned):
    out = np.zeros((PAD_ROWS, BLOCK * GRID), np.float32)
    for c in range(GRID):
        for d in range(GRID):
            out[1 + GRID * c + d, BLOCK * c + (GRID - 1 - d if turned else d)] = 1.0
    return out


def bias_kernel(heads, small_ref, rows_ref, lanes_ref, out_ref, wide_ref):
    head = lax.rem(pl.program_id(0), heads)
    table = small_ref[0, pl.ds(TABLE + head, 1), :]
    shifted = pltpu.roll(jnp.broadcast_to(table, (BLOCK, TILE)), TILE - (GRID - 1), 1)
    shifted = pltpu.roll(shifted, 0, 1, stride=1, stride_axis=0)
    for c in range(GRID):
        start = SPAN * (GRID - 1 - c)
        wide_ref[BLOCK * c : BLOCK * (c + 1), :] = shifted[:, start : start + WIDE].astype(B16)
    narrow = dot(wide_ref[...], lanes_ref[...], NN).astype(B16)
    val = dot(rows_ref[...], narrow, NN)
    row = lax.broadcasted_iota(jnp.int32, (PAD_ROWS, LANES), 0)
    lane = lax.broadcasted_iota(jnp.int32, (PAD_ROWS, LANES), 1)
    cls = SPAN * SPAN
    val = jnp.where(lane == 0, table[:, cls : cls + 1], val)
    first = jnp.where(lane == 0, table[:, cls + 2 : cls + 3], table[:, cls + 1 : cls + 2])
    val = jnp.where(row == 0, first, val)
    out_ref[0] = jnp.where(row >= IMG_ROWS, NEG, val)


def build_bias(small, heads):
    layers = small.shape[0]
    return pl.pallas_call(
        functools.partial(bias_kernel, heads),
        grid=(layers * heads,),
        out_shape=jax.ShapeDtypeStruct((layers * heads, PAD_ROWS, LANES), F32),
        in_specs=[
            pl.BlockSpec((1, SMALL_ROWS, TILE), lambda h: (h // heads, 0, 0)),
            pl.BlockSpec((PAD_ROWS, BLOCK * GRID), lambda h: (0, 0)),
            pl.BlockSpec((WIDE, LANES), lambda h: (0, 0)),
        ],
        out_specs=pl.BlockSpec((1, PAD_ROWS, LANES), lambda h: (h, 0, 0)),
        scratch_shapes=[pltpu.VMEM((BLOCK * GRID, WIDE), B16)],
        compiler_params=params(),
        cost_estimate=cost(18),
        name="bias_expand",
    )(small, jnp.asarray(row_onehot(False), B16), jnp.asarray(lane_onehot(), B16))


def bias_grad_kernel(g_ref, rows_ref, lanes_ref, *refs):
    out_ref, acc_ref = refs[-2:]
    row = lax.broadcasted_iota(jnp.int32, (PAD_ROWS, LANES), 0)
    lane = lax.broadcasted_iota(jnp.int32, (PAD_ROWS, LANES), 1)
    g = jnp.where((lane < IMG_ROWS) & (row < IMG_ROWS), g_ref[0], 0.0)
    high = g.astype(B16)
    wide = None
    for part in (high, (g - high.astype(F32)).astype(B16)):
        moved = dot(rows_ref[...], part, NN).astype(B16)
        moved = dot(moved, lanes_ref[...], NN)
        wide = moved if wide is None else wide + moved
    acc_ref[...] = jnp.zeros_like(acc_ref)
    for c in range(GRID):
        start = SPAN * (GRID - 1 - c)
        acc_ref[:, start : start + WIDE] += wide[BLOCK * c : BLOCK * (c + 1), :]
    turned = pltpu.roll(acc_ref[...], 0, 1, stride=1, stride_axis=0)
    total = jnp.sum(turned, axis=0, keepdims=True)
    column = jnp.sum(jnp.where(lane[:, :1] == 0, g[:, :1], 0.0), axis=0, keepdims=True)
    to_self = g[0:1, 0:1]
    to_patch = column - to_self
    from_patch = jnp.sum(g[0:1, :], axis=1, keepdims=True) - to_self
    spot = lax.broadcasted_iota(jnp.int32, (1, TILE), 1)
    cls = SPAN * SPAN
    total = jnp.where(spot == cls, to_patch, total)
    total = jnp.where(spot == cls + 1, from_patch, total)
    out_ref[0] = jnp.where(spot == cls + 2, to_self, total)


def reduce_bias(grad, after=()):
    heads = grad.shape[0]
    out = pl.pallas_call(
        bias_grad_kernel,
        grid=(heads,),
        out_shape=jax.ShapeDtypeStruct((heads, 1, TILE), F32),
        in_specs=[
            pl.BlockSpec((1, PAD_ROWS, LANES), lambda h: (h, 0, 0)),
            pl.BlockSpec((BLOCK * GRID, PAD_ROWS), lambda h: (0, 0)),
            pl.BlockSpec((LANES, WIDE), lambda h: (0, 0)),
        ]
        + [ANY] * len(after),
        out_specs=pl.BlockSpec((1, 1, TILE), lambda h: (h, 0, 0)),
        scratch_shapes=[pltpu.VMEM((BLOCK, TILE), F32)],
        compiler_params=params(),
        cost_estimate=cost(11),
        name="bias_reduce",
    )(grad, jnp.asarray(row_onehot(True).T, B16), jnp.asarray(lane_onehot().T, B16), *after)
    return out.reshape(heads, TILE)


def head_mask(which):
    lane = lax.broadcasted_iota(jnp.int32, (PAD_ROWS, PAIR), 1)
    return (lane < HEAD) if which == 0 else (lane >= HEAD)


def attention_kernel(width, qkv_ref, bias_ref, out_ref, lse_ref):
    heads = width // HEAD
    for pair in range(heads // 2):
        at = pair * PAIR
        q = qkv_ref[0, :, at : at + PAIR]
        k = qkv_ref[0, :, width + at : width + at + PAIR]
        v = qkv_ref[0, :, 2 * width + at : 2 * width + at + PAIR]
        q = q * jnp.asarray(HEAD ** (-0.5), B16)
        v_t = v.T
        parts = []
        for t in range(2):
            head = 2 * pair + t
            q_t = jnp.where(head_mask(t), q, jnp.zeros_like(q))
            scores = dot(k, q_t, NT) + bias_ref[head, :, 0:PAD_ROWS]
            top = jnp.max(scores, axis=0, keepdims=True)
            weights = jnp.exp(scores - top)
            total = jnp.sum(weights, axis=0, keepdims=True)
            probs = (weights * (1.0 / total)).astype(B16)
            lse_ref[0, head : head + 1, 0:PAD_ROWS] = top + jnp.log(total)
            parts.append(dot(v_t[t * HEAD : (t + 1) * HEAD], probs, NN))
        out_ref[0, :, at : at + PAIR] = jnp.concatenate(parts, axis=0).T.astype(B16)


def attention_forward(qkv, bias, layer):
    images = qkv.shape[0]
    width = qkv.shape[2] // 3
    heads = width // HEAD
    return pl.pallas_call(
        functools.partial(attention_kernel, width),
        grid=(images,),
        out_shape=(
            jax.ShapeDtypeStruct((images, PAD_ROWS, width), B16),
            jax.ShapeDtypeStruct((images, 16, LANES), F32),
        ),
        in_specs=[
            pl.BlockSpec((1, PAD_ROWS, 3 * width), lambda i: (i, 0, 0)),
            pl.BlockSpec((heads, PAD_ROWS, LANES), lambda i: (layer, 0, 0)),
        ],
        out_specs=(
            pl.BlockSpec((1, PAD_ROWS, width), lambda i: (i, 0, 0)),
            pl.BlockSpec((1, 16, LANES), lambda i: (i, 0, 0)),
        ),
        compiler_params=params(),
        cost_estimate=cost(8),
        name="attention",
    )(qkv, bias)


def attention_grad_kernel(width, qkv_ref, bias_ref, lse_ref, g_ref, *refs):
    out_ref, dbias_ref = refs[-2:]
    heads = width // HEAD
    scale = HEAD ** (-0.5)

    @pl.when(pl.program_id(0) == 0)
    def _():
        dbias_ref[...] = jnp.zeros_like(dbias_ref)

    for pair in range(heads // 2):
        at = pair * PAIR
        q = qkv_ref[0, :, at : at + PAIR]
        k = qkv_ref[0, :, width + at : width + at + PAIR]
        v = qkv_ref[0, :, 2 * width + at : 2 * width + at + PAIR]
        g = g_ref[0, :, at : at + PAIR]
        q = q * jnp.asarray(scale, B16)
        k_t = k.T
        dq_parts = []
        dk = None
        dv = None
        for t in range(2):
            head = 2 * pair + t
            q_t = jnp.where(head_mask(t), q, jnp.zeros_like(q))
            g_t = jnp.where(head_mask(t), g, jnp.zeros_like(g))
            scores = dot(k, q_t, NT) + bias_ref[head, :, 0:PAD_ROWS]
            probs = jnp.exp(scores - lse_ref[0, head : head + 1, 0:PAD_ROWS])
            dprobs = dot(v, g_t, NT)
            dv_t = dot(probs.astype(B16), g_t, NN)
            mean = jnp.sum(probs * dprobs, axis=0, keepdims=True)
            dscores = (probs * (dprobs - mean)).astype(B16)
            dbias_ref[head, :, 0:PAD_ROWS] += dscores.astype(F32)
            dk_t = dot(dscores, q_t, NN)
            dq_parts.append(dot(k_t[t * HEAD : (t + 1) * HEAD], dscores, NN))
            dk = dk_t if dk is None else dk + dk_t
            dv = dv_t if dv is None else dv + dv_t
        dq = jnp.concatenate(dq_parts, axis=0).T * scale
        out_ref[0, :, at : at + PAIR] = dq.astype(B16)
        out_ref[0, :, width + at : width + at + PAIR] = dk.astype(B16)
        out_ref[0, :, 2 * width + at : 2 * width + at + PAIR] = dv.astype(B16)


def attention_backward(qkv, bias, lse, grad, layer, after=()):
    images = qkv.shape[0]
    width = qkv.shape[2] // 3
    heads = width // HEAD
    return pl.pallas_call(
        functools.partial(attention_grad_kernel, width),
        grid=(images,),
        out_shape=(
            jax.ShapeDtypeStruct((images, PAD_ROWS, 3 * width), B16),
            jax.ShapeDtypeStruct((heads, PAD_ROWS, LANES), F32),
        ),
        in_specs=[
            pl.BlockSpec((1, PAD_ROWS, 3 * width), lambda i: (i, 0, 0)),
            pl.BlockSpec((heads, PAD_ROWS, LANES), lambda i: (layer, 0, 0)),
            pl.BlockSpec((1, 16, LANES), lambda i: (i, 0, 0)),
            pl.BlockSpec((1, PAD_ROWS, width), lambda i: (i, 0, 0)),
        ]
        + [ANY] * len(after),
        out_specs=(
            pl.BlockSpec((1, PAD_ROWS, 3 * width), lambda i: (i, 0, 0)),
            pl.BlockSpec((heads, PAD_ROWS, LANES), lambda i: (0, 0, 0)),
        ),
        compiler_params=params(),
        cost_estimate=cost(12),
        name="attention_grad",
    )(qkv, bias, lse, grad, *after)


def normalize(x):
    centered = x - jnp.mean(x, -1, keepdims=True)
    scale = lax.rsqrt(jnp.mean(centered * centered, -1, keepdims=True) + 1e-06)
    return centered * scale, scale


def normalize_grad(x_hat, scale, dy):
    return scale * (
        dy - jnp.mean(dy, -1, keepdims=True) - x_hat * jnp.mean(dy * x_hat, -1, keepdims=True)
    )


def gelu_and_slope(x):
    t = 1.0 / (1.0 + (0.3275911 / math.sqrt(2.0)) * jnp.abs(x))
    bell = jnp.exp(-0.5 * x * x)
    poly = 0.5 * 1.061405429
    for coef in (-1.453152027, 1.421413741, -0.284496736, 0.254829592):
        poly = poly * t + 0.5 * coef
    tail = poly * t * bell
    phi = jnp.where(x >= 0, 1.0 - tail, tail)
    return x * phi, phi + x * bell * (1.0 / math.sqrt(2.0 * math.pi))


def total_rows(v):
    return jnp.sum(v, axis=0, keepdims=True)


def small_spec(layer):
    return pl.BlockSpec((1, SMALL_ROWS, TILE), lambda i: (layer, 0, 0))


def whole_spec(shape):
    return pl.BlockSpec(shape, lambda i: (0,) * len(shape))


def col_spec(weight):
    array, first = weight
    return pl.BlockSpec((array.shape[0], TILE), lambda i: (0, first + i))


def qkv_kernel(x_ref, small_ref, w_ref, qkv_ref, h_ref):
    step = pl.program_id(0)

    @pl.when(step == 0)
    def _():
        x_hat, _ = normalize(x_ref[...])
        gain = small_ref[0, N1_GAIN : N1_GAIN + 1]
        h_ref[...] = (x_hat * gain + small_ref[0, N1_SHIFT : N1_SHIFT + 1]).astype(B16)

    zero = jnp.zeros((1, TILE), F32)
    bias = jnp.where(step == 0, small_ref[0, Q_BIAS : Q_BIAS + 1], zero)
    bias = jnp.where(step == 2, small_ref[0, V_BIAS : V_BIAS + 1], bias)
    qkv_ref[...] = (dot(h_ref[...], w_ref[...], NN) + bias).astype(B16)


def qkv_forward(x, small, layer, w_qkv):
    rows, width = x.shape
    return pl.pallas_call(
        qkv_kernel,
        grid=(3,),
        out_shape=(
            jax.ShapeDtypeStruct((rows, 3 * width), B16),
            jax.ShapeDtypeStruct((rows, width), B16),
        ),
        in_specs=[whole_spec((rows, width)), small_spec(layer), col_spec(w_qkv)],
        out_specs=(
            pl.BlockSpec((rows, TILE), lambda i: (0, i)),
            whole_spec((rows, width)),
        ),
        compiler_params=params(),
        cost_estimate=cost(6),
        name="qkv",
    )(x, small, w_qkv[0])


def qkv_grad_kernel(core_ref, g_ref, h_ref, x_ref, dmid_ref, small_ref, w_ref, *refs):
    theirs_ref, mine_ref, dx_ref, sums_ref, ht_ref, dh_ref = refs[-6:]
    step = pl.program_id(0)

    @pl.when(step == 0)
    def _():
        ht_ref[...] = h_ref[...].T
        sums_ref[...] = jnp.zeros_like(sums_ref)

    g = g_ref[...]
    dw = dot(ht_ref[...], g, NN).astype(B16)
    low, high = dw[:, : TILE // 2], dw[:, TILE // 2 :]

    @pl.when(core_ref[0] == 0)
    def _():
        mine_ref[...] = low
        theirs_ref[...] = high

    @pl.when(core_ref[0] != 0)
    def _():
        mine_ref[...] = high
        theirs_ref[...] = low

    part = dot(g, w_ref[...], NT)
    total = total_rows(g.astype(F32))

    @pl.when(step == 0)
    def _():
        dh_ref[...] = part
        sums_ref[Q_BIAS : Q_BIAS + 1] = total

    @pl.when(step > 0)
    def _():
        dh_ref[...] += part

    @pl.when(step == 2)
    def _():
        sums_ref[V_BIAS : V_BIAS + 1] = total
        dh = dh_ref[...]
        x_hat, scale = normalize(x_ref[...])
        sums_ref[N1_GAIN : N1_GAIN + 1] = total_rows(dh * x_hat)
        sums_ref[N1_SHIFT : N1_SHIFT + 1] = total_rows(dh)
        gain = small_ref[0, N1_GAIN : N1_GAIN + 1]
        dx_ref[...] = dmid_ref[...] + normalize_grad(x_hat, scale, dh * gain)


def qkv_backward(core, grad, h, x, d_mid, small, layer, w_qkv, after=()):
    rows, width = x.shape
    whole = whole_spec((rows, width))
    tiles = pl.BlockSpec((rows, TILE), lambda i: (0, i))
    return pl.pallas_call(
        qkv_grad_kernel,
        grid=(3,),
        out_shape=(
            jax.ShapeDtypeStruct((width, 3 * width // 2), B16),
            jax.ShapeDtypeStruct((width, 3 * width // 2), B16),
            jax.ShapeDtypeStruct((rows, width), F32),
            jax.ShapeDtypeStruct((8, width), F32),
        ),
        in_specs=[SMEM, tiles, whole, whole, whole, small_spec(layer), col_spec(w_qkv)]
        + [ANY] * len(after),
        out_specs=(
            pl.BlockSpec((width, TILE // 2), lambda i: (0, i)),
            pl.BlockSpec((width, TILE // 2), lambda i: (0, i)),
            whole,
            whole_spec((8, width)),
        ),
        scratch_shapes=[pltpu.VMEM((width, rows), B16), pltpu.VMEM((rows, width), F32)],
        compiler_params=params(),
        cost_estimate=cost(11),
        name="qkv_grad",
    )(core, grad, h, x, d_mid, small, w_qkv[0], *after)


def mlp_kernel(
    x_ref, att_ref, small_ref, wp_ref, w1_ref, w2_ref,
    out_ref, branch_ref, mid_ref, mlp_ref, h2_ref, act_ref, slope_ref,
):
    step = pl.program_id(0)

    def vec(i):
        return small_ref[0, i : i + 1]

    @pl.when(step == 0)
    def _():
        branch = dot(att_ref[...], wp_ref[...], NN) + vec(B_PROJ)
        branch_ref[...] = branch
        mid = x_ref[...] + vec(G_ATTN) * branch
        mid_ref[...] = mid
        x_hat, _ = normalize(mid)
        h2_ref[...] = (x_hat * vec(N2_GAIN) + vec(N2_SHIFT)).astype(B16)

    pre = dot(h2_ref[...], w1_ref[...], NN) + small_ref[0, pl.ds(B_ONE + step, 1)]
    act, slope = gelu_and_slope(pre)
    act = act.astype(B16)
    act_ref[...] = act
    slope_ref[...] = slope.astype(B16)
    part = dot(act, w2_ref[...], NN)

    @pl.when(step == 0)
    def _():
        mlp_ref[...] = part + vec(B_TWO)

    @pl.when(step > 0)
    def _():
        mlp_ref[...] += part

    @pl.when(step == pl.num_programs(0) - 1)
    def _():
        out_ref[...] = mid_ref[...] + vec(G_MLP) * mlp_ref[...]


def mlp_forward(x, att, small, layer, w_proj, w_one, w_two):
    rows, width = x.shape
    hidden = w_two.shape[0]
    whole = whole_spec((rows, width))
    cols = pl.BlockSpec((rows, TILE), lambda i: (0, i))
    full = jax.ShapeDtypeStruct((rows, width), F32)
    proj_at = w_proj[1]
    return pl.pallas_call(
        mlp_kernel,
        grid=(hidden // TILE,),
        out_shape=(
            full, full, full, full,
            jax.ShapeDtypeStruct((rows, width), B16),
            jax.ShapeDtypeStruct((rows, hidden), B16),
            jax.ShapeDtypeStruct((rows, hidden), B16),
        ),
        in_specs=[
            whole,
            whole,
            small_spec(layer),
            pl.BlockSpec((width, TILE), lambda i: (0, proj_at)),
            col_spec(w_one),
            pl.BlockSpec((TILE, width), lambda i: (i, 0)),
        ],
        out_specs=(whole, whole, whole, whole, whole, cols, cols),
        compiler_params=params(),
        cost_estimate=cost(15),
        name="mlp",
    )(x, att, small, w_proj[0], w_one[0], w_two)


SUM_ROWS = 16
STRIP = 128


def mlp_grad_kernel(
    core_ref, g_ref, mid_ref, mlp_ref, branch_ref, att_ref, small_ref, h2_ref, act_ref, slope_ref, wp_ref,
    w1_ref, w2_ref, *refs,
):
    (theirs_ref, mine_ref, dmid_ref, datt_ref, sums_ref,
     dmlp_ref, h2t_ref, dh2_ref, one_ref, wide_ref, two_ref, proj_ref, sems) = refs[-13:]
    step = pl.program_id(0)
    steps = pl.num_programs(0)
    slot = lax.rem(step, 2)
    width = mid_ref.shape[1]
    hidden = 4 * width
    part_rows = TILE // 4

    def vec(i):
        return small_ref[0, i : i + 1]

    def put(row, value):
        at = row - B_PROJ
        sums_ref[at : at + 1] = value

    def copy_one(out_ref, j, s):
        return pltpu.make_async_copy(
            one_ref.at[s],
            out_ref.at[:, pl.ds(pl.multiple_of(lax.rem(j, 2) * TILE, TILE), TILE)],
            sems.at[0, s],
        )

    def copy_two(out_ref, j, s, which):
        return pltpu.make_async_copy(
            two_ref.at[s, which],
            out_ref.at[pl.ds(pl.multiple_of(j * part_rows, part_rows), part_rows),
                       pl.ds(2 * width, 2 * width)],
            sems.at[1 + which, s],
        )

    def proj_copy(out_ref, which):
        return pltpu.make_async_copy(
            proj_ref.at[which], out_ref.at[:, pl.ds(4 * width, width // 2)], sems.at[3, which]
        )

    def on_halves(run):
        for core in range(2):

            @pl.when(core_ref[0] == core)
            def _(core=core):
                run(mine_ref, core)
                run(theirs_ref, 1 - core)

    def send_one(j, s):
        def run(out_ref, which):
            @pl.when(j // 2 == which)
            def _():
                copy_one(out_ref, j, s).start()

        on_halves(run)

    def send_two(j, s):
        on_halves(lambda out_ref, which: copy_two(out_ref, j, s, which).start())

    def wait_step(j, s):
        copy_one(mine_ref, j, s).wait()
        for which in range(2):
            copy_two(mine_ref, j, s, which).wait()

    @pl.when(step == 0)
    def _():
        g = g_ref[...]
        dmlp = (g * vec(G_MLP)).astype(B16)
        dmlp_ref[...] = dmlp
        h2t_ref[...] = h2_ref[...].T
        sums_ref[...] = jnp.zeros_like(sums_ref)
        put(G_MLP, total_rows(g * mlp_ref[...]))
        put(B_TWO, total_rows(dmlp.astype(F32)))

    @pl.when(step >= 2)
    def _():
        wait_step(step - 2, slot)

    dmlp = dmlp_ref[...]
    dact = dot(dmlp, w2_ref[...], NT)
    dpre = (dact * slope_ref[...].astype(F32)).astype(B16)
    wide = dot(act_ref[...].T, dmlp, NN)
    for t in range(wide_ref.shape[0]):
        wide_ref[t] = wide[:, t * STRIP : (t + 1) * STRIP]
        for k in range(4):
            at = (k % 2) * width + t * STRIP
            two_ref[slot, k // 2, :, at : at + STRIP] = wide_ref[
                t, pl.ds(k, part_rows, stride=4), :
            ].astype(B16)
    send_two(step, slot)
    one_ref[slot] = dot(h2t_ref[...], dpre, NN).astype(B16)
    send_one(step, slot)
    sums_ref[pl.ds(B_ONE - B_PROJ + step, 1)] = total_rows(dpre.astype(F32))
    part = dot(dpre, w1_ref[...], NT)

    @pl.when(step == 0)
    def _():
        dh2_ref[...] = part

    @pl.when(step > 0)
    def _():
        dh2_ref[...] += part

    @pl.when(step == steps - 1)
    def _():
        x_hat, scale = normalize(mid_ref[...])
        dh2 = dh2_ref[...]
        put(N2_GAIN, total_rows(dh2 * x_hat))
        put(N2_SHIFT, total_rows(dh2))
        dmid = g_ref[...] + normalize_grad(x_hat, scale, dh2 * vec(N2_GAIN))
        dmid_ref[...] = dmid
        dbranch = (dmid * vec(G_ATTN)).astype(B16)
        put(G_ATTN, total_rows(dmid * branch_ref[...]))
        put(B_PROJ, total_rows(dbranch.astype(F32)))
        dproj = dot(att_ref[...].T, dbranch, NN).astype(B16)
        proj_ref[0] = dproj[:, : width // 2]
        proj_ref[1] = dproj[:, width // 2 :]
        on_halves(lambda out_ref, which: proj_copy(out_ref, which).start())
        datt_ref[...] = dot(dbranch, wp_ref[...], NT).astype(B16)
        wait_step(step - 1, 1 - slot)
        wait_step(step, slot)
        for which in range(2):
            proj_copy(mine_ref, which).wait()


def mlp_backward(core, grad, mid, mlp_out, branch, att, small, layer, h2, act, slope, w_proj, w_one,
                 w_two, after=()):
    rows, width = mid.shape
    hidden = w_two.shape[0]
    whole = whole_spec((rows, width))
    cols = pl.BlockSpec((rows, TILE), lambda i: (0, i))
    proj_at = w_proj[1]
    return pl.pallas_call(
        mlp_grad_kernel,
        grid=(hidden // TILE,),
        out_shape=(
            jax.ShapeDtypeStruct((width, hidden + width // 2), B16),
            jax.ShapeDtypeStruct((width, hidden + width // 2), B16),
            jax.ShapeDtypeStruct((rows, width), F32),
            jax.ShapeDtypeStruct((rows, width), B16),
            jax.ShapeDtypeStruct((SUM_ROWS, width), F32),
        ),
        in_specs=[
            SMEM, whole, whole, whole, whole, whole, small_spec(layer), whole, cols, cols,
            pl.BlockSpec((width, TILE), lambda i: (0, proj_at)),
            col_spec(w_one),
            pl.BlockSpec((TILE, width), lambda i: (i, 0)),
        ]
        + [ANY] * len(after),
        out_specs=(ANY, ANY, whole, whole, whole_spec((SUM_ROWS, width))),
        scratch_shapes=[
            pltpu.VMEM((rows, width), B16),
            pltpu.VMEM((width, rows), B16),
            pltpu.VMEM((rows, width), F32),
            pltpu.VMEM((2, width, TILE), B16),
            pltpu.VMEM((width // STRIP, TILE, STRIP), F32),
            pltpu.VMEM((2, 2, TILE // 4, 2 * width), B16),
            pltpu.VMEM((2, width, width // 2), B16),
            pltpu.SemaphoreType.DMA((4, 2)),
        ],
        compiler_params=params(),
        cost_estimate=cost(20),
        name="mlp_grad",
    )(core, grad, mid, mlp_out, branch, att, small, h2, act, slope, w_proj[0], w_one[0], w_two, *after)


CHIP_Y, CORES, CHIP_Z, CHIP_X = 2, 2, 4, 2
FAST_SHARDS = CHIP_Y * CORES * CHIP_Z * CHIP_X

def place(y, c, z, x):
    return (y * CORES + c) * (CHIP_Z * CHIP_X) + z * CHIP_X + x

def moves(fn):
    pairs = []
    for y in range(CHIP_Y):
        for c in range(CORES):
            for z in range(CHIP_Z):
                for x in range(CHIP_X):
                    pairs.append((place(y, c, z, x), place(*fn(y, c, z, x))))
    return pairs

CORE_SWAP = moves(lambda y, c, z, x: (y, 1 - c, z, x))
PLANE = (
    moves(lambda y, c, z, x: (y, c, z, 1 - x) if c == 0 else (1 - y, c, z, x)),
    moves(lambda y, c, z, x: (1 - y, c, z, x) if c == 0 else (y, c, z, 1 - x)),
)
X_SWAP = moves(lambda y, c, z, x: (y, c, z, 1 - x))
Y_SWAP = moves(lambda y, c, z, x: (1 - y, c, z, x))
Z_SHIFT = [moves(lambda y, c, z, x, k=k: (y, c, (z + k) % CHIP_Z, x)) for k in range(CHIP_Z)]

def send(v, pairs):
    return lax.ppermute(v, AXES, pairs)

def my_place():
    dp = lax.axis_index("dp"); fs = lax.axis_index("fsdp")
    return dp // CORES, dp % CORES, fs // CHIP_X, fs % CHIP_X

def half_of(v, which):
    h = v.shape[-1] // 2
    return lax.dynamic_slice_in_dim(v, which * h, h, axis=v.ndim - 1)

def no_sooner(arrays):
    zero = jnp.zeros((), B16)
    for v in arrays:
        zero = zero + jnp.minimum(jnp.abs(v.reshape(-1)[0]), 0)
    return zero


class Gathering:
    def __init__(self, mats):
        self.mats = mats
        _, c, _, _ = my_place()

        def pick(which):
            return jnp.concatenate(
                [half_of(m, which)[i] for m in mats for i in range(m.shape[0])], axis=-1
            )

        self.piece = jnp.stack([pick(c), send(pick(1 - c), CORE_SWAP)])

    def along(self, behind=()):
        piece = self.piece + no_sooner(behind) if behind else self.piece
        self.moved = [send(piece, Z_SHIFT[k]) for k in range(1, CHIP_Z)]
        return self.moved

    def plane(self):
        base = jnp.stack([self.piece] + self.moved)
        first = send(base, PLANE[0])
        self.own = [base, first, send(base, PLANE[1]), send(first, PLANE[1])]
        self.other = [send(v, CORE_SWAP) for v in self.own]

    def finish(self, after=()):
        return assemble(self.own, self.other, self.mats, after)


def assemble_kernel(counts, widths, pos_ref, *refs):
    src = refs[:8]; outs = refs[-1 - len(counts):-1]; sem = refs[-1]
    y, c, z, x = (pos_ref[i] for i in range(4))
    copies = []
    for side in range(2):
        core = c if side == 0 else 1 - c
        for a in range(4):
            for e in range(4):
                f1, f2 = a & 1, a >> 1
                fx = jnp.where(core == 0, f1, f2)
                fy = jnp.where(core == 0, f2, f1)
                yy = (y + fy) % 2
                xx = (x + fx) % 2
                zz = (z + CHIP_Z - e) % CHIP_Z
                for dc in range(2):
                    cc = core if dc == 0 else 1 - core
                    d = place(yy, cc, zz, xx)
                    col = 0
                    for out, count, w in zip(outs, counts, widths):
                        for k in range(count):
                            cp = pltpu.make_async_copy(
                                src[side * 4 + a].at[e, dc, :, pl.ds(col, w)],
                                out.at[d, k, :, pl.ds(pl.multiple_of(core * w, 128), w)],
                                sem,
                            )
                            cp.start(); copies.append(cp)
                            col += w
    for cp in copies:
        cp.wait()

def assemble(own, other, mats, after=()):
    rows = mats[0].shape[1]
    counts = [m.shape[0] for m in mats]; widths = [m.shape[2] // 2 for m in mats]
    pos = jnp.stack([p.astype(jnp.int32) for p in my_place()])
    return pl.pallas_call(
        functools.partial(assemble_kernel, counts, widths),
        out_shape=[jax.ShapeDtypeStruct((FAST_SHARDS, n, rows, 2 * w), B16) for n, w in zip(counts, widths)],
        in_specs=[pl.BlockSpec(memory_space=pltpu.SMEM)] + [ANY] * (8 + len(after)),
        out_specs=[pl.BlockSpec(memory_space=pltpu.VMEM)] * len(counts),
        scratch_shapes=[pltpu.SemaphoreType.DMA],
        compiler_params=params(),
        cost_estimate=cost(7),
        name="assemble",
    )(pos, *own, *other, *after)


def sum_plane(v):
    for pairs in (CORE_SWAP, X_SWAP, Y_SWAP):
        v = v + send(v, pairs)
    return v


def sum_everywhere(v):
    v = sum_plane(v)
    parts = [send(v, Z_SHIFT[k]) for k in range(1, CHIP_Z)]
    return v + parts[0] + parts[1] + parts[2]


class Reduction:
    def __init__(self, theirs, mine):
        self.theirs = theirs
        self.own = mine
        self.y, self.c, self.z, self.x = my_place()
        self.split = (CHIP_Y, CORES, CHIP_Z, CHIP_X, mine.shape[0] // FAST_SHARDS)

    def swap(self):
        self.got = send(self.theirs, CORE_SWAP)
        return [self.got]

    def part(self, f1, f2):
        c = self.c
        fx = jnp.where(c == 0, f1, f2)
        fy = jnp.where(c == 0, f2, f1)

        def cut(v):
            v = v.reshape(self.split + (v.shape[-1],))
            at = ((self.y + fy) % CHIP_Y, 0, 0, (self.x + fx) % CHIP_X, 0, 0)
            size = (1, CORES, CHIP_Z, 1) + v.shape[4:]
            return lax.dynamic_slice(v, at, size)[0, :, :, 0].astype(F32)

        return cut(self.own) + cut(self.got)

    def far(self):
        self.r3 = send(self.part(1, 1).astype(B16), PLANE[1])
        self.r2 = send(self.part(0, 1).astype(B16), PLANE[1])
        return [self.r3, self.r2]

    def near(self):
        self.r1 = send((self.part(1, 0) + self.r3.astype(F32)).astype(B16), PLANE[0])
        return [self.r1]

    def along(self):
        base = self.part(0, 0) + self.r2.astype(F32) + self.r1.astype(F32)

        def at_z(k):
            return lax.dynamic_slice_in_dim(base, (self.z + k) % CHIP_Z, 1, axis=1)[:, 0]

        self.mine = at_z(0)
        self.rz = [send(at_z(k).astype(B16), Z_SHIFT[k]) for k in range(1, CHIP_Z)]
        return self.rz

    def finish(self):
        total = self.mine
        for r in self.rz:
            total = total + r.astype(F32)
        c = self.c
        keep = lax.dynamic_slice_in_dim(total, c, 1, axis=0)[0]
        give = lax.dynamic_slice_in_dim(total, 1 - c, 1, axis=0)[0]
        other = send(give, CORE_SWAP)
        first = jnp.where(c == 0, keep, other)
        second = jnp.where(c == 0, other, keep)
        return first, second


def unpack_kernel(first, src_ref, *refs):
    out_ref, sem = refs[-2:]
    shards, ratio, _, width = out_ref.shape
    copies = []
    for d in range(shards):
        for k in range(ratio):
            copy = pltpu.make_async_copy(
                src_ref.at[d, :, pl.ds(first + k * width, width)], out_ref.at[d, k], sem
            )
            copy.start()
            copies.append(copy)
    for copy in copies:
        copy.wait()


def unpack_two(packed, first, ratio, width, after=()):
    shards, rows, _ = packed.shape
    return pl.pallas_call(
        functools.partial(unpack_kernel, first),
        out_shape=jax.ShapeDtypeStruct((shards, ratio, rows, width), B16),
        in_specs=[ANY] * (1 + len(after)),
        out_specs=pl.BlockSpec(memory_space=pltpu.VMEM),
        scratch_shapes=[pltpu.SemaphoreType.DMA],
        compiler_params=params(),
        cost_estimate=cost(5),
        name="unpack",
    )(packed, *after)


def per_device(
    shards, fast,
    tokens, masked_rows, cotangent, norm1_gain, norm1_bias, qkv_weight, q_bias, v_bias,
    proj_weight, proj_bias, gamma_attn, norm2_gain, norm2_bias, fc1_weight, fc1_bias,
    fc2_weight, fc2_bias, gamma_mlp, rel_table,
):
    vectors = (norm1_gain, norm1_bias, q_bias, v_bias, proj_bias, gamma_attn, norm2_gain,
               norm2_bias, fc2_bias, gamma_mlp)
    width = tokens.shape[1]
    images = masked_rows.shape[0]
    heads, entries = rel_table.shape[1:]
    own = qkv_weight.shape[1]
    ratio = fc2_weight.shape[1] // own
    hidden = fc1_weight.shape[2]
    me = lax.axis_index("dp") * lax.axis_size("fsdp") + lax.axis_index("fsdp")

    def pad_rows(v):
        v = v.astype(F32).reshape(images, IMG_ROWS, width)
        v = jnp.pad(v, ((0, 0), (0, PAD_ROWS - IMG_ROWS), (0, 0)))
        return v.reshape(images * PAD_ROWS, width)

    def cut_rows(v):
        return v.reshape(images, PAD_ROWS, width)[:, :IMG_ROWS].reshape(images * IMG_ROWS, width)

    def everywhere(v):
        return sum_everywhere(v) if fast else lax.psum(v, AXES)

    def placed(shard, total):
        empty = jnp.zeros(shard.shape[:-1] + (total,), shard.dtype)
        at = (0,) * (shard.ndim - 1) + (me * shard.shape[-1],)
        return lax.dynamic_update_slice(empty, shard, at)

    small = jnp.concatenate(
        [
            placed(jnp.stack(vectors, axis=1), width),
            placed(fc1_bias, hidden).reshape(LAYERS, ratio, width),
            placed(rel_table, TILE),
        ],
        axis=1,
    )
    used = small.shape[1]
    small = everywhere(small.reshape(LAYERS * used, width)).reshape(LAYERS, used, width)
    small = jnp.pad(small.astype(F32), ((0, 0), (0, SMALL_ROWS - used), (0, 0)))
    bias = build_bias(small, heads)

    def two_blocks(layer):
        return fc2_weight[layer].reshape(ratio, own, width)

    def fetch_packed(layer):
        two = two_blocks(layer)
        block = jnp.concatenate(
            [qkv_weight[layer], proj_weight[layer], fc1_weight[layer]]
            + [two[i] for i in range(ratio)],
            axis=1,
        )
        return lax.all_gather(block, AXES, axis=0, tiled=True)

    packed_weights = [None if fast and layer == 0 else fetch_packed(layer) for layer in range(LAYERS)]
    if fast:
        first = Gathering([qkv_weight[0][None], proj_weight[0][None]])
        second = Gathering([fc1_weight[0][None], two_blocks(0)])
        second.along(first.along())
        first.plane()
        second.plane()
    weights = []
    x = pad_rows(tokens)
    saved = []
    for layer in range(LAYERS):
        full = packed_weights[layer]
        if full is None:
            w_qkv, w_proj = first.finish([bias])
            w_qkv = (w_qkv.reshape(width, 3 * width), 0)
            w_proj = (w_proj.reshape(width, width), 0)
        else:
            w_qkv, w_proj, w_one = (full, 0), (full, 3), (full, 4)
        qkv, h = qkv_forward(x, small, layer, w_qkv)
        qkv = qkv.reshape(images, PAD_ROWS, 3 * width)
        att, lse = attention_forward(qkv, bias, layer)
        att = att.reshape(images * PAD_ROWS, width)
        if full is None:
            w_one, w_two = second.finish([att])
            w_one = (w_one.reshape(width, hidden), 0)
        elif fast:
            w_two = unpack_two(full.reshape(shards, own, -1), 4 * width + hidden, ratio, width)
        else:
            w_two = full[:, 4 * width + hidden :].reshape(shards, own, ratio, width)
            w_two = w_two.transpose(0, 2, 1, 3)
        w_two = w_two.reshape(hidden, width)
        weights.append((w_qkv, w_proj, w_one, w_two))
        out, branch, mid, mlp_out, h2, act, slope = mlp_forward(
            x, att, small, layer, w_proj, w_one, w_two
        )
        saved.append((x, h, qkv, lse, att, branch, mid, mlp_out, h2, act, slope))
        x = out
    encoded = cut_rows(x.astype(B16))

    positions = jnp.arange(IMG_ROWS, dtype=jnp.int32)
    mask = jnp.any(masked_rows[:, :, None] == positions[None, None, :], axis=1)
    mask = jnp.pad(mask, ((0, 0), (0, PAD_ROWS - IMG_ROWS))).reshape(-1, 1)
    grad = jnp.where(mask, pad_rows(cotangent), 0.0)

    def scatter(theirs, mine):
        both = jnp.stack([mine, theirs])
        own_part = lax.psum_scatter(both, AXES, scatter_dimension=1, tiled=True).astype(F32)
        return own_part[0], own_part[1]

    core = (lax.axis_index("dp") % CORES if fast else jnp.int32(0)).astype(jnp.int32).reshape(1)
    reduced = [None] * LAYERS
    small_grads = [None] * LAYERS
    tables = [None] * LAYERS

    def backward(layer, grad, hooks):
        x, h, qkv, lse, att, branch, mid, mlp_out, h2, act, slope = saved[layer]
        w_qkv, w_proj, w_one, w_two = weights[layer]
        theirs, mine, d_mid, d_att, mlp_sums = mlp_backward(
            core, grad, mid, mlp_out, branch, att, small, layer, h2, act, slope, w_proj, w_one,
            w_two, hooks[0](),
        )
        main = (theirs, mine)
        d_qkv, d_bias = attention_backward(
            qkv, bias, lse, d_att.reshape(images, PAD_ROWS, width), layer, hooks[1](main)
        )
        theirs, mine, grad, qkv_sums = qkv_backward(
            core, d_qkv.reshape(images * PAD_ROWS, 3 * width), h, x, d_mid, small, layer, w_qkv,
            hooks[2](),
        )
        small_grads[layer] = (qkv_sums, mlp_sums)
        tables[layer] = d_bias
        return grad, main, (theirs, mine)

    if not fast:
        for layer in reversed(range(LAYERS)):
            none = (lambda: (), lambda main: (), lambda: ())
            grad, main, rest = backward(layer, grad, none)
            reduced[layer] = (scatter(*main), scatter(*rest))
        tables = [reduce_bias(t) for t in tables]
    else:
        a1, b1, a0, b0 = (None,) * 4

        def one_attention(main):
            nonlocal a1
            a1 = Reduction(*main)
            return ()

        def one_qkv():
            return a1.swap()

        grad, _, rest = backward(1, grad, (lambda: (), one_attention, one_qkv))
        b1 = Reduction(*rest)
        a1.far()

        def zero_mlp():
            return ()

        def zero_attention(main):
            nonlocal a0
            a0 = Reduction(*main)
            b1.swap()
            return [a1.r3, a1.r2, b1.got]

        def zero_qkv():
            return a1.near() + b1.far() + a0.swap()

        grad, _, rest = backward(0, grad, (zero_mlp, zero_attention, zero_qkv))
        b0 = Reduction(*rest)
        a0.far()
        a1.along()
        b1.near()
        b0.swap()
        tables[1] = reduce_bias(tables[1])
        b0.far()
        a0.near()
        b1.along()
        tables[0] = reduce_bias(tables[0])
        a0.along()
        b0.near()
        b0.along()
        reduced[1] = (a1.finish(), b1.finish())
        reduced[0] = (a0.finish(), b0.finish())

    rows = []
    for (qkv_sums, mlp_sums), table in zip(small_grads, tables):
        rows += [qkv_sums[:4], mlp_sums[: TABLE - B_PROJ], table]
    totals = jnp.concatenate(rows, axis=0)
    totals = sum_plane(totals) if fast else lax.psum(totals, AXES)
    totals = totals.reshape(LAYERS, used, width)

    def owned_by(device):
        def cut(v, size):
            return lax.dynamic_slice_in_dim(v, device * size, size, axis=v.ndim - 1)

        g_vec = cut(totals[:, :B_ONE], own).reshape(LAYERS, -1)
        g_b1 = cut(totals[:, B_ONE:TABLE].reshape(LAYERS, hidden), ratio * own)
        g_tab = cut(totals[:, TABLE:], entries).reshape(LAYERS, -1)
        return jnp.concatenate([g_vec, g_b1, g_tab], axis=1)

    g_small = owned_by(me)
    if fast:
        per_z = CHIP_X
        ring = CHIP_Z * CHIP_X
        for k in range(1, CHIP_Z):
            device = (me // ring) * ring + (me + k * per_z) % ring
            g_small = g_small + send(owned_by(device), Z_SHIFT[k])
    g = g_small[:, : B_ONE * own].reshape(LAYERS, B_ONE, own)
    g = [g[:, i] for i in range(B_ONE)]
    g_b1 = g_small[:, B_ONE * own : (B_ONE + ratio) * own]
    g_table = g_small[:, (B_ONE + ratio) * own :].reshape(LAYERS, heads, entries)

    def both(pick):
        return jnp.stack([pick(*r) for r in reduced])

    def thirds(low, high):
        half = width // 2
        cols = [v[:, i * half : (i + 1) * half] for i in range(3) for v in (low, high)]
        return jnp.concatenate(cols, axis=1)

    def join(low, high, first, last):
        return jnp.concatenate([low[:, first:last], high[:, first:last]], axis=1)

    half = hidden // 2
    g_qkv = both(lambda a, b: thirds(*b))
    g_one = both(lambda a, b: join(*a, 0, half))
    g_two = both(lambda a, b: join(*a, half, hidden).reshape(ratio * own, width))
    g_proj = both(lambda a, b: join(*a, hidden, hidden + width // 2))
    return (encoded, cut_rows(grad), g[N1_GAIN], g[N1_SHIFT], g_qkv, g[Q_BIAS], g[V_BIAS], g_proj,
            g[B_PROJ], g[G_ATTN], g[N2_GAIN], g[N2_SHIFT], g_one, g_b1, g_two, g[B_TWO], g[G_MLP],
            g_table)


def solution(mesh):
    shards = math.prod(mesh.shape[a] for a in AXES)
    fast = mesh.shape["dp"] == CHIP_Y * CORES and mesh.shape["fsdp"] == CHIP_Z * CHIP_X
    row = P(AXES, None)
    vec = P(None, AXES)
    mat = P(None, AXES, None)
    tab = P(None, None, AXES)
    return jax.shard_map(
        functools.partial(per_device, shards, fast),
        mesh=mesh,
        in_specs=(row, row, row, vec, vec, mat, vec, vec, mat, vec, vec, vec, vec, mat, vec, mat,
                  vec, vec, tab),
        out_specs=(row, row, vec, vec, mat, vec, vec, mat, vec, vec, vec, vec, mat, vec, mat,
                   vec, vec, tab),
        check_vma=False,
    )
```

time: 838 us -> 566 us (0.68)
  waiting for transfers between devices: 438 us -> 170 us
  local copies, waits for them, and re-layouts: 146 us -> 21.4 us
  starting transfers between devices: 0.16 us -> 101 us
  Pallas kernels: 140 us -> 205 us
  matrix products: 56.6 us -> 0 us
  other arithmetic: 33.9 us -> 45.4 us
    unnamed x6 -> x1, waiting for transfers between devices: 235 us -> 0.02 us
    all_gather x2 -> x1, waiting for transfers between devices: 203 us -> 0.01 us  [fetch_packed(): return lax.all_gather(block, AXES, axis=0, tiled=True)]
    ppermute x0 -> x66, waiting for transfers between devices: none -> 169 us  [send(): return lax.ppermute(v, AXES, pairs)]
    ppermute x0 -> x66, starting transfers between devices: none -> 101 us  [send(): return lax.ppermute(v, AXES, pairs)]
    pallas_call x8 -> x14, Pallas kernels: 99.9 us -> 165 us  [the longest x2 40.9 us: mlp_backward(): pl.pallas_call(mlp_grad_kernel, grid=(hidden // TILE,), out_shape=(jax.Sh...]
    dot_general x16 -> x0, matrix products: 56.6 us -> none  [the longest x12 47.7 us: dot(): return lax.dot_general(a, b, (dims, ((), ())), preferred_element_type=F32)]
    reshape x18 -> x16, local copies, waits for them, and re-layouts: 48.4 us -> 1.47 us  [the longest x3 0.59 us: no_sooner(): zero = zero + jnp.minimum(jnp.abs(v.reshape(-1)[0]), 0)]
    unnamed x82 -> x112, local copies, waits for them, and re-layouts: 34.2 us -> 9.26 us
  transfers between devices with their start and end apart: 4 -> 67, of which waited for: 4 -> 25; matrix products, arithmetic and copies ran while one was open for 7% -> 9% of each run, Pallas kernels for 5% -> 25%
where the time goes in v2:
time: 566 us; the launch traced here: 560 us
  Pallas kernels  205 us (36%)
  waiting for transfers between devices  170 us (30%)
  starting transfers between devices  101 us (18%)
  other arithmetic  45.4 us (8%)
  local copies, waits for them, and re-layouts  21.4 us (4%)
  between operations  17.9 us (3%)
    ppermute x66, waiting for transfers between devices, send(): return lax.ppermute(v, AXES, pairs)  169 us
    ppermute x66, starting transfers between devices, send(): return lax.ppermute(v, AXES, pairs)  101 us
    pallas_call x2, Pallas kernels, mlp_backward(): pl.pallas_call(mlp_grad_kernel, grid=(hidden // TILE,), out_shape=(jax.Sh...  40.9 us
    pallas_call x2, Pallas kernels, mlp_forward(): pl.pallas_call(mlp_kernel, grid=(hidden // TILE,), out_shape=(full, full,...  31.1 us
    pallas_call x2, Pallas kernels, attention_backward(): pl.pallas_call(functools.partial(attention_grad_kernel, width), grid=(ima...  23.5 us
    pallas_call x2, Pallas kernels, qkv_backward(): pl.pallas_call(qkv_grad_kernel, grid=(3,), out_shape=(jax.ShapeDtypeStruc...  22.4 us
    pallas_call x2, Pallas kernels, reduce_bias(): pl.pallas_call(bias_grad_kernel, grid=(heads,), out_shape=jax.ShapeDtypeS...  22.4 us
    pallas_call x1, Pallas kernels, build_bias(): pl.pallas_call(functools.partial(bias_kernel, heads), grid=(layers * head...  17.8 us
  transfers between devices with their start and end apart: 67, of which 25 were waited for; matrix products, arithmetic and copies ran while one was open for 9% of the time, Pallas kernels for 25%

profile of v2, /device:TPU:0, one launch (start us, length us, event | category | flops | bytes accessed | tf_op | source)
XLA Modules:
  0.0 560.1 jit_solution(4010290890752337939)
XLA Ops:
  16.2 5.0 collective-permute-start.9
  23.1 11.6 %collective-permute-done.7 = bf16[2,24,1536]{2,1,0:T(8,128)(2,1)S(1)} collective-permute-done((bf16[2,24,1536]{2,1,0:T(8,128)(2,1)S(1)}, bf16[2,24,1536]{2,1,0:T(8,128)(2,1)S(1)}, u32[]{:S(2)}, u32[]{:S(2)}) %collective-permute-start.7) | collective-permute-done | bytes 147488 | tf_op jit(solution)/shard_map/ppermute | solution.py:693
  36.0 4.8 collective-permute-done.8
  43.9 16.8 %collective-permute-start.19 = (bf16[2,24,3072]{2,1,0:T(8,128)(2,1)S(1)}, bf16[2,24,3072]{2,1,0:T(8,128)(2,1)S(1)}, u32[]{:S(2)}, u32[]{:S(2)}) collective-permute-start(bf16[2,24,3072]{2,1,0:T(8,128)(2,1)S(1)} %get-tuple-element.183), channel_id=1, source_target_pairs={{0,4},{1,5},{2,6},{3,7},{4,0},{5,1},{6,2},{7,3},{8,12},{9,13},{10,... | collective-permute-start | bytes 884744 | tf_op jit(solution)/shard_map/ppermute | solution.py:693
  65.7 27.7 %collective-permute-done.19 = bf16[2,24,3072]{2,1,0:T(8,128)(2,1)S(1)} collective-permute-done((bf16[2,24,3072]{2,1,0:T(8,128)(2,1)S(1)}, bf16[2,24,3072]{2,1,0:T(8,128)(2,1)S(1)}, u32[]{:S(2)}, u32[]{:S(2)}) %collective-permute-start.19) | collective-permute-done | bytes 294944 | tf_op jit(solution)/shard_map/ppermute | solution.py:693
  96.6 4.4 collective-permute-done.2
  104.3 5.5 collective-permute-done.5
  109.8 18.7 %collective-permute-start.4 = (bf16[52,768]{1,0:T(8,128)(2,1)S(1)}, bf16[52,768]{1,0:T(8,128)(2,1)S(1)}, u32[]{:S(2)}, u32[]{:S(2)}) collective-permute-start(bf16[52,768]{1,0:T(8,128)(2,1)S(1)} %add.649), channel_id=1, source_target_pairs={{0,4},{1,5},{2,6},{3,7},{4,0},{5,1},{6,2},{7,3},{8,12},{9,13},{10,... | collective-permute-start | bytes 239624 | tf_op jit(solution)/shard_map/ppermute | solution.py:693
  128.5 2.6 collective-permute-start.12
  132.2 3.0 collective-permute-done.4
  138.2 7.2 %collective-permute-done.3 = bf16[52,768]{1,0:T(8,128)(2,1)S(1)} collective-permute-done((bf16[52,768]{1,0:T(8,128)(2,1)S(1)}, bf16[52,768]{1,0:T(8,128)(2,1)S(1)}, u32[]{:S(2)}, u32[]{:S(2)}) %collective-permute-start.3) | collective-permute-done | bytes 79904 | tf_op jit(solution)/shard_map/ppermute | solution.py:693
  146.2 3.3 collective-permute-start.22
  150.6 17.8 %bias_expand.1.refs_8_.bias_ref = f32[24,208,256]{2,1,0:T(8,128)} custom-call(f32[2,32,768]{2,1,0:T(8,128)} %pad_convert_fusion.small_ref, bf16[208,224]{1,0:T(8,128)(2,1)} %constant.359.clone.rows_ref, bf16[384,256]{1,0:T(8,128)(2,1)} %constant.360.clone.lanes_ref), custom_call_target="tpu_custom_call" | custom-call | flops 19800000512 | bytes 63000000 | tf_op jit(solution)/shard_map/bias_expand/pallas_call | solution.py:92
  169.2 5.3 assemble.2
  176.4 6.3 %qkv.2 = (bf16[416,2304]{1,0:T(8,128)(2,1)}, bf16[416,768]{1,0:T(8,128)(2,1)}) custom-call(f32[416,768]{1,0:T(8,128)} %bitcast_convert_fusion.4.x_ref, f32[2,32,768]{2,1,0:T(8,128)} %pad_convert_fusion.small_ref, bf16[768,2304]{1,0:T(8,128)(2,1)} %bitcast.416), custom_call_target="tpu_custom_call" | custom-call | flops 6600000000 | bytes 21000000 | tf_op jit(solution)/shard_map/qkv/pallas_call | solution.py:337
  182.7 8.3 %attention.2 = (bf16[2,208,768]{2,1,0:T(8,128)(2,1)}, f32[2,16,256]{2,1,0:T(8,128)}) custom-call(bf16[2,208,2304]{2,1,0:T(8,128)(2,1)} %bitcast.418, f32[24,208,256]{2,1,0:T(8,128)} %bias_expand.1.refs_8_.bias_ref), custom_call_target="tpu_custom_call" | custom-call | flops 8800000000 | bytes 28000000 | tf_op jit(solution)/shard_map/attention/pallas_call | solution.py:190
  192.8 8.3 %assemble.3 = (bf16[32,1,24,3072]{3,2,1,0:T(8,128)(2,1)}, bf16[32,4,24,768]{3,2,1,0:T(8,128)(2,1)}) custom-call(s32[4]{0:T(128)} %pad_add_fusion.pos_ref, bf16[4,2,24,3072]{3,2,1,0:T(8,128)(2,1)} %copy-done.4, bf16[4,2,24,3072]{3,2,1,0:T(8,128)(2,1)} %collective-permute-done.21.refs_1_, bf16[4,2,24,3072]{3,2,1,0:T(8,128)(2,1)} %copy-done.21, ...), custom_call_target="tpu_custom_call" | custom-call | flops 7699999744 | bytes 24500000 | tf_op jit(solution)/shard_map/assemble/pallas_call | solution.py:771
  201.1 15.6 %mlp.2 = (f32[416,768]{1,0:T(8,128)}, f32[416,768]{1,0:T(8,128)}, f32[416,768]{1,0:T(8,128)}, f32[416,768]{1,0:T(8,128)}, bf16[416,768]{1,0:T(8,128)(2,1)}, /*in...) custom-call(f32[416,768]{1,0:T(8,128)} %bitcast_convert_fusion.4.x_ref, bf16[416,768]{1,0:T(8,128)(2,1)} %bitcast.427, ...), custom_call_target="tpu_custom_call" | custom-call | flops 16499999744 | bytes 52500000 | tf_op jit(solution)/shard_map/mlp/pallas_call | solution.py:474
  216.7 5.8 %qkv.3 = (bf16[416,2304]{1,0:T(8,128)(2,1)}, bf16[416,768]{1,0:T(8,128)(2,1)}) custom-call(f32[416,768]{1,0:T(8,128)} %get-tuple-element.72.x_ref, f32[2,32,768]{2,1,0:T(8,128)} %pad_convert_fusion.small_ref, bf16[768,9216]{1,0:T(8,128)(2,1)} %all-gather.2.cloned.1.call-done.w_ref.wp_ref.w1_ref), custom_call_target="tpu_custom_call" | custom-call | flops 6600000000 | bytes 21000000 | tf_op jit(solution)/shard_map/qkv/pallas_call | solution.py:337
  222.5 8.3 %attention.3 = (bf16[2,208,768]{2,1,0:T(8,128)(2,1)}, f32[2,16,256]{2,1,0:T(8,128)}) custom-call(bf16[2,208,2304]{2,1,0:T(8,128)(2,1)} %bitcast.420, f32[24,208,256]{2,1,0:T(8,128)} %bias_expand.1.refs_8_.bias_ref), custom_call_target="tpu_custom_call" | custom-call | flops 8800000000 | bytes 28000000 | tf_op jit(solution)/shard_map/attention/pallas_call | solution.py:190
  230.8 4.6 unpack.1
  235.3 15.6 %mlp.3 = (f32[416,768]{1,0:T(8,128)}, f32[416,768]{1,0:T(8,128)}, f32[416,768]{1,0:T(8,128)}, f32[416,768]{1,0:T(8,128)}, bf16[416,768]{1,0:T(8,128)(2,1)}, /*in...) custom-call(f32[416,768]{1,0:T(8,128)} %get-tuple-element.72.x_ref, bf16[416,768]{1,0:T(8,128)(2,1)} %bitcast.431, ...), custom_call_target="tpu_custom_call" | custom-call | flops 16499999744 | bytes 52500000 | tf_op jit(solution)/shard_map/mlp/pallas_call | solution.py:474
  250.9 20.6 %mlp_grad.2 = (bf16[768,3456]{1,0:T(8,128)(2,1)}, bf16[768,3456]{1,0:T(8,128)(2,1)}, f32[416,768]{1,0:T(8,128)}, bf16[416,768]{1,0:T(8,128)(2,1)}, f32[16,768]{1,0:T(8,128)}) custom-call(s32[1]{0:T(128)} %bitcast.13.core_ref, f32[416,768]{1,0:T(8,128)} %convert_select_fusion.g_ref, f32[416,768]{1,0:T(8,128)} %get-tuple-element.78.mid_ref, ...), custom_call_target="tpu_custom_call" | custom-call | flops 22000001024 | bytes 70000000 | tf_op jit(solution)/shard_map/mlp_grad/pallas_call | solution.py:634
  273.0 11.6 %attention_grad.2 = (bf16[2,208,2304]{2,1,0:T(8,128)(2,1)}, f32[12,208,256]{2,1,0:T(8,128)}) custom-call(bf16[2,208,2304]{2,1,0:T(8,128)(2,1)} %bitcast.421, f32[24,208,256]{2,1,0:T(8,128)} %bias_expand.1.refs_8_.bias_ref, f32[2,16,256]{2,1,0:T(8,128)} %get-tuple-element.77.lse_ref, bf16[2,208,768]{2,1,0:T(8,128)(2,1)} %bitcast.429), custom_call_target="tpu_custom_call" | custom-call | flops 13200000000 | bytes 42000000 | tf_op jit(solution)/shard_map/attention_grad/pallas_call | solution.py:256
  284.6 11.4 %bias_reduce.3 = f32[12,1,768]{2,1,0:T(1,128)} custom-call(f32[12,208,256]{2,1,0:T(8,128)} %get-tuple-element.110.g_ref, bf16[224,208]{1,0:T(8,128)(2,1)} %constant.361.clone.rows_ref, bf16[256,384]{1,0:T(8,128)(2,1)} %constant.362.clone.lanes_ref), custom_call_target="tpu_custom_call" | custom-call | flops 12099999744 | bytes 38500000 | tf_op jit(solution)/shard_map/bias_reduce/pallas_call | solution.py:139
  296.0 3.9 fusion.5
  301.9 11.2 %qkv_grad.2 = (bf16[768,1152]{1,0:T(8,128)(2,1)}, bf16[768,1152]{1,0:T(8,128)(2,1)}, f32[416,768]{1,0:T(8,128)}, f32[8,768]{1,0:T(8,128)}) custom-call(s32[1]{0:T(128)} %bitcast.13.core_ref, bf16[416,2304]{1,0:T(8,128)(2,1)} %bitcast.423, bf16[416,768]{1,0:T(8,128)(2,1)} %get-tuple-element.86.h_ref, f32[416,768]{1,0:T(8,128)} %get-tuple-element.72.x_ref, ...), custom_call_target="tpu_custom_call" | custom-call | flops 12099999744 | bytes 38500000 | tf_op jit(solution)/shard_map/qkv_grad/pallas_call | solution.py:405
  313.2 20.3 %mlp_grad.3 = (bf16[768,3456]{1,0:T(8,128)(2,1)}, bf16[768,3456]{1,0:T(8,128)(2,1)}, f32[416,768]{1,0:T(8,128)}, bf16[416,768]{1,0:T(8,128)(2,1)}, f32[16,768]{1,0:T(8,128)}) custom-call(s32[1]{0:T(128)} %bitcast.13.core_ref, f32[416,768]{1,0:T(8,128)} %get-tuple-element.89.g_ref, f32[416,768]{1,0:T(8,128)} %get-tuple-element.90.mid_ref, ...), custom_call_target="tpu_custom_call" | custom-call | flops 22000001024 | bytes 70000000 | tf_op jit(solution)/shard_map/mlp_grad/pallas_call | solution.py:634
  334.0 3.4 fusion.3
  341.8 12.0 %attention_grad.3 = (bf16[2,208,2304]{2,1,0:T(8,128)(2,1)}, f32[12,208,256]{2,1,0:T(8,128)}) custom-call(bf16[2,208,2304]{2,1,0:T(8,128)(2,1)} %bitcast.419, f32[24,208,256]{2,1,0:T(8,128)} %bias_expand.1.refs_8_.bias_ref, f32[2,16,256]{2,1,0:T(8,128)} %get-tuple-element.76.lse_ref, bf16[2,208,768]{2,1,0:T(8,128)(2,1)} %bitcast.430, ...), custom_call_target="tpu_custom_call" | custom-call | flops 13200000000 | bytes 42000000 | tf_op jit(solution)/shard_map/attention_grad/pallas_call | solution.py:256
  357.9 11.0 %bias_reduce.2 = f32[12,1,768]{2,1,0:T(1,128)} custom-call(f32[12,208,256]{2,1,0:T(8,128)} %get-tuple-element.107.g_ref, bf16[224,208]{1,0:T(8,128)(2,1)} %constant.361.clone.rows_ref, bf16[256,384]{1,0:T(8,128)(2,1)} %constant.362.clone.lanes_ref), custom_call_target="tpu_custom_call" | custom-call | flops 12099999744 | bytes 38500000 | tf_op jit(solution)/shard_map/bias_reduce/pallas_call | solution.py:139
  371.3 4.5 collective-permute-start.53
  376.5 2.7 fusion
  379.3 5.1 collective-permute-done.52
  389.6 5.6 %collective-permute-done.64 = bf16[2,24,3456]{2,1,0:T(8,128)(2,1)S(1)} collective-permute-done((bf16[2,24,3456]{2,1,0:T(8,128)(2,1)S(1)}, bf16[2,24,3456]{2,1,0:T(8,128)(2,1)S(1)}, u32[]{:S(2)}, u32[]{:S(2)}) %collective-permute-start.64) | collective-permute-done | bytes 331808 | tf_op jit(solution)/shard_map/ppermute | solution.py:693
  395.2 22.1 %collective-permute-done.63 = bf16[2,24,3456]{2,1,0:T(8,128)(2,1)S(1)} collective-permute-done((bf16[2,24,3456]{2,1,0:T(8,128)(2,1)S(1)}, bf16[2,24,3456]{2,1,0:T(8,128)(2,1)S(1)}, u32[]{:S(2)}, u32[]{:S(2)}) %collective-permute-start.63) | collective-permute-done | bytes 331808 | tf_op jit(solution)/shard_map/ppermute | solution.py:693
  419.3 11.2 %qkv_grad.3 = (bf16[768,1152]{1,0:T(8,128)(2,1)}, bf16[768,1152]{1,0:T(8,128)(2,1)}, f32[416,768]{1,0:T(8,128)}, f32[8,768]{1,0:T(8,128)}) custom-call(s32[1]{0:T(128)} %bitcast.13.core_ref, bf16[416,2304]{1,0:T(8,128)(2,1)} %bitcast.422, bf16[416,768]{1,0:T(8,128)(2,1)} %get-tuple-element.100.h_ref, f32[416,768]{1,0:T(8,128)} %bitcast_convert_fusion.4.x_ref, ...), custom_call_target="tpu_custom_call" | custom-call | flops 12099999744 | bytes 38500000 | tf_op jit(solution)/shard_map/qkv_grad/pallas_call | solution.py:405
  435.0 3.1 fusion.7
  441.8 3.1 fusion.6
  446.8 13.1 %collective-permute-done.38 = f32[52,768]{1,0:T(8,128)} collective-permute-done((f32[52,768]{1,0:T(8,128)}, f32[52,768]{1,0:T(8,128)}, u32[]{:S(2)}, u32[]{:S(2)}) %collective-permute-start.38) | collective-permute-done | bytes 159776 | tf_op jit(solution)/shard_map/ppermute | solution.py:693
  469.2 2.6 fusion.1
  473.7 6.9 %collective-permute-done.44 = bf16[2,4,24,1152]{3,2,1,0:T(8,128)(2,1)S(1)} collective-permute-done((bf16[2,4,24,1152]{3,2,1,0:T(8,128)(2,1)S(1)}, bf16[2,4,24,1152]{3,2,1,0:T(8,128)(2,1)S(1)}, u32[]{:S(2)}, u32[]{:S(2)}) %collective-permute-start.44) | collective-permute-done | bytes 442400 | tf_op jit(solution)/shard_map/ppermute | solution.py:693
  488.2 7.9 %collective-permute-done.43 = bf16[2,4,24,1152]{3,2,1,0:T(8,128)(2,1)} collective-permute-done((bf16[2,4,24,1152]{3,2,1,0:T(8,128)(2,1)}, bf16[2,4,24,1152]{3,2,1,0:T(8,128)(2,1)}, u32[]{:S(2)}, u32[]{:S(2)}) %collective-permute-start.43) | collective-permute-done | bytes 442400 | tf_op jit(solution)/shard_map/ppermute | solution.py:693
  496.1 7.7 %collective-permute-done.45 = bf16[2,4,24,1152]{3,2,1,0:T(8,128)(2,1)} collective-permute-done((bf16[2,4,24,1152]{3,2,1,0:T(8,128)(2,1)}, bf16[2,4,24,1152]{3,2,1,0:T(8,128)(2,1)}, u32[]{:S(2)}, u32[]{:S(2)}) %collective-permute-start.45) | collective-permute-done | bytes 442400 | tf_op jit(solution)/shard_map/ppermute | solution.py:693
  509.6 3.1 fusion.2
  512.8 4.0 collective-permute-done.47
  520.8 7.5 %collective-permute-done.60 = bf16[2,24,3456]{2,1,0:T(8,128)(2,1)S(1)} collective-permute-done((bf16[2,24,3456]{2,1,0:T(8,128)(2,1)S(1)}, bf16[2,24,3456]{2,1,0:T(8,128)(2,1)S(1)}, u32[]{:S(2)}, u32[]{:S(2)}) %collective-permute-start.60) | collective-permute-done | bytes 331808 | tf_op jit(solution)/shard_map/ppermute | solution.py:693
  528.3 20.2 %collective-permute-done.59 = bf16[2,24,3456]{2,1,0:T(8,128)(2,1)S(1)} collective-permute-done((bf16[2,24,3456]{2,1,0:T(8,128)(2,1)S(1)}, bf16[2,24,3456]{2,1,0:T(8,128)(2,1)S(1)}, u32[]{:S(2)}, u32[]{:S(2)}) %collective-permute-start.59) | collective-permute-done | bytes 331808 | tf_op jit(solution)/shard_map/ppermute | solution.py:693
  (352 shorter events, 100.1 us)
Async XLA Ops:
  7.3 209.3 %all-gather.2.cloned.1.call-start = ((), (), s32[]{:S(2)}) async-start(), calls=%async_computation | async-start | bytes 14598144 | tf_op jit(solution)/shard_map/all_gather | solution.py:935
  15.5 28.1 %collective-permute-start.17 = (bf16[24,3072]{1,0:T(8,128)(2,1)S(1)}, bf16[24,3072]{1,0:T(8,128)(2,1)S(1)}, u32[]{:S(2)}, u32[]{:S(2)}) collective-permute-start(bf16[24,3072]{1,0:T(8,128)(2,1)S(1)} %constant_dynamic-update-slice_fusion.15), channel_id=1, source_target_pairs={{0,8},{1,9},{2,10},{3,11},{4,12},{5,13},{6,14},{7,15},{8,0},{9,1},... | collective-permute-start | bytes 442376 | tf_op jit(solution)/shard_map/ppermute | solution.py:693
  16.2 26.0 %collective-permute-start.9 = (bf16[2,24,1536]{2,1,0:T(8,128)(2,1)S(1)}, bf16[2,24,1536]{2,1,0:T(8,128)(2,1)S(1)}, u32[]{:S(2)}, u32[]{:S(2)}) collective-permute-start(bf16[2,24,1536]{2,1,0:T(8,128)(2,1)S(1)} %get-tuple-element.193), channel_id=1, source_target_pairs={{0,6},{1,7},{2,0},{3,1},{4,2},{5,3},{6,4},{7,5},{8,14},{9,15},{10,... | collective-permute-start | bytes 442376 | tf_op jit(solution)/shard_map/ppermute | solution.py:693
  21.2 19.6 %collective-permute-start.8 = (bf16[2,24,1536]{2,1,0:T(8,128)(2,1)S(1)}, bf16[2,24,1536]{2,1,0:T(8,128)(2,1)S(1)}, u32[]{:S(2)}, u32[]{:S(2)}) collective-permute-start(bf16[2,24,1536]{2,1,0:T(8,128)(2,1)S(1)} %get-tuple-element.193), channel_id=1, source_target_pairs={{0,4},{1,5},{2,6},{3,7},{4,0},{5,1},{6,2},{7,3},{8,12},{9,13},{10,... | collective-permute-start | bytes 442376 | tf_op jit(solution)/shard_map/ppermute | solution.py:693
  21.2 13.4 %collective-permute-start.7 = (bf16[2,24,1536]{2,1,0:T(8,128)(2,1)S(1)}, bf16[2,24,1536]{2,1,0:T(8,128)(2,1)S(1)}, u32[]{:S(2)}, u32[]{:S(2)}) collective-permute-start(bf16[2,24,1536]{2,1,0:T(8,128)(2,1)S(1)} %get-tuple-element.193), channel_id=1, source_target_pairs={{0,2},{1,3},{2,4},{3,5},{4,6},{5,7},{6,0},{7,1},{8,10},{9,11},{10,... | collective-permute-start | bytes 442376 | tf_op jit(solution)/shard_map/ppermute | solution.py:693
  23.0 39.7 %collective-permute-start = (bf16[52,768]{1,0:T(8,128)(2,1)S(1)}, bf16[52,768]{1,0:T(8,128)(2,1)S(1)}, u32[]{:S(2)}, u32[]{:S(2)}) collective-permute-start(bf16[52,768]{1,0:T(8,128)(2,1)S(1)} %reshape.315), channel_id=1, source_target_pairs={{0,8},{1,9},{2,10},{3,11},{4,12},{5,13},{6,14},{7,15},{8,0},{9,1},... | collective-permute-start | bytes 239624 | tf_op jit(solution)/shard_map/ppermute | solution.py:693
  43.7 22.0 %collective-permute-start.20 = (bf16[2,24,3072]{2,1,0:T(8,128)(2,1)S(1)}, bf16[2,24,3072]{2,1,0:T(8,128)(2,1)S(1)}, u32[]{:S(2)}, u32[]{:S(2)}) collective-permute-start(bf16[2,24,3072]{2,1,0:T(8,128)(2,1)S(1)} %get-tuple-element.183), channel_id=1, source_target_pairs={{0,6},{1,7},{2,0},{3,1},{4,2},{5,3},{6,4},{7,5},{8,14},{9,15},{10,... | collective-permute-start | bytes 884744 | tf_op jit(solution)/shard_map/ppermute | solution.py:693
  43.9 49.5 %collective-permute-start.19 = (bf16[2,24,3072]{2,1,0:T(8,128)(2,1)S(1)}, bf16[2,24,3072]{2,1,0:T(8,128)(2,1)S(1)}, u32[]{:S(2)}, u32[]{:S(2)}) collective-permute-start(bf16[2,24,3072]{2,1,0:T(8,128)(2,1)S(1)} %get-tuple-element.183), channel_id=1, source_target_pairs={{0,4},{1,5},{2,6},{3,7},{4,0},{5,1},{6,2},{7,3},{8,12},{9,13},{10,... | collective-permute-start | bytes 884744 | tf_op jit(solution)/shard_map/ppermute | solution.py:693
  60.7 32.6 %collective-permute-start.18 = (bf16[2,24,3072]{2,1,0:T(8,128)(2,1)S(1)}, bf16[2,24,3072]{2,1,0:T(8,128)(2,1)S(1)}, u32[]{:S(2)}, u32[]{:S(2)}) collective-permute-start(bf16[2,24,3072]{2,1,0:T(8,128)(2,1)S(1)} %get-tuple-element.183), channel_id=1, source_target_pairs={{0,2},{1,3},{2,4},{3,5},{4,6},{5,7},{6,0},{7,1},{8,10},{9,11},{10,... | collective-permute-start | bytes 884744 | tf_op jit(solution)/shard_map/ppermute | solution.py:693
  62.7 32.1 %collective-permute-start.1 = (bf16[52,768]{1,0:T(8,128)(2,1)S(1)}, bf16[52,768]{1,0:T(8,128)(2,1)S(1)}, u32[]{:S(2)}, u32[]{:S(2)}) collective-permute-start(bf16[52,768]{1,0:T(8,128)(2,1)S(1)} %add.647), channel_id=1, source_target_pairs={{0,1},{1,0},{2,3},{3,2},{4,5},{5,4},{6,7},{7,6},{8,9},{9,8},{10,11... | collective-permute-start | bytes 239624 | tf_op jit(solution)/shard_map/ppermute | solution.py:693
  65.4 63.1 %collective-permute-start.10 = (bf16[4,2,24,1536]{3,2,1,0:T(8,128)(2,1)}, bf16[4,2,24,1536]{3,2,1,0:T(8,128)(2,1)}, u32[]{:S(2)}, u32[]{:S(2)}) collective-permute-start(bf16[4,2,24,1536]{3,2,1,0:T(8,128)(2,1)} %pad_maximum_fusion.1.refs_0_), channel_id=1, source_target_pairs={{0,1},{1,0},{2,3},{3,2},{4,5},{5,4},{6,7},{7,6},{8,24},{9,25},{10,... | collective-permute-start | bytes 1769480 | tf_op jit(solution)/shard_map/ppermute | solution.py:693
  93.5 56.6 %collective-permute-start.21 = (bf16[4,2,24,3072]{3,2,1,0:T(8,128)(2,1)S(1)}, bf16[4,2,24,3072]{3,2,1,0:T(8,128)(2,1)}, u32[]{:S(2)}, u32[]{:S(2)}) collective-permute-start(bf16[4,2,24,3072]{3,2,1,0:T(8,128)(2,1)S(1)} %pad_maximum_fusion.refs_0_), channel_id=1, source_target_pairs={{0,1},{1,0},{2,3},{3,2},{4,5},{5,4},{6,7},{7,6},{8,24},{9,25},{10,... | collective-permute-start | bytes 3538952 | tf_op jit(solution)/shard_map/ppermute | solution.py:693
  102.6 47.0 %collective-permute-start.11 = (bf16[4,2,24,1536]{3,2,1,0:T(8,128)(2,1)}, bf16[4,2,24,1536]{3,2,1,0:T(8,128)(2,1)S(1)}, u32[]{:S(2)}, u32[]{:S(2)}) collective-permute-start(bf16[4,2,24,1536]{3,2,1,0:T(8,128)(2,1)} %pad_maximum_fusion.1.refs_0_), channel_id=1, source_target_pairs={{0,16},{1,17},{2,18},{3,19},{4,20},{5,21},{6,22},{7,23},{8,9},{9,8... | collective-permute-start | bytes 1769480 | tf_op jit(solution)/shard_map/ppermute | solution.py:693
  104.3 45.3 %collective-permute-start.13 = (bf16[4,2,24,1536]{3,2,1,0:T(8,128)(2,1)}, bf16[4,2,24,1536]{3,2,1,0:T(8,128)(2,1)}, u32[]{:S(2)}, u32[]{:S(2)}) collective-permute-start(bf16[4,2,24,1536]{3,2,1,0:T(8,128)(2,1)} %pad_maximum_fusion.1.refs_0_), channel_id=1, source_target_pairs={{0,8},{1,9},{2,10},{3,11},{4,12},{5,13},{6,14},{7,15},{8,0},{9,1},... | collective-permute-start | bytes 1769480 | tf_op jit(solution)/shard_map/ppermute | solution.py:693
  109.8 25.4 %collective-permute-start.4 = (bf16[52,768]{1,0:T(8,128)(2,1)S(1)}, bf16[52,768]{1,0:T(8,128)(2,1)S(1)}, u32[]{:S(2)}, u32[]{:S(2)}) collective-permute-start(bf16[52,768]{1,0:T(8,128)(2,1)S(1)} %add.649), channel_id=1, source_target_pairs={{0,4},{1,5},{2,6},{3,7},{4,0},{5,1},{6,2},{7,3},{8,12},{9,13},{10,... | collective-permute-start | bytes 239624 | tf_op jit(solution)/shard_map/ppermute | solution.py:693
  128.5 21.6 %collective-permute-start.12 = (bf16[4,2,24,1536]{3,2,1,0:T(8,128)(2,1)}, bf16[4,2,24,1536]{3,2,1,0:T(8,128)(2,1)}, u32[]{:S(2)}, u32[]{:S(2)}) collective-permute-start(bf16[4,2,24,1536]{3,2,1,0:T(8,128)(2,1)} %collective-permute-done.10.refs_1_), channel_id=1, source_target_pairs={{0,16},{1,17},{2,18},{3,19},{4,20},{5,21},{6,22},{7,23},{8,9},{9,8... | collective-permute-start | bytes 1769480 | tf_op jit(solution)/shard_map/ppermute | solution.py:693
  146.2 22.9 %collective-permute-start.22 = (bf16[4,2,24,3072]{3,2,1,0:T(8,128)(2,1)S(1)}, bf16[4,2,24,3072]{3,2,1,0:T(8,128)(2,1)S(1)}, u32[]{:S(2)}, u32[]{:S(2)}) collective-permute-start(bf16[4,2,24,3072]{3,2,1,0:T(8,128)(2,1)S(1)} %pad_maximum_fusion.refs_0_), channel_id=1, source_target_pairs={{0,16},{1,17},{2,18},{3,19},{4,20},{5,21},{6,22},{7,23},{8,9},{9,8... | collective-permute-start | bytes 3538952 | tf_op jit(solution)/shard_map/ppermute | solution.py:693
  149.5 18.9 %collective-permute-start.14 = (bf16[4,2,24,1536]{3,2,1,0:T(8,128)(2,1)}, bf16[4,2,24,1536]{3,2,1,0:T(8,128)(2,1)}, u32[]{:S(2)}, u32[]{:S(2)}) collective-permute-start(bf16[4,2,24,1536]{3,2,1,0:T(8,128)(2,1)} %collective-permute-done.10.refs_1_), channel_id=1, source_target_pairs={{0,8},{1,9},{2,10},{3,11},{4,12},{5,13},{6,14},{7,15},{8,0},{9,1},... | collective-permute-start | bytes 1769480 | tf_op jit(solution)/shard_map/ppermute | solution.py:693
  149.5 19.0 %collective-permute-start.15 = (bf16[4,2,24,1536]{3,2,1,0:T(8,128)(2,1)S(1)}, bf16[4,2,24,1536]{3,2,1,0:T(8,128)(2,1)}, u32[]{:S(2)}, u32[]{:S(2)}) collective-permute-start(bf16[4,2,24,1536]{3,2,1,0:T(8,128)(2,1)S(1)} %collective-permute-done.11.refs_2_), channel_id=1, source_target_pairs={{0,8},{1,9},{2,10},{3,11},{4,12},{5,13},{6,14},{7,15},{8,0},{9,1},... | collective-permute-start | bytes 1769480 | tf_op jit(solution)/shard_map/ppermute | solution.py:693
  150.0 19.1 %collective-permute-start.16 = (bf16[4,2,24,1536]{3,2,1,0:T(8,128)(2,1)}, bf16[4,2,24,1536]{3,2,1,0:T(8,128)(2,1)}, u32[]{:S(2)}, u32[]{:S(2)}) collective-permute-start(bf16[4,2,24,1536]{3,2,1,0:T(8,128)(2,1)} %collective-permute-done.12.refs_3_), channel_id=1, source_target_pairs={{0,8},{1,9},{2,10},{3,11},{4,12},{5,13},{6,14},{7,15},{8,0},{9,1},... | collective-permute-start | bytes 1769480 | tf_op jit(solution)/shard_map/ppermute | solution.py:693
  150.1 26.2 %collective-permute-start.23 = (bf16[4,2,24,3072]{3,2,1,0:T(8,128)(2,1)}, bf16[4,2,24,3072]{3,2,1,0:T(8,128)(2,1)S(1)}, u32[]{:S(2)}, u32[]{:S(2)}) collective-permute-start(bf16[4,2,24,3072]{3,2,1,0:T(8,128)(2,1)} %collective-permute-done.21.refs_1_), channel_id=1, source_target_pairs={{0,16},{1,17},{2,18},{3,19},{4,20},{5,21},{6,22},{7,23},{8,9},{9,8... | collective-permute-start | bytes 3538952 | tf_op jit(solution)/shard_map/ppermute | solution.py:693
  168.5 22.5 %collective-permute-start.24 = (bf16[4,2,24,3072]{3,2,1,0:T(8,128)(2,1)S(1)}, bf16[4,2,24,3072]{3,2,1,0:T(8,128)(2,1)S(1)}, u32[]{:S(2)}, u32[]{:S(2)}) collective-permute-start(bf16[4,2,24,3072]{3,2,1,0:T(8,128)(2,1)S(1)} %pad_maximum_fusion.refs_0_), channel_id=1, source_target_pairs={{0,8},{1,9},{2,10},{3,11},{4,12},{5,13},{6,14},{7,15},{8,0},{9,1},... | collective-permute-start | bytes 3538952 | tf_op jit(solution)/shard_map/ppermute | solution.py:693
  168.6 22.4 %collective-permute-start.25 = (bf16[4,2,24,3072]{3,2,1,0:T(8,128)(2,1)}, bf16[4,2,24,3072]{3,2,1,0:T(8,128)(2,1)S(1)}, u32[]{:S(2)}, u32[]{:S(2)}) collective-permute-start(bf16[4,2,24,3072]{3,2,1,0:T(8,128)(2,1)} %collective-permute-done.21.refs_1_), channel_id=1, source_target_pairs={{0,8},{1,9},{2,10},{3,11},{4,12},{5,13},{6,14},{7,15},{8,0},{9,1},... | collective-permute-start | bytes 3538952 | tf_op jit(solution)/shard_map/ppermute | solution.py:693
  169.1 21.9 %collective-permute-start.26 = (bf16[4,2,24,3072]{3,2,1,0:T(8,128)(2,1)S(1)}, bf16[4,2,24,3072]{3,2,1,0:T(8,128)(2,1)S(1)}, u32[]{:S(2)}, u32[]{:S(2)}) collective-permute-start(bf16[4,2,24,3072]{3,2,1,0:T(8,128)(2,1)S(1)} %collective-permute-done.22.refs_2_), channel_id=1, source_target_pairs={{0,8},{1,9},{2,10},{3,11},{4,12},{5,13},{6,14},{7,15},{8,0},{9,1},... | collective-permute-start | bytes 3538952 | tf_op jit(solution)/shard_map/ppermute | solution.py:693
  176.3 14.7 %collective-permute-start.27 = (bf16[4,2,24,3072]{3,2,1,0:T(8,128)(2,1)S(1)}, bf16[4,2,24,3072]{3,2,1,0:T(8,128)(2,1)}, u32[]{:S(2)}, u32[]{:S(2)}) collective-permute-start(bf16[4,2,24,3072]{3,2,1,0:T(8,128)(2,1)S(1)} %collective-permute-done.23.refs_3_), channel_id=1, source_target_pairs={{0,8},{1,9},{2,10},{3,11},{4,12},{5,13},{6,14},{7,15},{8,0},{9,1},... | collective-permute-start | bytes 3538952 | tf_op jit(solution)/shard_map/ppermute | solution.py:693
  271.5 24.5 %collective-permute-start.28 = (bf16[768,3456]{1,0:T(8,128)(2,1)}, bf16[768,3456]{1,0:T(8,128)(2,1)}, u32[]{:S(2)}, u32[]{:S(2)}) collective-permute-start(bf16[768,3456]{1,0:T(8,128)(2,1)} %get-tuple-element.88), channel_id=1, source_target_pairs={{0,8},{1,9},{2,10},{3,11},{4,12},{5,13},{6,14},{7,15},{8,0},{9,1},... | collective-permute-start | bytes 15925256 | tf_op jit(solution)/shard_map/ppermute | solution.py:693
  299.8 34.2 %collective-permute-start.29 = (bf16[2,4,24,3456]{3,2,1,0:T(8,128)(2,1)}, bf16[2,4,24,3456]{3,2,1,0:T(8,128)(2,1)}, u32[]{:S(2)}, u32[]{:S(2)}) collective-permute-start(bf16[2,4,24,3456]{3,2,1,0:T(8,128)(2,1)} %get-tuple-element.151), channel_id=1, source_target_pairs={{0,16},{1,17},{2,18},{3,19},{4,20},{5,21},{6,22},{7,23},{8,9},{9,8... | collective-permute-start | bytes 3981320 | tf_op jit(solution)/shard_map/ppermute | solution.py:693
  301.9 39.9 %collective-permute-start.30 = (bf16[2,4,24,3456]{3,2,1,0:T(8,128)(2,1)}, bf16[2,4,24,3456]{3,2,1,0:T(8,128)(2,1)}, u32[]{:S(2)}, u32[]{:S(2)}) collective-permute-start(bf16[2,4,24,3456]{3,2,1,0:T(8,128)(2,1)} %get-tuple-element.150), channel_id=1, source_target_pairs={{0,16},{1,17},{2,18},{3,19},{4,20},{5,21},{6,22},{7,23},{8,9},{9,8... | collective-permute-start | bytes 3981320 | tf_op jit(solution)/shard_map/ppermute | solution.py:693
  313.1 24.4 %collective-permute-start.31 = (bf16[768,1152]{1,0:T(8,128)(2,1)}, bf16[768,1152]{1,0:T(8,128)(2,1)}, u32[]{:S(2)}, u32[]{:S(2)}) collective-permute-start(bf16[768,1152]{1,0:T(8,128)(2,1)} %get-tuple-element.98), channel_id=1, source_target_pairs={{0,8},{1,9},{2,10},{3,11},{4,12},{5,13},{6,14},{7,15},{8,0},{9,1},... | collective-permute-start | bytes 5308424 | tf_op jit(solution)/shard_map/ppermute | solution.py:693
  333.5 85.8 %collective-permute-start.35 = (bf16[768,3456]{1,0:T(8,128)(2,1)}, bf16[768,3456]{1,0:T(8,128)(2,1)}, u32[]{:S(2)}, u32[]{:S(2)}) collective-permute-start(bf16[768,3456]{1,0:T(8,128)(2,1)} %get-tuple-element.103), channel_id=1, source_target_pairs={{0,8},{1,9},{2,10},{3,11},{4,12},{5,13},{6,14},{7,15},{8,0},{9,1},... | collective-permute-start | bytes 15925256 | tf_op jit(solution)/shard_map/ppermute | solution.py:693
  337.5 39.0 %collective-permute-start.32 = (bf16[2,4,24,3456]{3,2,1,0:T(8,128)(2,1)}, bf16[2,4,24,3456]{3,2,1,0:T(8,128)(2,1)}, u32[]{:S(2)}, u32[]{:S(2)}) collective-permute-start(bf16[2,4,24,3456]{3,2,1,0:T(8,128)(2,1)} %fusion.3), channel_id=1, source_target_pairs={{0,1},{1,0},{2,3},{3,2},{4,5},{5,4},{6,7},{7,6},{8,24},{9,25},{10,... | collective-permute-start | bytes 3981320 | tf_op jit(solution)/shard_map/ppermute | solution.py:693
  339.8 14.0 %collective-permute-start.33 = (bf16[2,4,24,1152]{3,2,1,0:T(8,128)(2,1)}, bf16[2,4,24,1152]{3,2,1,0:T(8,128)(2,1)S(1)}, u32[]{:S(2)}, u32[]{:S(2)}) collective-permute-start(bf16[2,4,24,1152]{3,2,1,0:T(8,128)(2,1)} %get-tuple-element.153), channel_id=1, source_target_pairs={{0,16},{1,17},{2,18},{3,19},{4,20},{5,21},{6,22},{7,23},{8,9},{9,8... | collective-permute-start | bytes 1327112 | tf_op jit(solution)/shard_map/ppermute | solution.py:693
  341.8 27.9 %collective-permute-start.34 = (bf16[2,4,24,1152]{3,2,1,0:T(8,128)(2,1)}, bf16[2,4,24,1152]{3,2,1,0:T(8,128)(2,1)S(1)}, u32[]{:S(2)}, u32[]{:S(2)}) collective-permute-start(bf16[2,4,24,1152]{3,2,1,0:T(8,128)(2,1)} %get-tuple-element.152), channel_id=1, source_target_pairs={{0,16},{1,17},{2,18},{3,19},{4,20},{5,21},{6,22},{7,23},{8,9},{9,8... | collective-permute-start | bytes 1327112 | tf_op jit(solution)/shard_map/ppermute | solution.py:693
  355.9 13.8 %collective-permute-start.50 = (bf16[2,4,24,1152]{3,2,1,0:T(8,128)(2,1)}, bf16[2,4,24,1152]{3,2,1,0:T(8,128)(2,1)}, u32[]{:S(2)}, u32[]{:S(2)}) collective-permute-start(bf16[2,4,24,1152]{3,2,1,0:T(8,128)(2,1)} %fusion.8), channel_id=1, source_target_pairs={{0,1},{1,0},{2,3},{3,2},{4,5},{5,4},{6,7},{7,6},{8,24},{9,25},{10,... | collective-permute-start | bytes 1327112 | tf_op jit(solution)/shard_map/ppermute | solution.py:693
  387.0 30.3 %collective-permute-start.63 = (bf16[2,24,3456]{2,1,0:T(8,128)(2,1)S(1)}, bf16[2,24,3456]{2,1,0:T(8,128)(2,1)S(1)}, u32[]{:S(2)}, u32[]{:S(2)}) collective-permute-start(bf16[2,24,3456]{2,1,0:T(8,128)(2,1)S(1)} %get-tuple-element.159), channel_id=1, source_target_pairs={{0,4},{1,5},{2,6},{3,7},{4,0},{5,1},{6,2},{7,3},{8,12},{9,13},{10,... | collective-permute-start | bytes 995336 | tf_op jit(solution)/shard_map/ppermute | solution.py:693
  387.5 29.7 %collective-permute-start.62 = (bf16[2,24,3456]{2,1,0:T(8,128)(2,1)S(1)}, bf16[2,24,3456]{2,1,0:T(8,128)(2,1)S(1)}, u32[]{:S(2)}, u32[]{:S(2)}) collective-permute-start(bf16[2,24,3456]{2,1,0:T(8,128)(2,1)S(1)} %get-tuple-element.157), channel_id=1, source_target_pairs={{0,2},{1,3},{2,4},{3,5},{4,6},{5,7},{6,0},{7,1},{8,10},{9,11},{10,... | collective-permute-start | bytes 995336 | tf_op jit(solution)/shard_map/ppermute | solution.py:693
  432.8 31.7 %collective-permute-start.42 = (bf16[768,1152]{1,0:T(8,128)(2,1)}, bf16[768,1152]{1,0:T(8,128)(2,1)}, u32[]{:S(2)}, u32[]{:S(2)}) collective-permute-start(bf16[768,1152]{1,0:T(8,128)(2,1)} %get-tuple-element.112), channel_id=1, source_target_pairs={{0,8},{1,9},{2,10},{3,11},{4,12},{5,13},{6,14},{7,15},{8,0},{9,1},... | collective-permute-start | bytes 5308424 | tf_op jit(solution)/shard_map/ppermute | solution.py:693
  438.1 29.7 %collective-permute-start.56 = (bf16[2,4,24,3456]{3,2,1,0:T(8,128)(2,1)}, bf16[2,4,24,3456]{3,2,1,0:T(8,128)(2,1)}, u32[]{:S(2)}, u32[]{:S(2)}) collective-permute-start(bf16[2,4,24,3456]{3,2,1,0:T(8,128)(2,1)} %fusion.7), channel_id=1, source_target_pairs={{0,16},{1,17},{2,18},{3,19},{4,20},{5,21},{6,22},{7,23},{8,9},{9,8... | collective-permute-start | bytes 3981320 | tf_op jit(solution)/shard_map/ppermute | solution.py:693
  440.4 19.5 %collective-permute-start.38 = (f32[52,768]{1,0:T(8,128)}, f32[52,768]{1,0:T(8,128)}, u32[]{:S(2)}, u32[]{:S(2)}) collective-permute-start(f32[52,768]{1,0:T(8,128)} %add.692), channel_id=1, source_target_pairs={{0,16},{1,17},{2,18},{3,19},{4,20},{5,21},{6,22},{7,23},{8,24},{9,... | collective-permute-start | bytes 479240 | tf_op jit(solution)/shard_map/ppermute | solution.py:693
  446.1 63.5 %collective-permute-start.55 = (bf16[2,4,24,3456]{3,2,1,0:T(8,128)(2,1)}, bf16[2,4,24,3456]{3,2,1,0:T(8,128)(2,1)}, u32[]{:S(2)}, u32[]{:S(2)}) collective-permute-start(bf16[2,4,24,3456]{3,2,1,0:T(8,128)(2,1)} %fusion.6), channel_id=1, source_target_pairs={{0,16},{1,17},{2,18},{3,19},{4,20},{5,21},{6,22},{7,23},{8,9},{9,8... | collective-permute-start | bytes 3981320 | tf_op jit(solution)/shard_map/ppermute | solution.py:693
  461.6 21.1 %collective-permute-start.41 = (f32[2,612]{1,0:T(2,128)S(1)}, f32[2,612]{1,0:T(2,128)S(1)}, u32[]{:S(2)}, u32[]{:S(2)}) collective-permute-start(f32[2,612]{1,0:T(2,128)S(1)} %pad_maximum_fusion.14), channel_id=1, source_target_pairs={{0,6},{1,7},{2,0},{3,1},{4,2},{5,3},{6,4},{7,5},{8,14},{9,15},{10,... | collective-permute-start | bytes 14696 | tf_op jit(solution)/shard_map/ppermute | solution.py:693
  461.8 22.2 %collective-permute-start.40 = (f32[2,612]{1,0:T(2,128)S(1)}, f32[2,612]{1,0:T(2,128)S(1)}, u32[]{:S(2)}, u32[]{:S(2)}) collective-permute-start(f32[2,612]{1,0:T(2,128)S(1)} %pad_maximum_fusion.13), channel_id=1, source_target_pairs={{0,4},{1,5},{2,6},{3,7},{4,0},{5,1},{6,2},{7,3},{8,12},{9,13},{10,... | collective-permute-start | bytes 14696 | tf_op jit(solution)/shard_map/ppermute | solution.py:693
  464.4 21.6 %collective-permute-start.39 = (f32[2,612]{1,0:T(2,128)S(1)}, f32[2,612]{1,0:T(2,128)S(1)}, u32[]{:S(2)}, u32[]{:S(2)}) collective-permute-start(f32[2,612]{1,0:T(2,128)S(1)} %pad_maximum_fusion.12), channel_id=1, source_target_pairs={{0,2},{1,3},{2,4},{3,5},{4,6},{5,7},{6,0},{7,1},{8,10},{9,11},{10,... | collective-permute-start | bytes 14696 | tf_op jit(solution)/shard_map/ppermute | solution.py:693
  480.6 29.0 %collective-permute-start.57 = (bf16[2,4,24,3456]{3,2,1,0:T(8,128)(2,1)S(1)}, bf16[2,4,24,3456]{3,2,1,0:T(8,128)(2,1)}, u32[]{:S(2)}, u32[]{:S(2)}) collective-permute-start(bf16[2,4,24,3456]{3,2,1,0:T(8,128)(2,1)S(1)} %fusion.1), channel_id=1, source_target_pairs={{0,1},{1,0},{2,3},{3,2},{4,5},{5,4},{6,7},{7,6},{8,24},{9,25},{10,... | collective-permute-start | bytes 3981320 | tf_op jit(solution)/shard_map/ppermute | solution.py:693
  482.7 13.4 %collective-permute-start.43 = (bf16[2,4,24,1152]{3,2,1,0:T(8,128)(2,1)}, bf16[2,4,24,1152]{3,2,1,0:T(8,128)(2,1)}, u32[]{:S(2)}, u32[]{:S(2)}) collective-permute-start(bf16[2,4,24,1152]{3,2,1,0:T(8,128)(2,1)} %fusion.18), channel_id=1, source_target_pairs={{0,16},{1,17},{2,18},{3,19},{4,20},{5,21},{6,22},{7,23},{8,9},{9,8... | collective-permute-start | bytes 1327112 | tf_op jit(solution)/shard_map/ppermute | solution.py:693
  484.0 19.8 %collective-permute-start.45 = (bf16[2,4,24,1152]{3,2,1,0:T(8,128)(2,1)}, bf16[2,4,24,1152]{3,2,1,0:T(8,128)(2,1)}, u32[]{:S(2)}, u32[]{:S(2)}) collective-permute-start(bf16[2,4,24,1152]{3,2,1,0:T(8,128)(2,1)} %fusion.10), channel_id=1, source_target_pairs={{0,1},{1,0},{2,3},{3,2},{4,5},{5,4},{6,7},{7,6},{8,24},{9,25},{10,... | collective-permute-start | bytes 1327112 | tf_op jit(solution)/shard_map/ppermute | solution.py:693
  518.0 30.4 %collective-permute-start.59 = (bf16[2,24,3456]{2,1,0:T(8,128)(2,1)S(1)}, bf16[2,24,3456]{2,1,0:T(8,128)(2,1)S(1)}, u32[]{:S(2)}, u32[]{:S(2)}) collective-permute-start(bf16[2,24,3456]{2,1,0:T(8,128)(2,1)S(1)} %get-tuple-element.156), channel_id=1, source_target_pairs={{0,4},{1,5},{2,6},{3,7},{4,0},{5,1},{6,2},{7,3},{8,12},{9,13},{10,... | collective-permute-start | bytes 995336 | tf_op jit(solution)/shard_map/ppermute | solution.py:693
  518.8 29.7 %collective-permute-start.58 = (bf16[2,24,3456]{2,1,0:T(8,128)(2,1)S(1)}, bf16[2,24,3456]{2,1,0:T(8,128)(2,1)S(1)}, u32[]{:S(2)}, u32[]{:S(2)}) collective-permute-start(bf16[2,24,3456]{2,1,0:T(8,128)(2,1)S(1)} %get-tuple-element.154), channel_id=1, source_target_pairs={{0,2},{1,3},{2,4},{3,5},{4,6},{5,7},{6,0},{7,1},{8,10},{9,11},{10,... | collective-permute-start | bytes 995336 | tf_op jit(solution)/shard_map/ppermute | solution.py:693
  (60 other events, 605.5 us)
Sparse Core Ops, SparseCore 0:
  14.0 142.8 all-gather.1

commit v3 on v2

--- a/solution.py
+++ b/solution.py
@@ -20,6 +20,7 @@
 NEG = -1e30
 TILE = 768
 WIDE = 384
+GROUP = 4
 BLOCK = 16
 SMALL_ROWS = 32
 F32 = jnp.float32
@@ -28,7 +29,7 @@
 
 
 def cost(us):
-    return pl.CostEstimate(flops=us * 1_100_000_000, bytes_accessed=us * 3_500_000, transcendentals=0)
+    return pl.CostEstimate(flops=us * 4_400_000_000, bytes_accessed=us * 14_000_000, transcendentals=0)
 
 
 ANY = pl.BlockSpec(memory_space=pl.ANY)
@@ -68,9 +69,15 @@
     return out
 
 
-def bias_kernel(heads, small_ref, rows_ref, lanes_ref, out_ref, wide_ref):
-    head = lax.rem(pl.program_id(0), heads)
-    table = small_ref[0, pl.ds(TABLE + head, 1), :]
+def bias_kernel(heads, small_ref, rows_ref, lanes_ref, *refs):
+    out_ref, wide_ref = refs[-2:]
+    first = lax.rem(pl.program_id(0) * GROUP, heads)
+    for i in range(GROUP):
+        table = small_ref[0, pl.ds(TABLE + first + i, 1), :]
+        one_bias(table, rows_ref, lanes_ref, out_ref.at[i], wide_ref.at[i])
+
+
+def one_bias(table, rows_ref, lanes_ref, out_ref, wide_ref):
     shifted = pltpu.roll(jnp.broadcast_to(table, (BLOCK, TILE)), TILE - (GRID - 1), 1)
     shifted = pltpu.roll(shifted, 0, 1, stride=1, stride_axis=0)
     for c in range(GRID):
@@ -84,33 +91,39 @@
     val = jnp.where(lane == 0, table[:, cls : cls + 1], val)
     first = jnp.where(lane == 0, table[:, cls + 2 : cls + 3], table[:, cls + 1 : cls + 2])
     val = jnp.where(row == 0, first, val)
-    out_ref[0] = jnp.where(row >= IMG_ROWS, NEG, val)
-
-
-def build_bias(small, heads):
+    out_ref[...] = jnp.where(row >= IMG_ROWS, NEG, val)
+
+
+def build_bias(small, heads, after=()):
     layers = small.shape[0]
     return pl.pallas_call(
         functools.partial(bias_kernel, heads),
-        grid=(layers * heads,),
+        grid=(layers * heads // GROUP,),
         out_shape=jax.ShapeDtypeStruct((layers * heads, PAD_ROWS, LANES), F32),
         in_specs=[
-            pl.BlockSpec((1, SMALL_ROWS, TILE), lambda h: (h // heads, 0, 0)),
+            pl.BlockSpec((1, SMALL_ROWS, TILE), lambda h: (h * GROUP // heads, 0, 0)),
             pl.BlockSpec((PAD_ROWS, BLOCK * GRID), lambda h: (0, 0)),
             pl.BlockSpec((WIDE, LANES), lambda h: (0, 0)),
-        ],
-        out_specs=pl.BlockSpec((1, PAD_ROWS, LANES), lambda h: (h, 0, 0)),
-        scratch_shapes=[pltpu.VMEM((BLOCK * GRID, WIDE), B16)],
-        compiler_params=params(),
-        cost_estimate=cost(18),
+        ]
+        + [ANY] * len(after),
+        out_specs=pl.BlockSpec((GROUP, PAD_ROWS, LANES), lambda h: (h, 0, 0)),
+        scratch_shapes=[pltpu.VMEM((GROUP, BLOCK * GRID, WIDE), B16)],
+        compiler_params=params(),
+        cost_estimate=cost(10),
         name="bias_expand",
-    )(small, jnp.asarray(row_onehot(False), B16), jnp.asarray(lane_onehot(), B16))
+    )(small, jnp.asarray(row_onehot(False), B16), jnp.asarray(lane_onehot(), B16), *after)
 
 
 def bias_grad_kernel(g_ref, rows_ref, lanes_ref, *refs):
     out_ref, acc_ref = refs[-2:]
+    for i in range(GROUP):
+        one_bias_grad(g_ref.at[i], rows_ref, lanes_ref, out_ref.at[i], acc_ref.at[i])
+
+
+def one_bias_grad(g_ref, rows_ref, lanes_ref, out_ref, acc_ref):
     row = lax.broadcasted_iota(jnp.int32, (PAD_ROWS, LANES), 0)
     lane = lax.broadcasted_iota(jnp.int32, (PAD_ROWS, LANES), 1)
-    g = jnp.where((lane < IMG_ROWS) & (row < IMG_ROWS), g_ref[0], 0.0)
+    g = jnp.where((lane < IMG_ROWS) & (row < IMG_ROWS), g_ref[...], 0.0)
     high = g.astype(B16)
     wide = None
     for part in (high, (g - high.astype(F32)).astype(B16)):
@@ -131,28 +144,28 @@
     cls = SPAN * SPAN
     total = jnp.where(spot == cls, to_patch, total)
     total = jnp.where(spot == cls + 1, from_patch, total)
-    out_ref[0] = jnp.where(spot == cls + 2, to_self, total)
+    out_ref[...] = jnp.where(spot == cls + 2, to_self, total)
 
 
 def reduce_bias(grad, after=()):
     heads = grad.shape[0]
     out = pl.pallas_call(
         bias_grad_kernel,
-        grid=(heads,),
+        grid=(heads // GROUP,),
         out_shape=jax.ShapeDtypeStruct((heads, 1, TILE), F32),
         in_specs=[
-            pl.BlockSpec((1, PAD_ROWS, LANES), lambda h: (h, 0, 0)),
+            pl.BlockSpec((GROUP, PAD_ROWS, LANES), lambda h: (h, 0, 0)),
             pl.BlockSpec((BLOCK * GRID, PAD_ROWS), lambda h: (0, 0)),
             pl.BlockSpec((LANES, WIDE), lambda h: (0, 0)),
         ]
         + [ANY] * len(after),
-        out_specs=pl.BlockSpec((1, 1, TILE), lambda h: (h, 0, 0)),
-        scratch_shapes=[pltpu.VMEM((BLOCK, TILE), F32)],
-        compiler_params=params(),
-        cost_estimate=cost(11),
+        out_specs=pl.BlockSpec((GROUP, 1, TILE), lambda h: (h, 0, 0)),
+        scratch_shapes=[pltpu.VMEM((GROUP, BLOCK, TILE), F32)],
+        compiler_params=params(),
+        cost_estimate=cost(6),
         name="bias_reduce",
     )(grad, jnp.asarray(row_onehot(True).T, B16), jnp.asarray(lane_onehot().T, B16), *after)
-    return out.reshape(heads, TILE)
+    return out
 
 
 def head_mask(which):
@@ -703,7 +716,7 @@
 def no_sooner(arrays):
     zero = jnp.zeros((), B16)
     for v in arrays:
-        zero = zero + jnp.minimum(jnp.abs(v.reshape(-1)[0]), 0)
+        zero = zero + jnp.minimum(jnp.abs(v[(0,) * v.ndim]), 0).astype(B16)
     return zero
 
 
@@ -724,10 +737,16 @@
         self.moved = [send(piece, Z_SHIFT[k]) for k in range(1, CHIP_Z)]
         return self.moved
 
-    def plane(self):
+    def plane(self, behind=()):
         base = jnp.stack([self.piece] + self.moved)
-        first = send(base, PLANE[0])
-        self.own = [base, first, send(base, PLANE[1]), send(first, PLANE[1])]
+        if behind:
+            base = base + no_sooner(behind)
+        self.own = [base, send(base, PLANE[0]), send(base, PLANE[1])]
+        return self.own
+
+    def far(self, behind=()):
+        first = self.own[1] + no_sooner(behind) if behind else self.own[1]
+        self.own.append(send(first, PLANE[1]))
         self.other = [send(v, CORE_SWAP) for v in self.own]
 
     def finish(self, after=()):
@@ -786,12 +805,6 @@
     return v
 
 
-def sum_everywhere(v):
-    v = sum_plane(v)
-    parts = [send(v, Z_SHIFT[k]) for k in range(1, CHIP_Z)]
-    return v + parts[0] + parts[1] + parts[2]
-
-
 class Reduction:
     def __init__(self, theirs, mine):
         self.theirs = theirs
@@ -818,8 +831,11 @@
 
     def far(self):
         self.r3 = send(self.part(1, 1).astype(B16), PLANE[1])
+        return [self.r3]
+
+    def side(self):
         self.r2 = send(self.part(0, 1).astype(B16), PLANE[1])
-        return [self.r3, self.r2]
+        return [self.r2]
 
     def near(self):
         self.r1 = send((self.part(1, 0) + self.r3.astype(F32)).astype(B16), PLANE[0])
@@ -835,8 +851,8 @@
         self.rz = [send(at_z(k).astype(B16), Z_SHIFT[k]) for k in range(1, CHIP_Z)]
         return self.rz
 
-    def finish(self):
-        total = self.mine
+    def finish(self, behind=()):
+        total = self.mine + no_sooner(behind).astype(F32) if behind else self.mine
         for r in self.rz:
             total = total + r.astype(F32)
         c = self.c
@@ -875,6 +891,145 @@
         cost_estimate=cost(5),
         name="unpack",
     )(packed, *after)
+
+
+def fence_kernel(last_ref, *refs):
+    refs[-1][...] = last_ref[...]
+
+
+def fence(last, after):
+    whole = pl.BlockSpec(memory_space=pltpu.VMEM)
+    return pl.pallas_call(
+        fence_kernel,
+        out_shape=jax.ShapeDtypeStruct(last.shape, F32),
+        in_specs=[whole] + [ANY] * len(after),
+        out_specs=whole,
+        compiler_params=params(),
+        cost_estimate=cost(25),
+        name="fence",
+    )(last, *after)
+
+
+def small_offsets(own, entries, device):
+    per_row = TILE // (4 * own)
+    return own * device, 4 * own * lax.rem(device, per_row), entries * device, device // per_row
+
+
+def by_row(vectors, hidden, tables):
+    row = lax.broadcasted_iota(jnp.int32, vectors.shape, 0)
+    return jnp.where(row < B_ONE, vectors, jnp.where(row < TABLE, hidden, tables))
+
+
+def own_kernel(*refs):
+    out_ref, tmp_ref = refs[-2:]
+    hidden_ref, table_ref = refs[-4:-2]
+    tmp_ref[...] = jnp.zeros_like(tmp_ref)
+    for layer in range(LAYERS):
+        for i, ref in enumerate(refs[:B_ONE]):
+            tmp_ref[layer, i : i + 1, : ref.shape[1]] = ref[layer : layer + 1, :].astype(F32)
+        for i in range(B_ONE, TABLE):
+            tmp_ref[layer, i : i + 1, : hidden_ref.shape[1]] = hidden_ref[
+                layer : layer + 1, :
+            ].astype(F32)
+        heads, entries = table_ref.shape[1:]
+        tmp_ref[layer, TABLE : TABLE + heads, :entries] = table_ref[layer].astype(F32)
+    out_ref[...] = tmp_ref[...].astype(B16)
+
+
+def own_small(vectors, hidden, table):
+    whole = pl.BlockSpec(memory_space=pltpu.VMEM)
+    return pl.pallas_call(
+        own_kernel,
+        out_shape=jax.ShapeDtypeStruct((LAYERS, SMALL_ROWS, STRIP), B16),
+        in_specs=[whole] * (len(vectors) + 2),
+        out_specs=whole,
+        scratch_shapes=[pltpu.VMEM((LAYERS, SMALL_ROWS, STRIP), F32)],
+        compiler_params=params(),
+        cost_estimate=cost(1),
+        name="small_own",
+    )(*vectors, hidden, table)
+
+
+def place_kernel(own, entries, device_ref, *refs):
+    out_ref = refs[-1]
+    row = lax.broadcasted_iota(jnp.int32, (SMALL_ROWS, TILE), 0)
+    for layer in range(out_ref.shape[0]):
+        total = jnp.zeros((SMALL_ROWS, TILE), F32)
+        for k, piece_ref in enumerate(refs[:-1]):
+            vec_at, b1_at, tab_at, line = small_offsets(own, entries, device_ref[k])
+            piece = piece_ref[layer].astype(F32)
+            rest = jnp.zeros((SMALL_ROWS, TILE - piece.shape[1]), F32)
+            wide = jnp.concatenate([piece, rest], axis=1)
+            hidden = jnp.where(row - B_ONE == line, pltpu.roll(wide, b1_at, 1), 0.0)
+            total += by_row(pltpu.roll(wide, vec_at, 1), hidden, pltpu.roll(wide, tab_at, 1))
+        out_ref[layer] = total.astype(B16)
+
+
+def put_small(pieces, devices, own, entries):
+    whole = pl.BlockSpec(memory_space=pltpu.VMEM)
+    return pl.pallas_call(
+        functools.partial(place_kernel, own, entries),
+        out_shape=jax.ShapeDtypeStruct(pieces[0].shape[:2] + (TILE,), B16),
+        in_specs=[SMEM] + [whole] * len(pieces),
+        out_specs=whole,
+        compiler_params=params(),
+        cost_estimate=cost(1),
+        name="small_place",
+    )(devices, *pieces)
+
+
+def collect_kernel(own, entries, device_ref, total_ref, *refs):
+    outs = refs[-device_ref.shape[0] :]
+    for k, out_ref in enumerate(outs):
+        vec_at, b1_at, tab_at, line = small_offsets(own, entries, device_ref[k])
+
+        def turn(v, at):
+            return pltpu.roll(v, lax.rem(TILE - at, TILE), 1)
+
+        for layer in range(total_ref.shape[0]):
+            total = total_ref[layer]
+            hidden = jnp.broadcast_to(total_ref[layer, pl.ds(B_ONE + line, 1), :], total.shape)
+            wide = by_row(turn(total, vec_at), turn(hidden, b1_at), turn(total, tab_at))
+            out_ref[layer] = wide[:, : out_ref.shape[2]]
+
+
+def collect(total, devices, own, entries, after=()):
+    whole = pl.BlockSpec(memory_space=pltpu.VMEM)
+    count = devices.shape[0]
+    piece = jax.ShapeDtypeStruct(total.shape[:2] + (STRIP,), F32)
+    return pl.pallas_call(
+        functools.partial(collect_kernel, own, entries),
+        out_shape=[piece] * count,
+        in_specs=[SMEM, whole] + [ANY] * len(after),
+        out_specs=[whole] * count,
+        compiler_params=params(),
+        cost_estimate=cost(2),
+        name="small_collect",
+    )(devices, total, *after)
+
+
+def pack_kernel(*refs):
+    out_ref = refs[-1]
+    out_ref[...] = jnp.zeros_like(out_ref)
+    for layer in range(LAYERS):
+        first, second, table = refs[3 * layer : 3 * layer + 3]
+        out_ref[layer, 0:B_PROJ] = first[0:B_PROJ]
+        out_ref[layer, B_PROJ:TABLE] = second[0 : TABLE - B_PROJ]
+        for head in range(table.shape[0]):
+            out_ref[layer, TABLE + head : TABLE + head + 1] = table[head]
+
+
+def pack_small(parts, after=()):
+    whole = pl.BlockSpec(memory_space=pltpu.VMEM)
+    return pl.pallas_call(
+        pack_kernel,
+        out_shape=jax.ShapeDtypeStruct((LAYERS, SMALL_ROWS, TILE), F32),
+        in_specs=[whole] * len(parts) + [ANY] * len(after),
+        out_specs=whole,
+        compiler_params=params(),
+        cost_estimate=cost(2),
+        name="small_pack",
+    )(*parts, *after)
 
 
 def per_device(
@@ -901,46 +1056,46 @@
     def cut_rows(v):
         return v.reshape(images, PAD_ROWS, width)[:, :IMG_ROWS].reshape(images * IMG_ROWS, width)
 
-    def everywhere(v):
-        return sum_everywhere(v) if fast else lax.psum(v, AXES)
-
-    def placed(shard, total):
-        empty = jnp.zeros(shard.shape[:-1] + (total,), shard.dtype)
-        at = (0,) * (shard.ndim - 1) + (me * shard.shape[-1],)
-        return lax.dynamic_update_slice(empty, shard, at)
-
-    small = jnp.concatenate(
-        [
-            placed(jnp.stack(vectors, axis=1), width),
-            placed(fc1_bias, hidden).reshape(LAYERS, ratio, width),
-            placed(rel_table, TILE),
-        ],
-        axis=1,
-    )
-    used = small.shape[1]
-    small = everywhere(small.reshape(LAYERS * used, width)).reshape(LAYERS, used, width)
-    small = jnp.pad(small.astype(F32), ((0, 0), (0, SMALL_ROWS - used), (0, 0)))
-    bias = build_bias(small, heads)
+    used = TABLE + heads
+    piece = own_small(vectors, fc1_bias, rel_table)
+    hops = range(CHIP_Z) if fast else range(1)
+    ring = CHIP_Z * CHIP_X
+
+    def along_z(k):
+        return (me // ring) * ring + (me + k * CHIP_X) % ring if fast else me
+
+    backs = jnp.stack([along_z(-k) for k in hops]).astype(jnp.int32)
+    ahead = jnp.stack([along_z(k) for k in hops]).astype(jnp.int32)
+    pieces = [piece] + [send(piece, Z_SHIFT[k]) for k in hops[1:]]
+    small = put_small(pieces, backs, own, entries)
+    small = (sum_plane(small) if fast else lax.psum(small, AXES)).astype(F32)
 
     def two_blocks(layer):
         return fc2_weight[layer].reshape(ratio, own, width)
 
-    def fetch_packed(layer):
+    def fetch_packed(layer, behind=()):
         two = two_blocks(layer)
         block = jnp.concatenate(
             [qkv_weight[layer], proj_weight[layer], fc1_weight[layer]]
             + [two[i] for i in range(ratio)],
             axis=1,
         )
+        if behind:
+            block = block + no_sooner(behind)
         return lax.all_gather(block, AXES, axis=0, tiled=True)
 
-    packed_weights = [None if fast and layer == 0 else fetch_packed(layer) for layer in range(LAYERS)]
-    if fast:
+    if not fast:
+        packed_weights = [fetch_packed(layer) for layer in range(LAYERS)]
+        bias = build_bias(small, heads)
+    else:
         first = Gathering([qkv_weight[0][None], proj_weight[0][None]])
         second = Gathering([fc1_weight[0][None], two_blocks(0)])
-        second.along(first.along())
+        moved = first.along()
         first.plane()
-        second.plane()
+        first.far()
+        moved = second.along(moved)
+        bias = build_bias(small, heads, [moved[0], moved[2]])
+        packed_weights = [None, fetch_packed(1)]
     weights = []
     x = pad_rows(tokens)
     saved = []
@@ -957,7 +1112,9 @@
         att, lse = attention_forward(qkv, bias, layer)
         att = att.reshape(images * PAD_ROWS, width)
         if full is None:
-            w_one, w_two = second.finish([att])
+            second.plane([w_qkv[0]])
+            second.far([att])
+            w_one, w_two = second.finish()
             w_one = (w_one.reshape(width, hidden), 0)
         elif fast:
             w_two = unpack_two(full.reshape(shards, own, -1), 4 * width + hidden, ratio, width)
@@ -999,12 +1156,12 @@
         d_qkv, d_bias = attention_backward(
             qkv, bias, lse, d_att.reshape(images, PAD_ROWS, width), layer, hooks[1](main)
         )
+        tables[layer] = d_bias
         theirs, mine, grad, qkv_sums = qkv_backward(
             core, d_qkv.reshape(images * PAD_ROWS, 3 * width), h, x, d_mid, small, layer, w_qkv,
             hooks[2](),
         )
         small_grads[layer] = (qkv_sums, mlp_sums)
-        tables[layer] = d_bias
         return grad, main, (theirs, mine)
 
     if not fast:
@@ -1026,64 +1183,52 @@
 
         grad, _, rest = backward(1, grad, (lambda: (), one_attention, one_qkv))
         b1 = Reduction(*rest)
-        a1.far()
 
         def zero_mlp():
-            return ()
+            return a1.far()
 
         def zero_attention(main):
             nonlocal a0
             a0 = Reduction(*main)
-            b1.swap()
-            return [a1.r3, a1.r2, b1.got]
+            a0.swap()
+            return a1.side() + b1.swap()
 
         def zero_qkv():
-            return a1.near() + b1.far() + a0.swap()
+            for layer in range(LAYERS):
+                tables[layer] = reduce_bias(tables[layer])
+            moved = a1.near() + b1.far() + a0.far()
+            a1.along()
+            return moved + a1.rz + [tables[0], tables[1]]
 
         grad, _, rest = backward(0, grad, (zero_mlp, zero_attention, zero_qkv))
         b0 = Reduction(*rest)
-        a0.far()
-        a1.along()
+        a0.side()
+        a0.near()
+        b1.side()
+        b0.swap()
+
+    parts = []
+    for (qkv_sums, mlp_sums), table in zip(small_grads, tables):
+        parts += [qkv_sums, mlp_sums, table]
+    totals = pack_small(parts, [b0.got] if fast else ())
+    totals = sum_plane(totals) if fast else lax.psum(totals, AXES)
+    late = ()
+    if fast:
         b1.near()
-        b0.swap()
-        tables[1] = reduce_bias(tables[1])
-        b0.far()
-        a0.near()
-        b1.along()
-        tables[0] = reduce_bias(tables[0])
         a0.along()
-        b0.near()
+        gate = fence(small_grads[0][0], b0.far() + b0.side() + [b1.r1, a0.rz[0], a0.rz[2], totals])
+        late = [gate, a0.rz[1]] + b1.along() + b0.near()
+    pieces = collect(totals, ahead, own, entries, late)
+    if fast:
         b0.along()
-        reduced[1] = (a1.finish(), b1.finish())
-        reduced[0] = (a0.finish(), b0.finish())
-
-    rows = []
-    for (qkv_sums, mlp_sums), table in zip(small_grads, tables):
-        rows += [qkv_sums[:4], mlp_sums[: TABLE - B_PROJ], table]
-    totals = jnp.concatenate(rows, axis=0)
-    totals = sum_plane(totals) if fast else lax.psum(totals, AXES)
-    totals = totals.reshape(LAYERS, used, width)
-
-    def owned_by(device):
-        def cut(v, size):
-            return lax.dynamic_slice_in_dim(v, device * size, size, axis=v.ndim - 1)
-
-        g_vec = cut(totals[:, :B_ONE], own).reshape(LAYERS, -1)
-        g_b1 = cut(totals[:, B_ONE:TABLE].reshape(LAYERS, hidden), ratio * own)
-        g_tab = cut(totals[:, TABLE:], entries).reshape(LAYERS, -1)
-        return jnp.concatenate([g_vec, g_b1, g_tab], axis=1)
-
-    g_small = owned_by(me)
-    if fast:
-        per_z = CHIP_X
-        ring = CHIP_Z * CHIP_X
-        for k in range(1, CHIP_Z):
-            device = (me // ring) * ring + (me + k * per_z) % ring
-            g_small = g_small + send(owned_by(device), Z_SHIFT[k])
-    g = g_small[:, : B_ONE * own].reshape(LAYERS, B_ONE, own)
-    g = [g[:, i] for i in range(B_ONE)]
-    g_b1 = g_small[:, B_ONE * own : (B_ONE + ratio) * own]
-    g_table = g_small[:, (B_ONE + ratio) * own :].reshape(LAYERS, heads, entries)
+        reduced[1] = (a1.finish([pieces[0]]), b1.finish([pieces[0]]))
+        reduced[0] = (a0.finish([pieces[0]]), b0.finish())
+    g_small = pieces[0]
+    for k in hops[1:]:
+        g_small = g_small + send(pieces[k], Z_SHIFT[k])
+    g = [g_small[:, i, :own] for i in range(B_ONE)]
+    g_b1 = g_small[:, B_ONE, : ratio * own]
+    g_table = g_small[:, TABLE:used, :entries]
 
     def both(pick):
         return jnp.stack([pick(*r) for r in reduced])

time: 566 us -> 508 us (0.90)
  waiting for transfers between devices: 170 us -> 122 us
  local copies, waits for them, and re-layouts: 21.4 us -> 49.5 us
  starting transfers between devices: 101 us -> 79.4 us
  Pallas kernels: 205 us -> 196 us
  other arithmetic: 45.4 us -> 37.5 us
    ppermute x66, waiting for transfers between devices: 169 us -> 122 us  [send(): return lax.ppermute(v, AXES, pairs)]
    ppermute x66, starting transfers between devices: 101 us -> 79.4 us  [send(): return lax.ppermute(v, AXES, pairs)]
    dynamic_slice x3 -> x6, local copies, waits for them, and re-layouts: 0.3 us -> 17.3 us  [cut(): return lax.dynamic_slice(v, at, size)[0, :, :, 0].astype(F32)]
    ppermute x0 -> x6, local copies, waits for them, and re-layouts: none -> 10.9 us  [send(): return lax.ppermute(v, AXES, pairs)]
    pallas_call x1, Pallas kernels: 17.8 us -> 10.2 us  [build_bias(): pl.pallas_call(functools.partial(bias_kernel, heads), grid=(layers * head...]
    pallas_call x2 -> x7, Pallas kernels: 22.4 us -> 21.1 us  [the longest x2 12.9 us: reduce_bias(): pl.pallas_call(bias_grad_kernel, grid=(heads // GROUP,), out_shape=jax.Sh...]
  transfers between devices with their start and end apart: 67 -> 67, of which waited for: 25 -> 19; matrix products, arithmetic and copies ran while one was open for 9% -> 14% of each run, Pallas kernels for 25% -> 27%
where the time goes in v3:
time: 508 us; the launch traced here: 504 us
  Pallas kernels  196 us (39%)
  waiting for transfers between devices  122 us (24%)
  starting transfers between devices  79.4 us (16%)
  local copies, waits for them, and re-layouts  49.5 us (10%)
  other arithmetic  37.5 us (7%)
  between operations  19.7 us (4%)
    ppermute x66, waiting for transfers between devices, send(): return lax.ppermute(v, AXES, pairs)  122 us
    ppermute x66, starting transfers between devices, send(): return lax.ppermute(v, AXES, pairs)  79.4 us
    pallas_call x2, Pallas kernels, mlp_backward(): pl.pallas_call(mlp_grad_kernel, grid=(hidden // TILE,), out_shape=(jax.Sh...  40.7 us
    pallas_call x2, Pallas kernels, mlp_forward(): pl.pallas_call(mlp_kernel, grid=(hidden // TILE,), out_shape=(full, full,...  31 us
    pallas_call x2, Pallas kernels, attention_backward(): pl.pallas_call(functools.partial(attention_grad_kernel, width), grid=(ima...  23.5 us
    pallas_call x2, Pallas kernels, qkv_backward(): pl.pallas_call(qkv_grad_kernel, grid=(3,), out_shape=(jax.ShapeDtypeStruc...  22.6 us
    dynamic_slice x6, local copies, waits for them, and re-layouts, cut(): return lax.dynamic_slice(v, at, size)[0, :, :, 0].astype(F32)  17.3 us
    pallas_call x2, Pallas kernels, attention_forward(): pl.pallas_call(functools.partial(attention_kernel, width), grid=(images,)...  16.7 us
  transfers between devices with their start and end apart: 67, of which 19 were waited for; matrix products, arithmetic and copies ran while one was open for 14% of the time, Pallas kernels for 27%

profile of v3, /device:TPU:0, one launch (start us, length us, event | category | flops | bytes accessed | tf_op | source)
XLA Modules:
  0.0 503.9 jit_solution(18319301614237657861)
XLA Ops:
  10.1 3.0 collective-permute-start
  13.1 2.6 collective-permute-start.1
  20.1 3.7 collective-permute-done.9
  23.8 3.3 collective-permute-start.2
  27.1 12.9 %collective-permute-done.8 = bf16[2,24,1536]{2,1,0:T(8,128)(2,1)S(1)} collective-permute-done((bf16[2,24,1536]{2,1,0:T(8,128)(2,1)S(1)}, bf16[2,24,1536]{2,1,0:T(8,128)(2,1)S(1)}, u32[]{:S(2)}, u32[]{:S(2)}) %collective-permute-start.8) | collective-permute-done | bytes 147488 | tf_op jit(solution)/shard_map/ppermute | solution.py:706
  48.0 10.1 %collective-permute-done.4 = bf16[2,32,768]{2,1,0:T(8,128)(2,1)S(1)} collective-permute-done((bf16[2,32,768]{2,1,0:T(8,128)(2,1)S(1)}, bf16[2,32,768]{2,1,0:T(8,128)(2,1)S(1)}, u32[]{:S(2)}, u32[]{:S(2)}) %collective-permute-start.4) | collective-permute-done | bytes 98336 | tf_op jit(solution)/shard_map/ppermute | solution.py:706
  66.5 2.8 collective-permute-start.19
  70.6 10.5 %collective-permute-done.18.refs_0_ = bf16[2,24,3072]{2,1,0:T(8,128)(2,1)S(1)} collective-permute-done((bf16[2,24,3072]{2,1,0:T(8,128)(2,1)S(1)}, bf16[2,24,3072]{2,1,0:T(8,128)(2,1)S(1)}, u32[]{:S(2)}, u32[]{:S(2)}) %collective-permute-start.18) | collective-permute-done | bytes 294944 | tf_op jit(solution)/shard_map/ppermute | solution.py:706
  81.0 11.6 %collective-permute-start.20 = (bf16[2,24,3072]{2,1,0:T(8,128)(2,1)S(1)}, bf16[2,24,3072]{2,1,0:T(8,128)(2,1)S(1)}, u32[]{:S(2)}, u32[]{:S(2)}) collective-permute-start(bf16[2,24,3072]{2,1,0:T(8,128)(2,1)S(1)} %get-tuple-element.231), channel_id=1, source_target_pairs={{0,4},{1,5},{2,6},{3,7},{4,0},{5,1},{6,2},{7,3},{8,12},{9,13},{10,... | collective-permute-start | bytes 884744 | tf_op jit(solution)/shard_map/ppermute | solution.py:706
  93.4 10.2 %bias_expand.1.refs_8_.bias_ref = f32[24,208,256]{2,1,0:T(8,128)} custom-call(f32[2,32,768]{2,1,0:T(8,128)} %add_convert_fusion.8.small_ref, bf16[208,224]{1,0:T(8,128)(2,1)} %constant.389.clone.rows_ref, bf16[384,256]{1,0:T(8,128)(2,1)} %constant.390.clone.lanes_ref, bf16[2,24,3072]{2,1,0:T(8,128)(2,1)} %copy-done.36, bf16[2,24,3072]{2,1,0:T(8,128)(2,1)} %copy-done.38), custom_call_target="tpu_custom_call" | custom-call | flops 44000002048 | bytes 140000000 | tf_op jit(solution)/shard_map/bias_expand/pallas_call | solution.py:99
  105.7 5.3 %assemble.2 = (bf16[32,1,24,2304]{3,2,1,0:T(8,128)(2,1)}, bf16[32,1,24,768]{3,2,1,0:T(8,128)(2,1)}) custom-call(s32[4]{0:T(128)} %pad_add_fusion.1.pos_ref, bf16[4,2,24,1536]{3,2,1,0:T(8,128)(2,1)} %copy-done.18, bf16[4,2,24,1536]{3,2,1,0:T(8,128)(2,1)} %copy-done.48, bf16[4,2,24,1536]{3,2,1,0:T(8,128)(2,1)} %copy-done.49, ...), custom_call_target="tpu_custom_call" | custom-call | flops 30799998976 | bytes 98000000 | tf_op jit(solution)/shard_map/assemble/pallas_call | solution.py:790
  116.6 5.9 %qkv.2 = (bf16[416,2304]{1,0:T(8,128)(2,1)}, bf16[416,768]{1,0:T(8,128)(2,1)}) custom-call(f32[416,768]{1,0:T(8,128)} %bitcast_convert_fusion.x_ref, f32[2,32,768]{2,1,0:T(8,128)} %add_convert_fusion.8.small_ref, bf16[768,2304]{1,0:T(8,128)(2,1)} %bitcast.320), custom_call_target="tpu_custom_call" | custom-call | flops 26400000000 | bytes 84000000 | tf_op jit(solution)/shard_map/qkv/pallas_call | solution.py:350
  122.5 8.3 %attention.2 = (bf16[2,208,768]{2,1,0:T(8,128)(2,1)}, f32[2,16,256]{2,1,0:T(8,128)}) custom-call(bf16[2,208,2304]{2,1,0:T(8,128)(2,1)} %bitcast.331, f32[24,208,256]{2,1,0:T(8,128)} %bias_expand.1.refs_8_.bias_ref), custom_call_target="tpu_custom_call" | custom-call | flops 35200000000 | bytes 112000000 | tf_op jit(solution)/shard_map/attention/pallas_call | solution.py:203
  132.6 14.4 %collective-permute-done.21.refs_1_ = bf16[4,2,24,3072]{3,2,1,0:T(8,128)(2,1)} collective-permute-done((bf16[4,2,24,3072]{3,2,1,0:T(8,128)(2,1)S(1)}, bf16[4,2,24,3072]{3,2,1,0:T(8,128)(2,1)}, u32[]{:S(2)}, u32[]{:S(2)}) %collective-permute-start.21) | collective-permute-done | bytes 1179680 | tf_op jit(solution)/shard_map/ppermute | solution.py:706
  150.6 14.3 %collective-permute-done.23.refs_3_ = bf16[4,2,24,3072]{3,2,1,0:T(8,128)(2,1)} collective-permute-done((bf16[4,2,24,3072]{3,2,1,0:T(8,128)(2,1)S(1)}, bf16[4,2,24,3072]{3,2,1,0:T(8,128)(2,1)}, u32[]{:S(2)}, u32[]{:S(2)}) %collective-permute-start.23) | collective-permute-done | bytes 1179680 | tf_op jit(solution)/shard_map/ppermute | solution.py:706
  168.1 8.2 %assemble.3 = (bf16[32,1,24,3072]{3,2,1,0:T(8,128)(2,1)}, bf16[32,4,24,768]{3,2,1,0:T(8,128)(2,1)}) custom-call(s32[4]{0:T(128)} %pad_add_fusion.1.pos_ref, bf16[4,2,24,3072]{3,2,1,0:T(8,128)(2,1)} %copy-done.14, bf16[4,2,24,3072]{3,2,1,0:T(8,128)(2,1)} %collective-permute-done.21.refs_1_, bf16[4,2,24,3072]{3,2,1,0:T(8,128)(2,1)} %collective-permute-done.22.refs_2_, ...), custom_call_target="tpu_custom_call" | custom-call | flops 30799998976 | bytes 98000000 | tf_op jit(solution)/shard_map/assemble/pallas_call | solution.py:790
  176.3 15.6 %mlp.2 = (f32[416,768]{1,0:T(8,128)}, f32[416,768]{1,0:T(8,128)}, f32[416,768]{1,0:T(8,128)}, f32[416,768]{1,0:T(8,128)}, bf16[416,768]{1,0:T(8,128)(2,1)}, /*in...) custom-call(f32[416,768]{1,0:T(8,128)} %bitcast_convert_fusion.x_ref, bf16[416,768]{1,0:T(8,128)(2,1)} %bitcast.329, ...), custom_call_target="tpu_custom_call" | custom-call | flops 65999998976 | bytes 210000000 | tf_op jit(solution)/shard_map/mlp/pallas_call | solution.py:487
  191.9 5.9 %qkv.3 = (bf16[416,2304]{1,0:T(8,128)(2,1)}, bf16[416,768]{1,0:T(8,128)(2,1)}) custom-call(f32[416,768]{1,0:T(8,128)} %get-tuple-element.76.x_ref, f32[2,32,768]{2,1,0:T(8,128)} %add_convert_fusion.8.small_ref, bf16[768,9216]{1,0:T(8,128)(2,1)} %all-gather.2.cloned.1.call-done.w_ref.wp_ref.w1_ref), custom_call_target="tpu_custom_call" | custom-call | flops 26400000000 | bytes 84000000 | tf_op jit(solution)/shard_map/qkv/pallas_call | solution.py:350
  197.7 8.5 %attention.3 = (bf16[2,208,768]{2,1,0:T(8,128)(2,1)}, f32[2,16,256]{2,1,0:T(8,128)}) custom-call(bf16[2,208,2304]{2,1,0:T(8,128)(2,1)} %bitcast.334, f32[24,208,256]{2,1,0:T(8,128)} %bias_expand.1.refs_8_.bias_ref), custom_call_target="tpu_custom_call" | custom-call | flops 35200000000 | bytes 112000000 | tf_op jit(solution)/shard_map/attention/pallas_call | solution.py:203
  206.2 4.5 unpack.1
  210.7 15.4 %mlp.3 = (f32[416,768]{1,0:T(8,128)}, f32[416,768]{1,0:T(8,128)}, f32[416,768]{1,0:T(8,128)}, f32[416,768]{1,0:T(8,128)}, bf16[416,768]{1,0:T(8,128)(2,1)}, /*in...) custom-call(f32[416,768]{1,0:T(8,128)} %get-tuple-element.76.x_ref, bf16[416,768]{1,0:T(8,128)(2,1)} %bitcast.341, ...), custom_call_target="tpu_custom_call" | custom-call | flops 65999998976 | bytes 210000000 | tf_op jit(solution)/shard_map/mlp/pallas_call | solution.py:487
  228.5 20.3 %mlp_grad.2 = (bf16[768,3456]{1,0:T(8,128)(2,1)}, bf16[768,3456]{1,0:T(8,128)(2,1)}, f32[416,768]{1,0:T(8,128)}, bf16[416,768]{1,0:T(8,128)(2,1)}, f32[16,768]{1,0:T(8,128)}) custom-call(s32[1]{0:T(128)} %bitcast.7.core_ref, f32[416,768]{1,0:T(8,128)} %convert_select_fusion.g_ref, f32[416,768]{1,0:T(8,128)} %get-tuple-element.82.mid_ref, ...), custom_call_target="tpu_custom_call" | custom-call | flops 88000004096 | bytes 280000000 | tf_op jit(solution)/shard_map/mlp_grad/pallas_call | solution.py:647
  249.0 4.5 constant_dynamic-slice_fusion.13
  253.5 11.9 %attention_grad.2 = (bf16[2,208,2304]{2,1,0:T(8,128)(2,1)}, f32[12,208,256]{2,1,0:T(8,128)}) custom-call(bf16[2,208,2304]{2,1,0:T(8,128)(2,1)} %bitcast.335, f32[24,208,256]{2,1,0:T(8,128)} %bias_expand.1.refs_8_.bias_ref, f32[2,16,256]{2,1,0:T(8,128)} %get-tuple-element.81.lse_ref, bf16[2,208,768]{2,1,0:T(8,128)(2,1)} %bitcast.340), custom_call_target="tpu_custom_call" | custom-call | flops 52800000000 | bytes 168000000 | tf_op jit(solution)/shard_map/attention_grad/pallas_call | solution.py:269
  265.4 6.3 %bias_reduce.3.refs_7_.refs_5_ = f32[12,1,768]{2,1,0:T(1,128)} custom-call(f32[12,208,256]{2,1,0:T(8,128)} %get-tuple-element.110.g_ref, bf16[224,208]{1,0:T(8,128)(2,1)} %constant.391.clone.rows_ref, bf16[256,384]{1,0:T(8,128)(2,1)} %constant.392.clone.lanes_ref), custom_call_target="tpu_custom_call" | custom-call | flops 26400000000 | bytes 84000000 | tf_op jit(solution)/shard_map/bias_reduce/pallas_call | solution.py:152
  278.6 11.2 %qkv_grad.2 = (bf16[768,1152]{1,0:T(8,128)(2,1)}, bf16[768,1152]{1,0:T(8,128)(2,1)}, f32[416,768]{1,0:T(8,128)}, f32[8,768]{1,0:T(8,128)}) custom-call(s32[1]{0:T(128)} %bitcast.7.core_ref, bf16[416,2304]{1,0:T(8,128)(2,1)} %bitcast.336, bf16[416,768]{1,0:T(8,128)(2,1)} %get-tuple-element.90.h_ref, f32[416,768]{1,0:T(8,128)} %get-tuple-element.76.x_ref, ...), custom_call_target="tpu_custom_call" | custom-call | flops 48399998976 | bytes 154000000 | tf_op jit(solution)/shard_map/qkv_grad/pallas_call | solution.py:418
  289.9 2.7 constant_dynamic-slice_fusion.3
  296.0 20.4 %mlp_grad.3 = (bf16[768,3456]{1,0:T(8,128)(2,1)}, bf16[768,3456]{1,0:T(8,128)(2,1)}, f32[416,768]{1,0:T(8,128)}, bf16[416,768]{1,0:T(8,128)(2,1)}, f32[16,768]{1,0:T(8,128)}) custom-call(s32[1]{0:T(128)} %bitcast.7.core_ref, f32[416,768]{1,0:T(8,128)} %get-tuple-element.93.g_ref, f32[416,768]{1,0:T(8,128)} %get-tuple-element.94.mid_ref, ...), custom_call_target="tpu_custom_call" | custom-call | flops 88000004096 | bytes 280000000 | tf_op jit(solution)/shard_map/mlp_grad/pallas_call | solution.py:647
  317.1 2.5 copy.101.refs_0_
  319.6 4.4 constant_dynamic-slice_fusion.9
  324.0 2.6 constant_dynamic-slice_fusion.2
  328.4 11.6 %attention_grad.3 = (bf16[2,208,2304]{2,1,0:T(8,128)(2,1)}, f32[12,208,256]{2,1,0:T(8,128)}) custom-call(bf16[2,208,2304]{2,1,0:T(8,128)(2,1)} %bitcast.332, f32[24,208,256]{2,1,0:T(8,128)} %bias_expand.1.refs_8_.bias_ref, f32[2,16,256]{2,1,0:T(8,128)} %get-tuple-element.80.lse_ref, bf16[2,208,768]{2,1,0:T(8,128)(2,1)} %bitcast.339, ...), custom_call_target="tpu_custom_call" | custom-call | flops 52800000000 | bytes 168000000 | tf_op jit(solution)/shard_map/attention_grad/pallas_call | solution.py:269
  339.9 6.5 %bias_reduce.2.refs_6_.refs_2_ = f32[12,1,768]{2,1,0:T(1,128)} custom-call(f32[12,208,256]{2,1,0:T(8,128)} %get-tuple-element.109.g_ref, bf16[224,208]{1,0:T(8,128)(2,1)} %constant.391.clone.rows_ref, bf16[256,384]{1,0:T(8,128)(2,1)} %constant.392.clone.lanes_ref), custom_call_target="tpu_custom_call" | custom-call | flops 26400000000 | bytes 84000000 | tf_op jit(solution)/shard_map/bias_reduce/pallas_call | solution.py:152
  354.4 2.3 fusion.2
  362.4 2.6 collective-permute-start.37
  365.0 2.5 copy.110.refs_0_
  367.8 9.4 %collective-permute-done.35 = bf16[2,4,24,3456]{3,2,0,1:T(8,128)(2,1)S(1)} collective-permute-done((bf16[2,4,24,3456]{3,2,0,1:T(8,128)(2,1)S(1)}, bf16[2,4,24,3456]{3,2,0,1:T(8,128)(2,1)S(1)}, u32[]{:S(2)}, u32[]{:S(2)}) %collective-permute-start.35) | collective-permute-done | bytes 1327136 | tf_op jit(solution)/shard_map/ppermute | solution.py:706
  377.2 3.3 collective-permute-start.38
  386.9 5.9 %collective-permute-done.38.refs_5_ = bf16[2,24,3456]{2,1,0:T(8,128)(2,1)S(1)} collective-permute-done((bf16[2,24,3456]{2,1,0:T(8,128)(2,1)S(1)}, bf16[2,24,3456]{2,1,0:T(8,128)(2,1)S(1)}, u32[]{:S(2)}, u32[]{:S(2)}) %collective-permute-start.38) | collective-permute-done | bytes 331808 | tf_op jit(solution)/shard_map/ppermute | solution.py:706
  393.5 11.4 %qkv_grad.3 = (bf16[768,1152]{1,0:T(8,128)(2,1)}, bf16[768,1152]{1,0:T(8,128)(2,1)}, f32[416,768]{1,0:T(8,128)}, f32[8,768]{1,0:T(8,128)}) custom-call(s32[1]{0:T(128)} %bitcast.7.core_ref, bf16[416,2304]{1,0:T(8,128)(2,1)} %bitcast.333, bf16[416,768]{1,0:T(8,128)(2,1)} %get-tuple-element.104.h_ref, f32[416,768]{1,0:T(8,128)} %bitcast_convert_fusion.x_ref, ...), custom_call_target="tpu_custom_call" | custom-call | flops 48399998976 | bytes 154000000 | tf_op jit(solution)/shard_map/qkv_grad/pallas_call | solution.py:418
  413.2 3.1 fusion.1
  424.1 3.8 collective-permute-start.49
  427.9 3.1 collective-permute-done.41
  434.4 9.2 %collective-permute-done.42 = f32[2,32,768]{2,1,0:T(8,128)S(1)} collective-permute-done((f32[2,32,768]{2,1,0:T(8,128)S(1)}, f32[2,32,768]{2,1,0:T(8,128)S(1)}, u32[]{:S(2)}, u32[]{:S(2)}) %collective-permute-start.42) | collective-permute-done | bytes 196640 | tf_op jit(solution)/shard_map/ppermute | solution.py:706
  449.4 8.3 %collective-permute-done.53.refs_3_ = bf16[2,24,1152]{2,1,0:T(8,128)(2,1)S(1)} collective-permute-done((bf16[2,24,1152]{2,1,0:T(8,128)(2,1)}, bf16[2,24,1152]{2,1,0:T(8,128)(2,1)S(1)}, u32[]{:S(2)}, u32[]{:S(2)}) %collective-permute-start.53) | collective-permute-done | bytes 110624 | tf_op jit(solution)/shard_map/ppermute | solution.py:706
  457.8 7.5 %collective-permute-done.50.refs_1_ = bf16[2,24,3456]{2,1,0:T(8,128)(2,1)S(1)} collective-permute-done((bf16[2,24,3456]{2,1,0:T(8,128)(2,1)S(1)}, bf16[2,24,3456]{2,1,0:T(8,128)(2,1)S(1)}, u32[]{:S(2)}, u32[]{:S(2)}) %collective-permute-start.50) | collective-permute-done | bytes 331808 | tf_op jit(solution)/shard_map/ppermute | solution.py:706
  475.7 3.3 collective-permute-start.61
  485.4 6.0 %collective-permute-done.60 = bf16[2,24,1152]{2,1,0:T(8,128)(2,1)S(1)} collective-permute-done((bf16[2,24,1152]{2,1,0:T(8,128)(2,1)S(1)}, bf16[2,24,1152]{2,1,0:T(8,128)(2,1)S(1)}, u32[]{:S(2)}, u32[]{:S(2)}) %collective-permute-start.60) | collective-permute-done | bytes 110624 | tf_op jit(solution)/shard_map/ppermute | solution.py:706
  (364 shorter events, 120.7 us)
Async XLA Ops:
  7.2 184.7 %all-gather.2.cloned.1.call-start = ((), (), s32[]{:S(2)}) async-start(), calls=%async_computation | async-start | bytes 14598144 | tf_op jit(solution)/shard_map/all_gather | solution.py:1085
  10.1 32.1 %collective-permute-start = (bf16[2,32,128]{2,1,0:T(8,128)(2,1)}, bf16[2,32,128]{2,1,0:T(8,128)(2,1)S(1)}, u32[]{:S(2)}, u32[]{:S(2)}) collective-permute-start(bf16[2,32,128]{2,1,0:T(8,128)(2,1)} %small_own.1.refs_0_), channel_id=1, source_target_pairs={{0,2},{1,3},{2,4},{3,5},{4,6},{5,7},{6,0},{7,1},{8,10},{9,11},{10,... | collective-permute-start | bytes 49160 | tf_op jit(solution)/shard_map/ppermute | solution.py:706
  13.1 29.1 %collective-permute-start.1 = (bf16[2,32,128]{2,1,0:T(8,128)(2,1)}, bf16[2,32,128]{2,1,0:T(8,128)(2,1)S(1)}, u32[]{:S(2)}, u32[]{:S(2)}) collective-permute-start(bf16[2,32,128]{2,1,0:T(8,128)(2,1)} %small_own.1.refs_0_), channel_id=1, source_target_pairs={{0,4},{1,5},{2,6},{3,7},{4,0},{5,1},{6,2},{7,3},{8,12},{9,13},{10,... | collective-permute-start | bytes 49160 | tf_op jit(solution)/shard_map/ppermute | solution.py:706
  18.5 21.5 %collective-permute-start.8 = (bf16[2,24,1536]{2,1,0:T(8,128)(2,1)S(1)}, bf16[2,24,1536]{2,1,0:T(8,128)(2,1)S(1)}, u32[]{:S(2)}, u32[]{:S(2)}) collective-permute-start(bf16[2,24,1536]{2,1,0:T(8,128)(2,1)S(1)} %get-tuple-element.241), channel_id=1, source_target_pairs={{0,4},{1,5},{2,6},{3,7},{4,0},{5,1},{6,2},{7,3},{8,12},{9,13},{10,... | collective-permute-start | bytes 442376 | tf_op jit(solution)/shard_map/ppermute | solution.py:706
  18.7 21.3 %collective-permute-start.7 = (bf16[2,24,1536]{2,1,0:T(8,128)(2,1)S(1)}, bf16[2,24,1536]{2,1,0:T(8,128)(2,1)S(1)}, u32[]{:S(2)}, u32[]{:S(2)}) collective-permute-start(bf16[2,24,1536]{2,1,0:T(8,128)(2,1)S(1)} %get-tuple-element.241), channel_id=1, source_target_pairs={{0,2},{1,3},{2,4},{3,5},{4,6},{5,7},{6,0},{7,1},{8,10},{9,11},{10,... | collective-permute-start | bytes 442376 | tf_op jit(solution)/shard_map/ppermute | solution.py:706
  23.8 18.4 %collective-permute-start.2 = (bf16[2,32,128]{2,1,0:T(8,128)(2,1)S(1)}, bf16[2,32,128]{2,1,0:T(8,128)(2,1)S(1)}, u32[]{:S(2)}, u32[]{:S(2)}) collective-permute-start(bf16[2,32,128]{2,1,0:T(8,128)(2,1)S(1)} %copy-done.55), channel_id=1, source_target_pairs={{0,6},{1,7},{2,0},{3,1},{4,2},{5,3},{6,4},{7,5},{8,14},{9,15},{10,... | collective-permute-start | bytes 49160 | tf_op jit(solution)/shard_map/ppermute | solution.py:706
  40.1 23.7 %collective-permute-start.10 = (bf16[4,2,24,1536]{3,2,1,0:T(8,128)(2,1)S(1)}, bf16[4,2,24,1536]{3,2,1,0:T(8,128)(2,1)S(1)}, u32[]{:S(2)}, u32[]{:S(2)}) collective-permute-start(bf16[4,2,24,1536]{3,2,1,0:T(8,128)(2,1)S(1)} %pad_maximum_fusion.refs_0_), channel_id=1, source_target_pairs={{0,1},{1,0},{2,3},{3,2},{4,5},{5,4},{6,7},{7,6},{8,24},{9,25},{10,... | collective-permute-start | bytes 1769480 | tf_op jit(solution)/shard_map/ppermute | solution.py:706
  45.2 20.0 %collective-permute-start.17 = (bf16[24,3072]{1,0:T(8,128)(2,1)S(1)}, bf16[24,3072]{1,0:T(8,128)(2,1)S(1)}, u32[]{:S(2)}, u32[]{:S(2)}) collective-permute-start(bf16[24,3072]{1,0:T(8,128)(2,1)S(1)} %constant_dynamic-update-slice_fusion.4), channel_id=1, source_target_pairs={{0,8},{1,9},{2,10},{3,11},{4,12},{5,13},{6,14},{7,15},{8,0},{9,1},... | collective-permute-start | bytes 442376 | tf_op jit(solution)/shard_map/ppermute | solution.py:706
  58.1 11.7 %collective-permute-start.5 = (bf16[2,32,768]{2,1,0:T(8,128)(2,1)S(1)}, bf16[2,32,768]{2,1,0:T(8,128)(2,1)S(1)}, u32[]{:S(2)}, u32[]{:S(2)}) collective-permute-start(bf16[2,32,768]{2,1,0:T(8,128)(2,1)S(1)} %add.678), channel_id=1, source_target_pairs={{0,16},{1,17},{2,18},{3,19},{4,20},{5,21},{6,22},{7,23},{8,24},{9,... | collective-permute-start | bytes 294920 | tf_op jit(solution)/shard_map/ppermute | solution.py:706
  59.5 33.1 %collective-permute-start.11 = (bf16[4,2,24,1536]{3,2,1,0:T(8,128)(2,1)S(1)}, bf16[4,2,24,1536]{3,2,1,0:T(8,128)(2,1)S(1)}, u32[]{:S(2)}, u32[]{:S(2)}) collective-permute-start(bf16[4,2,24,1536]{3,2,1,0:T(8,128)(2,1)S(1)} %pad_maximum_fusion.refs_0_), channel_id=1, source_target_pairs={{0,16},{1,17},{2,18},{3,19},{4,20},{5,21},{6,22},{7,23},{8,9},{9,8... | collective-permute-start | bytes 1769480 | tf_op jit(solution)/shard_map/ppermute | solution.py:706
  63.8 29.4 %collective-permute-start.12 = (bf16[4,2,24,1536]{3,2,1,0:T(8,128)(2,1)S(1)}, bf16[4,2,24,1536]{3,2,1,0:T(8,128)(2,1)S(1)}, u32[]{:S(2)}, u32[]{:S(2)}) collective-permute-start(bf16[4,2,24,1536]{3,2,1,0:T(8,128)(2,1)S(1)} %collective-permute-done.10.refs_1_), channel_id=1, source_target_pairs={{0,16},{1,17},{2,18},{3,19},{4,20},{5,21},{6,22},{7,23},{8,9},{9,8... | collective-permute-start | bytes 1769480 | tf_op jit(solution)/shard_map/ppermute | solution.py:706
  65.3 15.8 %collective-permute-start.18 = (bf16[2,24,3072]{2,1,0:T(8,128)(2,1)S(1)}, bf16[2,24,3072]{2,1,0:T(8,128)(2,1)S(1)}, u32[]{:S(2)}, u32[]{:S(2)}) collective-permute-start(bf16[2,24,3072]{2,1,0:T(8,128)(2,1)S(1)} %get-tuple-element.231), channel_id=1, source_target_pairs={{0,2},{1,3},{2,4},{3,5},{4,6},{5,7},{6,0},{7,1},{8,10},{9,11},{10,... | collective-permute-start | bytes 884744 | tf_op jit(solution)/shard_map/ppermute | solution.py:706
  66.5 26.1 %collective-permute-start.19 = (bf16[2,24,3072]{2,1,0:T(8,128)(2,1)S(1)}, bf16[2,24,3072]{2,1,0:T(8,128)(2,1)S(1)}, u32[]{:S(2)}, u32[]{:S(2)}) collective-permute-start(bf16[2,24,3072]{2,1,0:T(8,128)(2,1)S(1)} %get-tuple-element.231), channel_id=1, source_target_pairs={{0,6},{1,7},{2,0},{3,1},{4,2},{5,3},{6,4},{7,5},{8,14},{9,15},{10,... | collective-permute-start | bytes 884744 | tf_op jit(solution)/shard_map/ppermute | solution.py:706
  69.9 33.8 %collective-permute-start.13 = (bf16[4,2,24,1536]{3,2,1,0:T(8,128)(2,1)S(1)}, bf16[4,2,24,1536]{3,2,1,0:T(8,128)(2,1)S(1)}, u32[]{:S(2)}, u32[]{:S(2)}) collective-permute-start(bf16[4,2,24,1536]{3,2,1,0:T(8,128)(2,1)S(1)} %pad_maximum_fusion.refs_0_), channel_id=1, source_target_pairs={{0,8},{1,9},{2,10},{3,11},{4,12},{5,13},{6,14},{7,15},{8,0},{9,1},... | collective-permute-start | bytes 1769480 | tf_op jit(solution)/shard_map/ppermute | solution.py:706
  81.0 32.7 %collective-permute-start.20 = (bf16[2,24,3072]{2,1,0:T(8,128)(2,1)S(1)}, bf16[2,24,3072]{2,1,0:T(8,128)(2,1)S(1)}, u32[]{:S(2)}, u32[]{:S(2)}) collective-permute-start(bf16[2,24,3072]{2,1,0:T(8,128)(2,1)S(1)} %get-tuple-element.231), channel_id=1, source_target_pairs={{0,4},{1,5},{2,6},{3,7},{4,0},{5,1},{6,2},{7,3},{8,12},{9,13},{10,... | collective-permute-start | bytes 884744 | tf_op jit(solution)/shard_map/ppermute | solution.py:706
  114.0 33.1 %collective-permute-start.21 = (bf16[4,2,24,3072]{3,2,1,0:T(8,128)(2,1)S(1)}, bf16[4,2,24,3072]{3,2,1,0:T(8,128)(2,1)}, u32[]{:S(2)}, u32[]{:S(2)}) collective-permute-start(bf16[4,2,24,3072]{3,2,1,0:T(8,128)(2,1)S(1)} %maximum_add_fusion.refs_0_), channel_id=1, source_target_pairs={{0,1},{1,0},{2,3},{3,2},{4,5},{5,4},{6,7},{7,6},{8,24},{9,25},{10,... | collective-permute-start | bytes 3538952 | tf_op jit(solution)/shard_map/ppermute | solution.py:706
  115.6 34.9 %collective-permute-start.22 = (bf16[4,2,24,3072]{3,2,1,0:T(8,128)(2,1)S(1)}, bf16[4,2,24,3072]{3,2,1,0:T(8,128)(2,1)}, u32[]{:S(2)}, u32[]{:S(2)}) collective-permute-start(bf16[4,2,24,3072]{3,2,1,0:T(8,128)(2,1)S(1)} %maximum_add_fusion.refs_0_), channel_id=1, source_target_pairs={{0,16},{1,17},{2,18},{3,19},{4,20},{5,21},{6,22},{7,23},{8,9},{9,8... | collective-permute-start | bytes 3538952 | tf_op jit(solution)/shard_map/ppermute | solution.py:706
  148.5 16.4 %collective-permute-start.23 = (bf16[4,2,24,3072]{3,2,1,0:T(8,128)(2,1)S(1)}, bf16[4,2,24,3072]{3,2,1,0:T(8,128)(2,1)}, u32[]{:S(2)}, u32[]{:S(2)}) collective-permute-start(bf16[4,2,24,3072]{3,2,1,0:T(8,128)(2,1)S(1)} %broadcast_add_fusion), channel_id=1, source_target_pairs={{0,16},{1,17},{2,18},{3,19},{4,20},{5,21},{6,22},{7,23},{8,9},{9,8... | collective-permute-start | bytes 3538952 | tf_op jit(solution)/shard_map/ppermute | solution.py:706
  150.0 17.6 %collective-permute-start.24 = (bf16[4,2,24,3072]{3,2,1,0:T(8,128)(2,1)S(1)}, bf16[4,2,24,3072]{3,2,1,0:T(8,128)(2,1)}, u32[]{:S(2)}, u32[]{:S(2)}) collective-permute-start(bf16[4,2,24,3072]{3,2,1,0:T(8,128)(2,1)S(1)} %maximum_add_fusion.refs_0_), channel_id=1, source_target_pairs={{0,8},{1,9},{2,10},{3,11},{4,12},{5,13},{6,14},{7,15},{8,0},{9,1},... | collective-permute-start | bytes 3538952 | tf_op jit(solution)/shard_map/ppermute | solution.py:706
  150.0 17.6 %collective-permute-start.25 = (bf16[4,2,24,3072]{3,2,1,0:T(8,128)(2,1)}, bf16[4,2,24,3072]{3,2,1,0:T(8,128)(2,1)}, u32[]{:S(2)}, u32[]{:S(2)}) collective-permute-start(bf16[4,2,24,3072]{3,2,1,0:T(8,128)(2,1)} %collective-permute-done.21.refs_1_), channel_id=1, source_target_pairs={{0,8},{1,9},{2,10},{3,11},{4,12},{5,13},{6,14},{7,15},{8,0},{9,1},... | collective-permute-start | bytes 3538952 | tf_op jit(solution)/shard_map/ppermute | solution.py:706
  150.5 17.1 %collective-permute-start.26 = (bf16[4,2,24,3072]{3,2,1,0:T(8,128)(2,1)}, bf16[4,2,24,3072]{3,2,1,0:T(8,128)(2,1)}, u32[]{:S(2)}, u32[]{:S(2)}) collective-permute-start(bf16[4,2,24,3072]{3,2,1,0:T(8,128)(2,1)} %collective-permute-done.22.refs_2_), channel_id=1, source_target_pairs={{0,8},{1,9},{2,10},{3,11},{4,12},{5,13},{6,14},{7,15},{8,0},{9,1},... | collective-permute-start | bytes 3538952 | tf_op jit(solution)/shard_map/ppermute | solution.py:706
  248.7 23.0 %collective-permute-start.28 = (bf16[768,3456]{1,0:T(8,128)(2,1)}, bf16[768,3456]{1,0:T(8,128)(2,1)S(1)}, u32[]{:S(2)}, u32[]{:S(2)}) collective-permute-start(bf16[768,3456]{1,0:T(8,128)(2,1)} %get-tuple-element.92), channel_id=1, source_target_pairs={{0,8},{1,9},{2,10},{3,11},{4,12},{5,13},{6,14},{7,15},{8,0},{9,1},... | collective-permute-start | bytes 15925256 | tf_op jit(solution)/shard_map/ppermute | solution.py:706
  274.8 17.8 %collective-permute-start.29 = (bf16[2,4,24,3456]{3,2,0,1:T(8,128)(2,1)S(1)}, bf16[2,4,24,3456]{3,2,0,1:T(8,128)(2,1)S(1)}, u32[]{:S(2)}, u32[]{:S(2)}) collective-permute-start(bf16[2,4,24,3456]{3,2,0,1:T(8,128)(2,1)S(1)} %fusion.4), channel_id=1, source_target_pairs={{0,16},{1,17},{2,18},{3,19},{4,20},{5,21},{6,22},{7,23},{8,9},{9,8... | collective-permute-start | bytes 3981320 | tf_op jit(solution)/shard_map/ppermute | solution.py:706
  277.7 39.5 %collective-permute-start.30 = (bf16[2,4,24,3456]{3,2,0,1:T(8,128)(2,1)}, bf16[2,4,24,3456]{3,2,0,1:T(8,128)(2,1)}, u32[]{:S(2)}, u32[]{:S(2)}) collective-permute-start(bf16[2,4,24,3456]{3,2,0,1:T(8,128)(2,1)} %fusion.5), channel_id=1, source_target_pairs={{0,16},{1,17},{2,18},{3,19},{4,20},{5,21},{6,22},{7,23},{8,9},{9,8... | collective-permute-start | bytes 3981320 | tf_op jit(solution)/shard_map/ppermute | solution.py:706
  289.8 34.2 %collective-permute-start.31 = (bf16[768,1152]{1,0:T(8,128)(2,1)}, bf16[768,1152]{1,0:T(8,128)(2,1)}, u32[]{:S(2)}, u32[]{:S(2)}) collective-permute-start(bf16[768,1152]{1,0:T(8,128)(2,1)} %get-tuple-element.102), channel_id=1, source_target_pairs={{0,8},{1,9},{2,10},{3,11},{4,12},{5,13},{6,14},{7,15},{8,0},{9,1},... | collective-permute-start | bytes 5308424 | tf_op jit(solution)/shard_map/ppermute | solution.py:706
  294.2 60.1 %collective-permute-start.32 = (bf16[2,4,24,3456]{3,2,0,1:T(8,128)(2,1)}, bf16[2,4,24,3456]{3,2,0,1:T(8,128)(2,1)}, u32[]{:S(2)}, u32[]{:S(2)}) collective-permute-start(bf16[2,4,24,3456]{3,2,0,1:T(8,128)(2,1)} %fusion.3), channel_id=1, source_target_pairs={{0,1},{1,0},{2,3},{3,2},{4,5},{5,4},{6,7},{7,6},{8,24},{9,25},{10,... | collective-permute-start | bytes 3981320 | tf_op jit(solution)/shard_map/ppermute | solution.py:706
  316.4 40.3 %collective-permute-start.34 = (bf16[768,3456]{1,0:T(8,128)(2,1)}, bf16[768,3456]{1,0:T(8,128)(2,1)S(1)}, u32[]{:S(2)}, u32[]{:S(2)}) collective-permute-start(bf16[768,3456]{1,0:T(8,128)(2,1)} %get-tuple-element.108), channel_id=1, source_target_pairs={{0,8},{1,9},{2,10},{3,11},{4,12},{5,13},{6,14},{7,15},{8,0},{9,1},... | collective-permute-start | bytes 15925256 | tf_op jit(solution)/shard_map/ppermute | solution.py:706
  327.4 22.2 %collective-permute-start.33 = (bf16[2,4,24,1152]{3,2,0,1:T(8,128)(2,1)}, bf16[2,4,24,1152]{3,2,0,1:T(8,128)(2,1)}, u32[]{:S(2)}, u32[]{:S(2)}) collective-permute-start(bf16[2,4,24,1152]{3,2,0,1:T(8,128)(2,1)} %fusion.16), channel_id=1, source_target_pairs={{0,16},{1,17},{2,18},{3,19},{4,20},{5,21},{6,22},{7,23},{8,9},{9,8... | collective-permute-start | bytes 1327112 | tf_op jit(solution)/shard_map/ppermute | solution.py:706
  348.6 56.4 %collective-permute-start.51 = (bf16[2,4,24,1152]{3,2,0,1:T(8,128)(2,1)}, bf16[2,4,24,1152]{3,2,0,1:T(8,128)(2,1)}, u32[]{:S(2)}, u32[]{:S(2)}) collective-permute-start(bf16[2,4,24,1152]{3,2,0,1:T(8,128)(2,1)} %fusion.19), channel_id=1, source_target_pairs={{0,16},{1,17},{2,18},{3,19},{4,20},{5,21},{6,22},{7,23},{8,9},{9,8... | collective-permute-start | bytes 1327112 | tf_op jit(solution)/shard_map/ppermute | solution.py:706
  351.8 53.2 %collective-permute-start.45 = (bf16[2,4,24,1152]{3,2,0,1:T(8,128)(2,1)}, bf16[2,4,24,1152]{3,2,0,1:T(8,128)(2,1)}, u32[]{:S(2)}, u32[]{:S(2)}) collective-permute-start(bf16[2,4,24,1152]{3,2,0,1:T(8,128)(2,1)} %fusion.11), channel_id=1, source_target_pairs={{0,1},{1,0},{2,3},{3,2},{4,5},{5,4},{6,7},{7,6},{8,24},{9,25},{10,... | collective-permute-start | bytes 1327112 | tf_op jit(solution)/shard_map/ppermute | solution.py:706
  359.3 17.8 %collective-permute-start.35 = (bf16[2,4,24,3456]{3,2,0,1:T(8,128)(2,1)S(1)}, bf16[2,4,24,3456]{3,2,0,1:T(8,128)(2,1)S(1)}, u32[]{:S(2)}, u32[]{:S(2)}) collective-permute-start(bf16[2,4,24,3456]{3,2,0,1:T(8,128)(2,1)S(1)} %fusion.6), channel_id=1, source_target_pairs={{0,16},{1,17},{2,18},{3,19},{4,20},{5,21},{6,22},{7,23},{8,9},{9,8... | collective-permute-start | bytes 3981320 | tf_op jit(solution)/shard_map/ppermute | solution.py:706
  361.0 22.3 %collective-permute-start.36 = (bf16[2,24,3456]{2,1,0:T(8,128)(2,1)S(1)}, bf16[2,24,3456]{2,1,0:T(8,128)(2,1)S(1)}, u32[]{:S(2)}, u32[]{:S(2)}) collective-permute-start(bf16[2,24,3456]{2,1,0:T(8,128)(2,1)S(1)} %get-tuple-element.199), channel_id=1, source_target_pairs={{0,2},{1,3},{2,4},{3,5},{4,6},{5,7},{6,0},{7,1},{8,10},{9,11},{10,... | collective-permute-start | bytes 995336 | tf_op jit(solution)/shard_map/ppermute | solution.py:706
  362.4 23.9 %collective-permute-start.37 = (bf16[2,24,3456]{2,1,0:T(8,128)(2,1)S(1)}, bf16[2,24,3456]{2,1,0:T(8,128)(2,1)S(1)}, u32[]{:S(2)}, u32[]{:S(2)}) collective-permute-start(bf16[2,24,3456]{2,1,0:T(8,128)(2,1)S(1)} %get-tuple-element.198), channel_id=1, source_target_pairs={{0,4},{1,5},{2,6},{3,7},{4,0},{5,1},{6,2},{7,3},{8,12},{9,13},{10,... | collective-permute-start | bytes 995336 | tf_op jit(solution)/shard_map/ppermute | solution.py:706
  377.2 15.5 %collective-permute-start.38 = (bf16[2,24,3456]{2,1,0:T(8,128)(2,1)S(1)}, bf16[2,24,3456]{2,1,0:T(8,128)(2,1)S(1)}, u32[]{:S(2)}, u32[]{:S(2)}) collective-permute-start(bf16[2,24,3456]{2,1,0:T(8,128)(2,1)S(1)} %get-tuple-element.197), channel_id=1, source_target_pairs={{0,6},{1,7},{2,0},{3,1},{4,2},{5,3},{6,4},{7,5},{8,14},{9,15},{10,... | collective-permute-start | bytes 995336 | tf_op jit(solution)/shard_map/ppermute | solution.py:706
  383.3 29.9 %collective-permute-start.46 = (bf16[2,4,24,3456]{3,2,0,1:T(8,128)(2,1)S(1)}, bf16[2,4,24,3456]{3,2,0,1:T(8,128)(2,1)}, u32[]{:S(2)}, u32[]{:S(2)}) collective-permute-start(bf16[2,4,24,3456]{3,2,0,1:T(8,128)(2,1)S(1)} %fusion.7), channel_id=1, source_target_pairs={{0,16},{1,17},{2,18},{3,19},{4,20},{5,21},{6,22},{7,23},{8,9},{9,8... | collective-permute-start | bytes 3981320 | tf_op jit(solution)/shard_map/ppermute | solution.py:706
  386.3 26.9 %collective-permute-start.47 = (bf16[2,4,24,3456]{3,2,0,1:T(8,128)(2,1)}, bf16[2,4,24,3456]{3,2,0,1:T(8,128)(2,1)}, u32[]{:S(2)}, u32[]{:S(2)}) collective-permute-start(bf16[2,4,24,3456]{3,2,0,1:T(8,128)(2,1)} %fusion), channel_id=1, source_target_pairs={{0,1},{1,0},{2,3},{3,2},{4,5},{5,4},{6,7},{7,6},{8,24},{9,25},{10,... | collective-permute-start | bytes 3981320 | tf_op jit(solution)/shard_map/ppermute | solution.py:706
  407.1 42.3 %collective-permute-start.52 = (bf16[2,24,1152]{2,1,0:T(8,128)(2,1)}, bf16[2,24,1152]{2,1,0:T(8,128)(2,1)}, u32[]{:S(2)}, u32[]{:S(2)}) collective-permute-start(bf16[2,24,1152]{2,1,0:T(8,128)(2,1)} %get-tuple-element.217), channel_id=1, source_target_pairs={{0,2},{1,3},{2,4},{3,5},{4,6},{5,7},{6,0},{7,1},{8,10},{9,11},{10,... | collective-permute-start | bytes 331784 | tf_op jit(solution)/shard_map/ppermute | solution.py:706
  424.0 20.2 %collective-permute-start.48 = (bf16[2,24,3456]{2,1,0:T(8,128)(2,1)S(1)}, bf16[2,24,3456]{2,1,0:T(8,128)(2,1)S(1)}, u32[]{:S(2)}, u32[]{:S(2)}) collective-permute-start(bf16[2,24,3456]{2,1,0:T(8,128)(2,1)S(1)} %get-tuple-element.196), channel_id=1, source_target_pairs={{0,2},{1,3},{2,4},{3,5},{4,6},{5,7},{6,0},{7,1},{8,10},{9,11},{10,... | collective-permute-start | bytes 995336 | tf_op jit(solution)/shard_map/ppermute | solution.py:706
  424.1 21.2 %collective-permute-start.49 = (bf16[2,24,3456]{2,1,0:T(8,128)(2,1)S(1)}, bf16[2,24,3456]{2,1,0:T(8,128)(2,1)S(1)}, u32[]{:S(2)}, u32[]{:S(2)}) collective-permute-start(bf16[2,24,3456]{2,1,0:T(8,128)(2,1)S(1)} %get-tuple-element.195), channel_id=1, source_target_pairs={{0,6},{1,7},{2,0},{3,1},{4,2},{5,3},{6,4},{7,5},{8,14},{9,15},{10,... | collective-permute-start | bytes 995336 | tf_op jit(solution)/shard_map/ppermute | solution.py:706
  431.0 16.2 %collective-permute-start.44 = (bf16[2,4,24,1152]{3,2,1,0:T(8,128)(2,1)S(1)}, bf16[2,4,24,1152]{3,2,1,0:T(8,128)(2,1)S(1)}, u32[]{:S(2)}, u32[]{:S(2)}) collective-permute-start(bf16[2,4,24,1152]{3,2,1,0:T(8,128)(2,1)S(1)} %get-tuple-element.192), channel_id=1, source_target_pairs={{0,16},{1,17},{2,18},{3,19},{4,20},{5,21},{6,22},{7,23},{8,9},{9,8... | collective-permute-start | bytes 1327112 | tf_op jit(solution)/shard_map/ppermute | solution.py:706
  431.6 11.9 %collective-permute-start.42 = (f32[2,32,768]{2,1,0:T(8,128)S(1)}, f32[2,32,768]{2,1,0:T(8,128)S(1)}, u32[]{:S(2)}, u32[]{:S(2)}) collective-permute-start(f32[2,32,768]{2,1,0:T(8,128)S(1)} %add.749), channel_id=1, source_target_pairs={{0,16},{1,17},{2,18},{3,19},{4,20},{5,21},{6,22},{7,23},{8,24},{9,... | collective-permute-start | bytes 589832 | tf_op jit(solution)/shard_map/ppermute | solution.py:706
  443.5 14.2 %collective-permute-start.53 = (bf16[2,24,1152]{2,1,0:T(8,128)(2,1)}, bf16[2,24,1152]{2,1,0:T(8,128)(2,1)S(1)}, u32[]{:S(2)}, u32[]{:S(2)}) collective-permute-start(bf16[2,24,1152]{2,1,0:T(8,128)(2,1)} %get-tuple-element.216), channel_id=1, source_target_pairs={{0,4},{1,5},{2,6},{3,7},{4,0},{5,1},{6,2},{7,3},{8,12},{9,13},{10,... | collective-permute-start | bytes 331784 | tf_op jit(solution)/shard_map/ppermute | solution.py:706
  444.2 13.5 %collective-permute-start.54 = (bf16[2,24,1152]{2,1,0:T(8,128)(2,1)}, bf16[2,24,1152]{2,1,0:T(8,128)(2,1)S(1)}, u32[]{:S(2)}, u32[]{:S(2)}) collective-permute-start(bf16[2,24,1152]{2,1,0:T(8,128)(2,1)} %get-tuple-element.215), channel_id=1, source_target_pairs={{0,6},{1,7},{2,0},{3,1},{4,2},{5,3},{6,4},{7,5},{8,14},{9,15},{10,... | collective-permute-start | bytes 331784 | tf_op jit(solution)/shard_map/ppermute | solution.py:706
  445.3 20.0 %collective-permute-start.50 = (bf16[2,24,3456]{2,1,0:T(8,128)(2,1)S(1)}, bf16[2,24,3456]{2,1,0:T(8,128)(2,1)S(1)}, u32[]{:S(2)}, u32[]{:S(2)}) collective-permute-start(bf16[2,24,3456]{2,1,0:T(8,128)(2,1)S(1)} %get-tuple-element.194), channel_id=1, source_target_pairs={{0,4},{1,5},{2,6},{3,7},{4,0},{5,1},{6,2},{7,3},{8,12},{9,13},{10,... | collective-permute-start | bytes 995336 | tf_op jit(solution)/shard_map/ppermute | solution.py:706
  447.3 18.0 %collective-permute-start.55 = (bf16[2,4,24,1152]{3,2,1,0:T(8,128)(2,1)S(1)}, bf16[2,4,24,1152]{3,2,1,0:T(8,128)(2,1)S(1)}, u32[]{:S(2)}, u32[]{:S(2)}) collective-permute-start(bf16[2,4,24,1152]{3,2,1,0:T(8,128)(2,1)S(1)} %fusion.9), channel_id=1, source_target_pairs={{0,1},{1,0},{2,3},{3,2},{4,5},{5,4},{6,7},{7,6},{8,24},{9,25},{10,... | collective-permute-start | bytes 1327112 | tf_op jit(solution)/shard_map/ppermute | solution.py:706
  468.7 11.9 %collective-permute-start.58 = (f32[2,32,128]{2,1,0:T(8,128)}, f32[2,32,128]{2,1,0:T(8,128)}, u32[]{:S(2)}, u32[]{:S(2)}) collective-permute-start(f32[2,32,128]{2,1,0:T(8,128)} %get-tuple-element.121), channel_id=1, source_target_pairs={{0,6},{1,7},{2,0},{3,1},{4,2},{5,3},{6,4},{7,5},{8,14},{9,15},{10,... | collective-permute-start | bytes 98312 | tf_op jit(solution)/shard_map/ppermute | solution.py:706
  470.2 12.0 %collective-permute-start.56 = (f32[2,32,128]{2,1,0:T(8,128)}, f32[2,32,128]{2,1,0:T(8,128)}, u32[]{:S(2)}, u32[]{:S(2)}) collective-permute-start(f32[2,32,128]{2,1,0:T(8,128)} %get-tuple-element.119), channel_id=1, source_target_pairs={{0,2},{1,3},{2,4},{3,5},{4,6},{5,7},{6,0},{7,1},{8,10},{9,11},{10,... | collective-permute-start | bytes 98312 | tf_op jit(solution)/shard_map/ppermute | solution.py:706
  482.2 11.7 %collective-permute-start.64 = (f32[24,3456]{1,0:T(8,128)S(1)}, f32[24,3456]{1,0:T(8,128)S(1)}, u32[]{:S(2)}, u32[]{:S(2)}) collective-permute-start(f32[24,3456]{1,0:T(8,128)S(1)} %dynamic-slice_bitcast_fusion.1), channel_id=1, source_target_pairs={{0,8},{1,9},{2,10},{3,11},{4,12},{5,13},{6,14},{7,15},{8,0},{9,1},... | collective-permute-start | bytes 995336 | tf_op jit(solution)/shard_map/ppermute | solution.py:706
  (81 other events, 548.2 us)
Sparse Core Ops, SparseCore 0:
  16.9 130.1 all-gather.1

commit v4 on v3

--- a/solution.py
+++ b/solution.py
@@ -799,10 +799,12 @@
     )(pos, *own, *other, *after)
 
 
-def sum_plane(v):
-    for pairs in (CORE_SWAP, X_SWAP, Y_SWAP):
-        v = v + send(v, pairs)
-    return v
+def sum_plane(v, behind=()):
+    v = v + send(v, CORE_SWAP)
+    v = v + send(v, X_SWAP)
+    if behind:
+        v = v + no_sooner(behind).astype(v.dtype)
+    return v + send(v, Y_SWAP)
 
 
 class Reduction:
@@ -825,9 +827,10 @@
             v = v.reshape(self.split + (v.shape[-1],))
             at = ((self.y + fy) % CHIP_Y, 0, 0, (self.x + fx) % CHIP_X, 0, 0)
             size = (1, CORES, CHIP_Z, 1) + v.shape[4:]
-            return lax.dynamic_slice(v, at, size)[0, :, :, 0].astype(F32)
-
-        return cut(self.own) + cut(self.got)
+            return lax.dynamic_slice(v, at, size)[0, :, :, 0].transpose(1, 0, 2, 3).astype(F32)
+
+        own, got = lax.optimization_barrier((self.own, self.got))
+        return cut(own) + cut(got)
 
     def far(self):
         self.r3 = send(self.part(1, 1).astype(B16), PLANE[1])
@@ -845,7 +848,7 @@
         base = self.part(0, 0) + self.r2.astype(F32) + self.r1.astype(F32)
 
         def at_z(k):
-            return lax.dynamic_slice_in_dim(base, (self.z + k) % CHIP_Z, 1, axis=1)[:, 0]
+            return lax.dynamic_slice_in_dim(base, (self.z + k) % CHIP_Z, 1, axis=0)[0]
 
         self.mine = at_z(0)
         self.rz = [send(at_z(k).astype(B16), Z_SHIFT[k]) for k in range(1, CHIP_Z)]
@@ -891,23 +894,6 @@
         cost_estimate=cost(5),
         name="unpack",
     )(packed, *after)
-
-
-def fence_kernel(last_ref, *refs):
-    refs[-1][...] = last_ref[...]
-
-
-def fence(last, after):
-    whole = pl.BlockSpec(memory_space=pltpu.VMEM)
-    return pl.pallas_call(
-        fence_kernel,
-        out_shape=jax.ShapeDtypeStruct(last.shape, F32),
-        in_specs=[whole] + [ANY] * len(after),
-        out_specs=whole,
-        compiler_params=params(),
-        cost_estimate=cost(25),
-        name="fence",
-    )(last, *after)
 
 
 def small_offsets(own, entries, device):
@@ -1194,30 +1180,30 @@
             return a1.side() + b1.swap()
 
         def zero_qkv():
-            for layer in range(LAYERS):
-                tables[layer] = reduce_bias(tables[layer])
-            moved = a1.near() + b1.far() + a0.far()
-            a1.along()
-            return moved + a1.rz + [tables[0], tables[1]]
+            return a1.near() + b1.far() + a0.far()
 
         grad, _, rest = backward(0, grad, (zero_mlp, zero_attention, zero_qkv))
         b0 = Reduction(*rest)
+        moved = a1.along()
         a0.side()
         a0.near()
         b1.side()
         b0.swap()
+        b0.far()
+        b0.side()
+        tables[1] = reduce_bias(tables[1], [small_grads[0][0]] + moved)
+        tables[0] = reduce_bias(tables[0], [tables[1], a0.r1] + b1.near())
+        a0.along()
+        b1.along()
 
     parts = []
     for (qkv_sums, mlp_sums), table in zip(small_grads, tables):
         parts += [qkv_sums, mlp_sums, table]
-    totals = pack_small(parts, [b0.got] if fast else ())
-    totals = sum_plane(totals) if fast else lax.psum(totals, AXES)
+    totals = pack_small(parts, [b0.r3, b0.r2, a0.rz[0]] if fast else ())
+    totals = sum_plane(totals, a0.rz) if fast else lax.psum(totals, AXES)
     late = ()
     if fast:
-        b1.near()
-        a0.along()
-        gate = fence(small_grads[0][0], b0.far() + b0.side() + [b1.r1, a0.rz[0], a0.rz[2], totals])
-        late = [gate, a0.rz[1]] + b1.along() + b0.near()
+        late = b0.near() + b1.rz
     pieces = collect(totals, ahead, own, entries, late)
     if fast:
         b0.along()

time: 508 us -> 488 us (0.961)
  waiting for transfers between devices: 122 us -> 113 us
  other arithmetic: 37.5 us -> 31.3 us
  local copies, waits for them, and re-layouts: 49.5 us -> 43.5 us
    ppermute x6 -> x0, local copies, waits for them, and re-layouts: 10.9 us -> none  [send(): return lax.ppermute(v, AXES, pairs)]
    ppermute x66, waiting for transfers between devices: 122 us -> 113 us  [send(): return lax.ppermute(v, AXES, pairs)]
    dynamic_slice x6 -> x7, local copies, waits for them, and re-layouts: 17.3 us -> 11 us  [cut(): lax.dynamic_slice(v, at, size)[0, :, :, 0].transpose(1, 0, 2, 3).astype(F32)]
    unnamed x140 -> x122, local copies, waits for them, and re-layouts: 10.8 us -> 13.9 us
  transfers between devices with their start and end apart: 67 -> 67, of which waited for: 19 -> 18; matrix products, arithmetic and copies ran while one was open for 14% -> 10% of each run, Pallas kernels for 27% -> 29%
where the time goes in v4:
time: 488 us; the launch traced here: 484 us
  Pallas kernels  195 us (40%)
  waiting for transfers between devices  113 us (23%)
  starting transfers between devices  79.4 us (16%)
  local copies, waits for them, and re-layouts  43.5 us (9%)
  other arithmetic  31.3 us (6%)
  between operations  21.9 us (4%)
    ppermute x66, waiting for transfers between devices, send(): return lax.ppermute(v, AXES, pairs)  113 us
    ppermute x66, starting transfers between devices, send(): return lax.ppermute(v, AXES, pairs)  79.3 us
    pallas_call x2, Pallas kernels, mlp_backward(): pl.pallas_call(mlp_grad_kernel, grid=(hidden // TILE,), out_shape=(jax.Sh...  40.8 us
    pallas_call x2, Pallas kernels, mlp_forward(): pl.pallas_call(mlp_kernel, grid=(hidden // TILE,), out_shape=(full, full,...  31 us
    pallas_call x2, Pallas kernels, attention_backward(): pl.pallas_call(functools.partial(attention_grad_kernel, width), grid=(ima...  23.7 us
    pallas_call x2, Pallas kernels, qkv_backward(): pl.pallas_call(qkv_grad_kernel, grid=(3,), out_shape=(jax.ShapeDtypeStruc...  22.6 us
    pallas_call x2, Pallas kernels, attention_forward(): pl.pallas_call(functools.partial(attention_kernel, width), grid=(images,)...  16.7 us
    unnamed x122, local copies, waits for them, and re-layouts  13.9 us
  transfers between devices with their start and end apart: 67, of which 18 were waited for; matrix products, arithmetic and copies ran while one was open for 10% of the time, Pallas kernels for 29%

profile of v4, /device:TPU:0, one launch (start us, length us, event | category | flops | bytes accessed | tf_op | source)
XLA Modules:
  0.0 484.0 jit_solution(8492768453311484613)
XLA Ops:
  10.1 3.0 collective-permute-start
  13.1 2.6 collective-permute-start.1
  20.1 3.7 collective-permute-done.9
  23.8 3.3 collective-permute-start.2
  27.1 12.9 %collective-permute-done.8 = bf16[2,24,1536]{2,1,0:T(8,128)(2,1)S(1)} collective-permute-done((bf16[2,24,1536]{2,1,0:T(8,128)(2,1)S(1)}, bf16[2,24,1536]{2,1,0:T(8,128)(2,1)S(1)}, u32[]{:S(2)}, u32[]{:S(2)}) %collective-permute-start.8) | collective-permute-done | bytes 147488 | tf_op jit(solution)/shard_map/ppermute | solution.py:706
  40.1 2.0 collective-permute-start.10
  48.0 10.1 %collective-permute-done.4 = bf16[2,32,768]{2,1,0:T(8,128)(2,1)S(1)} collective-permute-done((bf16[2,32,768]{2,1,0:T(8,128)(2,1)S(1)}, bf16[2,32,768]{2,1,0:T(8,128)(2,1)S(1)}, u32[]{:S(2)}, u32[]{:S(2)}) %collective-permute-start.4) | collective-permute-done | bytes 98336 | tf_op jit(solution)/shard_map/ppermute | solution.py:706
  66.5 2.8 collective-permute-start.19
  70.6 10.5 %collective-permute-done.18.refs_0_ = bf16[2,24,3072]{2,1,0:T(8,128)(2,1)S(1)} collective-permute-done((bf16[2,24,3072]{2,1,0:T(8,128)(2,1)S(1)}, bf16[2,24,3072]{2,1,0:T(8,128)(2,1)S(1)}, u32[]{:S(2)}, u32[]{:S(2)}) %collective-permute-start.18) | collective-permute-done | bytes 294944 | tf_op jit(solution)/shard_map/ppermute | solution.py:706
  81.0 11.6 %collective-permute-start.20 = (bf16[2,24,3072]{2,1,0:T(8,128)(2,1)S(1)}, bf16[2,24,3072]{2,1,0:T(8,128)(2,1)S(1)}, u32[]{:S(2)}, u32[]{:S(2)}) collective-permute-start(bf16[2,24,3072]{2,1,0:T(8,128)(2,1)S(1)} %get-tuple-element.253), channel_id=1, source_target_pairs={{0,4},{1,5},{2,6},{3,7},{4,0},{5,1},{6,2},{7,3},{8,12},{9,13},{10,... | collective-permute-start | bytes 884744 | tf_op jit(solution)/shard_map/ppermute | solution.py:706
  93.4 10.3 %bias_expand.1.refs_8_.bias_ref = f32[24,208,256]{2,1,0:T(8,128)} custom-call(f32[2,32,768]{2,1,0:T(8,128)} %add_convert_fusion.8.small_ref, bf16[208,224]{1,0:T(8,128)(2,1)} %constant.392.clone.rows_ref, bf16[384,256]{1,0:T(8,128)(2,1)} %constant.393.clone.lanes_ref, bf16[2,24,3072]{2,1,0:T(8,128)(2,1)} %copy-done.24, bf16[2,24,3072]{2,1,0:T(8,128)(2,1)} %copy-done.26), custom_call_target="tpu_custom_call" | custom-call | flops 44000002048 | bytes 140000000 | tf_op jit(solution)/shard_map/bias_expand/pallas_call | solution.py:99
  105.8 5.3 %assemble.2 = (bf16[32,1,24,2304]{3,2,1,0:T(8,128)(2,1)}, bf16[32,1,24,768]{3,2,1,0:T(8,128)(2,1)}) custom-call(s32[4]{0:T(128)} %pad_add_fusion.1.pos_ref, bf16[4,2,24,1536]{3,2,1,0:T(8,128)(2,1)} %copy-done.17, bf16[4,2,24,1536]{3,2,1,0:T(8,128)(2,1)} %copy-done.35, bf16[4,2,24,1536]{3,2,1,0:T(8,128)(2,1)} %copy-done.36, ...), custom_call_target="tpu_custom_call" | custom-call | flops 30799998976 | bytes 98000000 | tf_op jit(solution)/shard_map/assemble/pallas_call | solution.py:790
  116.6 5.9 %qkv.2 = (bf16[416,2304]{1,0:T(8,128)(2,1)}, bf16[416,768]{1,0:T(8,128)(2,1)}) custom-call(f32[416,768]{1,0:T(8,128)} %bitcast_convert_fusion.x_ref, f32[2,32,768]{2,1,0:T(8,128)} %add_convert_fusion.8.small_ref, bf16[768,2304]{1,0:T(8,128)(2,1)} %bitcast.332), custom_call_target="tpu_custom_call" | custom-call | flops 26400000000 | bytes 84000000 | tf_op jit(solution)/shard_map/qkv/pallas_call | solution.py:350
  122.5 8.3 %attention.2 = (bf16[2,208,768]{2,1,0:T(8,128)(2,1)}, f32[2,16,256]{2,1,0:T(8,128)}) custom-call(bf16[2,208,2304]{2,1,0:T(8,128)(2,1)} %bitcast.343, f32[24,208,256]{2,1,0:T(8,128)} %bias_expand.1.refs_8_.bias_ref), custom_call_target="tpu_custom_call" | custom-call | flops 35200000000 | bytes 112000000 | tf_op jit(solution)/shard_map/attention/pallas_call | solution.py:203
  132.7 14.3 %collective-permute-done.21.refs_1_ = bf16[4,2,24,3072]{3,2,1,0:T(8,128)(2,1)} collective-permute-done((bf16[4,2,24,3072]{3,2,1,0:T(8,128)(2,1)S(1)}, bf16[4,2,24,3072]{3,2,1,0:T(8,128)(2,1)}, u32[]{:S(2)}, u32[]{:S(2)}) %collective-permute-start.21) | collective-permute-done | bytes 1179680 | tf_op jit(solution)/shard_map/ppermute | solution.py:706
  150.5 14.3 %collective-permute-done.23.refs_3_ = bf16[4,2,24,3072]{3,2,1,0:T(8,128)(2,1)} collective-permute-done((bf16[4,2,24,3072]{3,2,1,0:T(8,128)(2,1)S(1)}, bf16[4,2,24,3072]{3,2,1,0:T(8,128)(2,1)}, u32[]{:S(2)}, u32[]{:S(2)}) %collective-permute-start.23) | collective-permute-done | bytes 1179680 | tf_op jit(solution)/shard_map/ppermute | solution.py:706
  168.0 8.2 %assemble.3 = (bf16[32,1,24,3072]{3,2,1,0:T(8,128)(2,1)}, bf16[32,4,24,768]{3,2,1,0:T(8,128)(2,1)}) custom-call(s32[4]{0:T(128)} %pad_add_fusion.1.pos_ref, bf16[4,2,24,3072]{3,2,1,0:T(8,128)(2,1)} %copy-done.11, bf16[4,2,24,3072]{3,2,1,0:T(8,128)(2,1)} %collective-permute-done.21.refs_1_, bf16[4,2,24,3072]{3,2,1,0:T(8,128)(2,1)} %collective-permute-done.22.refs_2_, ...), custom_call_target="tpu_custom_call" | custom-call | flops 30799998976 | bytes 98000000 | tf_op jit(solution)/shard_map/assemble/pallas_call | solution.py:790
  176.2 15.4 %mlp.2 = (f32[416,768]{1,0:T(8,128)}, f32[416,768]{1,0:T(8,128)}, f32[416,768]{1,0:T(8,128)}, f32[416,768]{1,0:T(8,128)}, bf16[416,768]{1,0:T(8,128)(2,1)}, /*in...) custom-call(f32[416,768]{1,0:T(8,128)} %bitcast_convert_fusion.x_ref, bf16[416,768]{1,0:T(8,128)(2,1)} %bitcast.341, ...), custom_call_target="tpu_custom_call" | custom-call | flops 65999998976 | bytes 210000000 | tf_op jit(solution)/shard_map/mlp/pallas_call | solution.py:487
  191.6 5.9 %qkv.3 = (bf16[416,2304]{1,0:T(8,128)(2,1)}, bf16[416,768]{1,0:T(8,128)(2,1)}) custom-call(f32[416,768]{1,0:T(8,128)} %get-tuple-element.84.x_ref, f32[2,32,768]{2,1,0:T(8,128)} %add_convert_fusion.8.small_ref, bf16[768,9216]{1,0:T(8,128)(2,1)} %all-gather.2.cloned.1.call-done.w_ref.wp_ref.w1_ref), custom_call_target="tpu_custom_call" | custom-call | flops 26400000000 | bytes 84000000 | tf_op jit(solution)/shard_map/qkv/pallas_call | solution.py:350
  197.6 8.5 %attention.3 = (bf16[2,208,768]{2,1,0:T(8,128)(2,1)}, f32[2,16,256]{2,1,0:T(8,128)}) custom-call(bf16[2,208,2304]{2,1,0:T(8,128)(2,1)} %bitcast.345, f32[24,208,256]{2,1,0:T(8,128)} %bias_expand.1.refs_8_.bias_ref), custom_call_target="tpu_custom_call" | custom-call | flops 35200000000 | bytes 112000000 | tf_op jit(solution)/shard_map/attention/pallas_call | solution.py:203
  206.0 4.5 unpack.1
  210.6 15.6 %mlp.3 = (f32[416,768]{1,0:T(8,128)}, f32[416,768]{1,0:T(8,128)}, f32[416,768]{1,0:T(8,128)}, f32[416,768]{1,0:T(8,128)}, bf16[416,768]{1,0:T(8,128)(2,1)}, /*in...) custom-call(f32[416,768]{1,0:T(8,128)} %get-tuple-element.84.x_ref, bf16[416,768]{1,0:T(8,128)(2,1)} %bitcast.353, ...), custom_call_target="tpu_custom_call" | custom-call | flops 65999998976 | bytes 210000000 | tf_op jit(solution)/shard_map/mlp/pallas_call | solution.py:487
  226.2 20.4 %mlp_grad.2 = (bf16[768,3456]{1,0:T(8,128)(2,1)}, bf16[768,3456]{1,0:T(8,128)(2,1)}, f32[416,768]{1,0:T(8,128)}, bf16[416,768]{1,0:T(8,128)(2,1)}, f32[16,768]{1,0:T(8,128)}) custom-call(s32[1]{0:T(128)} %bitcast.7.core_ref, f32[416,768]{1,0:T(8,128)} %convert_select_fusion.g_ref, f32[416,768]{1,0:T(8,128)} %get-tuple-element.90.mid_ref, ...), custom_call_target="tpu_custom_call" | custom-call | flops 88000004096 | bytes 280000000 | tf_op jit(solution)/shard_map/mlp_grad/pallas_call | solution.py:647
  248.7 12.1 %attention_grad.2 = (bf16[2,208,2304]{2,1,0:T(8,128)(2,1)}, f32[12,208,256]{2,1,0:T(8,128)}) custom-call(bf16[2,208,2304]{2,1,0:T(8,128)(2,1)} %bitcast.346, f32[24,208,256]{2,1,0:T(8,128)} %bias_expand.1.refs_8_.bias_ref, f32[2,16,256]{2,1,0:T(8,128)} %get-tuple-element.89.lse_ref, bf16[2,208,768]{2,1,0:T(8,128)(2,1)} %bitcast.351), custom_call_target="tpu_custom_call" | custom-call | flops 52800000000 | bytes 168000000 | tf_op jit(solution)/shard_map/attention_grad/pallas_call | solution.py:269
  260.8 4.0 constant_dynamic-slice_fusion.20
  269.6 11.4 %qkv_grad.2 = (bf16[768,1152]{1,0:T(8,128)(2,1)}, bf16[768,1152]{1,0:T(8,128)(2,1)}, f32[416,768]{1,0:T(8,128)}, f32[8,768]{1,0:T(8,128)}) custom-call(s32[1]{0:T(128)} %bitcast.7.core_ref, bf16[416,2304]{1,0:T(8,128)(2,1)} %bitcast.348, bf16[416,768]{1,0:T(8,128)(2,1)} %get-tuple-element.98.h_ref, f32[416,768]{1,0:T(8,128)} %get-tuple-element.84.x_ref, ...), custom_call_target="tpu_custom_call" | custom-call | flops 48399998976 | bytes 154000000 | tf_op jit(solution)/shard_map/qkv_grad/pallas_call | solution.py:418
  281.0 4.0 collective-permute-done.29.refs_0_
  287.2 20.4 %mlp_grad.3 = (bf16[768,3456]{1,0:T(8,128)(2,1)}, bf16[768,3456]{1,0:T(8,128)(2,1)}, f32[416,768]{1,0:T(8,128)}, bf16[416,768]{1,0:T(8,128)(2,1)}, f32[16,768]{1,0:T(8,128)}) custom-call(s32[1]{0:T(128)} %bitcast.7.core_ref, f32[416,768]{1,0:T(8,128)} %get-tuple-element.101.g_ref, f32[416,768]{1,0:T(8,128)} %get-tuple-element.102.mid_ref, ...), custom_call_target="tpu_custom_call" | custom-call | flops 88000004096 | bytes 280000000 | tf_op jit(solution)/shard_map/mlp_grad/pallas_call | solution.py:647
  312.5 6.1 %collective-permute-done.33.refs_1_ = bf16[4,2,24,1152]{3,2,1,0:T(8,128)(2,1)S(1)} collective-permute-done((bf16[4,2,24,1152]{3,2,1,0:T(8,128)(2,1)S(1)}, bf16[4,2,24,1152]{3,2,1,0:T(8,128)(2,1)S(1)}, u32[]{:S(2)}, u32[]{:S(2)}) %collective-permute-start.33) | collective-permute-done | bytes 442400 | tf_op jit(solution)/shard_map/ppermute | solution.py:706
  320.5 11.6 %attention_grad.3 = (bf16[2,208,2304]{2,1,0:T(8,128)(2,1)}, f32[12,208,256]{2,1,0:T(8,128)}) custom-call(bf16[2,208,2304]{2,1,0:T(8,128)(2,1)} %bitcast.344, f32[24,208,256]{2,1,0:T(8,128)} %bias_expand.1.refs_8_.bias_ref, f32[2,16,256]{2,1,0:T(8,128)} %get-tuple-element.88.lse_ref, bf16[2,208,768]{2,1,0:T(8,128)(2,1)} %bitcast.352, ...), custom_call_target="tpu_custom_call" | custom-call | flops 52800000000 | bytes 168000000 | tf_op jit(solution)/shard_map/attention_grad/pallas_call | solution.py:269
  334.5 2.1 fusion.2
  336.6 3.0 constant_dynamic-slice_fusion.10
  344.1 2.6 collective-permute-start.37
  350.2 8.0 %collective-permute-done.35.refs_2_ = bf16[4,2,24,3456]{3,2,1,0:T(8,128)(2,1)S(1)} collective-permute-done((bf16[4,2,24,3456]{3,2,1,0:T(8,128)(2,1)S(1)}, bf16[4,2,24,3456]{3,2,1,0:T(8,128)(2,1)S(1)}, u32[]{:S(2)}, u32[]{:S(2)}) %collective-permute-start.35) | collective-permute-done | bytes 1327136 | tf_op jit(solution)/shard_map/ppermute | solution.py:706
  360.3 11.2 %qkv_grad.3 = (bf16[768,1152]{1,0:T(8,128)(2,1)}, bf16[768,1152]{1,0:T(8,128)(2,1)}, f32[416,768]{1,0:T(8,128)}, f32[8,768]{1,0:T(8,128)}) custom-call(s32[1]{0:T(128)} %bitcast.7.core_ref, bf16[416,2304]{1,0:T(8,128)(2,1)} %bitcast.347, bf16[416,768]{1,0:T(8,128)(2,1)} %get-tuple-element.114.h_ref, f32[416,768]{1,0:T(8,128)} %bitcast_convert_fusion.x_ref, ...), custom_call_target="tpu_custom_call" | custom-call | flops 48399998976 | bytes 154000000 | tf_op jit(solution)/shard_map/qkv_grad/pallas_call | solution.py:418
  371.7 6.4 %bias_reduce.2.refs_0_.refs_5_ = f32[12,1,768]{2,1,0:T(1,128)} custom-call(f32[12,208,256]{2,1,0:T(8,128)} %get-tuple-element.127.g_ref, bf16[224,208]{1,0:T(8,128)(2,1)} %constant.394.clone.rows_ref, bf16[256,384]{1,0:T(8,128)(2,1)} %constant.395.clone.lanes_ref, f32[8,768]{1,0:T(8,128)} %get-tuple-element.124.refs_0_, ...), custom_call_target="tpu_custom_call" | custom-call | flops 26400000000 | bytes 84000000 | tf_op jit(solution)/shard_map/bias_reduce/pallas_call | solution.py:152
  378.0 5.8 %collective-permute-done.44 = bf16[4,2,24,3456]{3,2,1,0:T(8,128)(2,1)} collective-permute-done((bf16[4,2,24,3456]{3,2,1,0:T(8,128)(2,1)}, bf16[4,2,24,3456]{3,2,1,0:T(8,128)(2,1)}, u32[]{:S(2)}, u32[]{:S(2)}) %collective-permute-start.44) | collective-permute-done | bytes 1327136 | tf_op jit(solution)/shard_map/ppermute | solution.py:706
  385.1 2.3 fusion
  391.2 2.6 collective-permute-start.48
  395.3 6.5 %bias_reduce.3.refs_2_ = f32[12,1,768]{2,1,0:T(1,128)} custom-call(f32[12,208,256]{2,1,0:T(8,128)} %get-tuple-element.126.g_ref, bf16[224,208]{1,0:T(8,128)(2,1)} %constant.394.clone.rows_ref, bf16[256,384]{1,0:T(8,128)(2,1)} %constant.395.clone.lanes_ref, f32[12,1,768]{2,1,0:T(1,128)} %bias_reduce.2.refs_0_.refs_5_, ...), custom_call_target="tpu_custom_call" | custom-call | flops 26400000000 | bytes 84000000 | tf_op jit(solution)/shard_map/bias_reduce/pallas_call | solution.py:152
  405.4 6.1 %collective-permute-done.42.refs_6_ = bf16[4,2,24,1152]{3,2,1,0:T(8,128)(2,1)S(1)} collective-permute-done((bf16[4,2,24,1152]{3,2,1,0:T(8,128)(2,1)S(1)}, bf16[4,2,24,1152]{3,2,1,0:T(8,128)(2,1)S(1)}, u32[]{:S(2)}, u32[]{:S(2)}) %collective-permute-start.42) | collective-permute-done | bytes 442400 | tf_op jit(solution)/shard_map/ppermute | solution.py:706
  413.9 3.3 collective-permute-done.43.refs_7_
  422.1 2.4 reshape.306
  431.4 2.8 collective-permute-start.47
  435.9 2.9 collective-permute-start.61
  442.6 3.9 collective-permute-start.55
  446.6 5.1 %collective-permute-done.60 = bf16[2,24,1152]{2,1,0:T(8,128)(2,1)S(1)} collective-permute-done((bf16[2,24,1152]{2,1,0:T(8,128)(2,1)S(1)}, bf16[2,24,1152]{2,1,0:T(8,128)(2,1)S(1)}, u32[]{:S(2)}, u32[]{:S(2)}) %collective-permute-start.60) | collective-permute-done | bytes 110624 | tf_op jit(solution)/shard_map/ppermute | solution.py:706
  453.1 4.3 collective-permute-done.50
  (349 shorter events, 111.9 us)
Async XLA Ops:
  7.2 184.4 %all-gather.2.cloned.1.call-start = ((), (), s32[]{:S(2)}) async-start(), calls=%async_computation | async-start | bytes 14598144 | tf_op jit(solution)/shard_map/all_gather | solution.py:1071
  10.1 32.1 %collective-permute-start = (bf16[2,32,128]{2,1,0:T(8,128)(2,1)}, bf16[2,32,128]{2,1,0:T(8,128)(2,1)S(1)}, u32[]{:S(2)}, u32[]{:S(2)}) collective-permute-start(bf16[2,32,128]{2,1,0:T(8,128)(2,1)} %small_own.1.refs_0_), channel_id=1, source_target_pairs={{0,2},{1,3},{2,4},{3,5},{4,6},{5,7},{6,0},{7,1},{8,10},{9,11},{10,... | collective-permute-start | bytes 49160 | tf_op jit(solution)/shard_map/ppermute | solution.py:706
  13.1 29.1 %collective-permute-start.1 = (bf16[2,32,128]{2,1,0:T(8,128)(2,1)}, bf16[2,32,128]{2,1,0:T(8,128)(2,1)S(1)}, u32[]{:S(2)}, u32[]{:S(2)}) collective-permute-start(bf16[2,32,128]{2,1,0:T(8,128)(2,1)} %small_own.1.refs_0_), channel_id=1, source_target_pairs={{0,4},{1,5},{2,6},{3,7},{4,0},{5,1},{6,2},{7,3},{8,12},{9,13},{10,... | collective-permute-start | bytes 49160 | tf_op jit(solution)/shard_map/ppermute | solution.py:706
  18.5 21.5 %collective-permute-start.8 = (bf16[2,24,1536]{2,1,0:T(8,128)(2,1)S(1)}, bf16[2,24,1536]{2,1,0:T(8,128)(2,1)S(1)}, u32[]{:S(2)}, u32[]{:S(2)}) collective-permute-start(bf16[2,24,1536]{2,1,0:T(8,128)(2,1)S(1)} %get-tuple-element.263), channel_id=1, source_target_pairs={{0,4},{1,5},{2,6},{3,7},{4,0},{5,1},{6,2},{7,3},{8,12},{9,13},{10,... | collective-permute-start | bytes 442376 | tf_op jit(solution)/shard_map/ppermute | solution.py:706
  18.7 21.3 %collective-permute-start.7 = (bf16[2,24,1536]{2,1,0:T(8,128)(2,1)S(1)}, bf16[2,24,1536]{2,1,0:T(8,128)(2,1)S(1)}, u32[]{:S(2)}, u32[]{:S(2)}) collective-permute-start(bf16[2,24,1536]{2,1,0:T(8,128)(2,1)S(1)} %get-tuple-element.263), channel_id=1, source_target_pairs={{0,2},{1,3},{2,4},{3,5},{4,6},{5,7},{6,0},{7,1},{8,10},{9,11},{10,... | collective-permute-start | bytes 442376 | tf_op jit(solution)/shard_map/ppermute | solution.py:706
  23.8 18.4 %collective-permute-start.2 = (bf16[2,32,128]{2,1,0:T(8,128)(2,1)S(1)}, bf16[2,32,128]{2,1,0:T(8,128)(2,1)S(1)}, u32[]{:S(2)}, u32[]{:S(2)}) collective-permute-start(bf16[2,32,128]{2,1,0:T(8,128)(2,1)S(1)} %copy-done.42), channel_id=1, source_target_pairs={{0,6},{1,7},{2,0},{3,1},{4,2},{5,3},{6,4},{7,5},{8,14},{9,15},{10,... | collective-permute-start | bytes 49160 | tf_op jit(solution)/shard_map/ppermute | solution.py:706
  40.1 23.7 %collective-permute-start.10 = (bf16[4,2,24,1536]{3,2,1,0:T(8,128)(2,1)S(1)}, bf16[4,2,24,1536]{3,2,1,0:T(8,128)(2,1)S(1)}, u32[]{:S(2)}, u32[]{:S(2)}) collective-permute-start(bf16[4,2,24,1536]{3,2,1,0:T(8,128)(2,1)S(1)} %pad_maximum_fusion.refs_0_), channel_id=1, source_target_pairs={{0,1},{1,0},{2,3},{3,2},{4,5},{5,4},{6,7},{7,6},{8,24},{9,25},{10,... | collective-permute-start | bytes 1769480 | tf_op jit(solution)/shard_map/ppermute | solution.py:706
  45.2 20.0 %collective-permute-start.17 = (bf16[24,3072]{1,0:T(8,128)(2,1)S(1)}, bf16[24,3072]{1,0:T(8,128)(2,1)S(1)}, u32[]{:S(2)}, u32[]{:S(2)}) collective-permute-start(bf16[24,3072]{1,0:T(8,128)(2,1)S(1)} %constant_dynamic-update-slice_fusion.4), channel_id=1, source_target_pairs={{0,8},{1,9},{2,10},{3,11},{4,12},{5,13},{6,14},{7,15},{8,0},{9,1},... | collective-permute-start | bytes 442376 | tf_op jit(solution)/shard_map/ppermute | solution.py:706
  46.7 11.4 %collective-permute-start.4 = (bf16[2,32,768]{2,1,0:T(8,128)(2,1)S(1)}, bf16[2,32,768]{2,1,0:T(8,128)(2,1)S(1)}, u32[]{:S(2)}, u32[]{:S(2)}) collective-permute-start(bf16[2,32,768]{2,1,0:T(8,128)(2,1)S(1)} %add.725), channel_id=1, source_target_pairs={{0,1},{1,0},{2,3},{3,2},{4,5},{5,4},{6,7},{7,6},{8,9},{9,8},{10,11... | collective-permute-start | bytes 294920 | tf_op jit(solution)/shard_map/ppermute | solution.py:706
  58.1 11.7 %collective-permute-start.5 = (bf16[2,32,768]{2,1,0:T(8,128)(2,1)S(1)}, bf16[2,32,768]{2,1,0:T(8,128)(2,1)S(1)}, u32[]{:S(2)}, u32[]{:S(2)}) collective-permute-start(bf16[2,32,768]{2,1,0:T(8,128)(2,1)S(1)} %add.726), channel_id=1, source_target_pairs={{0,16},{1,17},{2,18},{3,19},{4,20},{5,21},{6,22},{7,23},{8,24},{9,... | collective-permute-start | bytes 294920 | tf_op jit(solution)/shard_map/ppermute | solution.py:706
  59.5 33.1 %collective-permute-start.11 = (bf16[4,2,24,1536]{3,2,1,0:T(8,128)(2,1)S(1)}, bf16[4,2,24,1536]{3,2,1,0:T(8,128)(2,1)S(1)}, u32[]{:S(2)}, u32[]{:S(2)}) collective-permute-start(bf16[4,2,24,1536]{3,2,1,0:T(8,128)(2,1)S(1)} %pad_maximum_fusion.refs_0_), channel_id=1, source_target_pairs={{0,16},{1,17},{2,18},{3,19},{4,20},{5,21},{6,22},{7,23},{8,9},{9,8... | collective-permute-start | bytes 1769480 | tf_op jit(solution)/shard_map/ppermute | solution.py:706
  63.8 29.4 %collective-permute-start.12 = (bf16[4,2,24,1536]{3,2,1,0:T(8,128)(2,1)S(1)}, bf16[4,2,24,1536]{3,2,1,0:T(8,128)(2,1)S(1)}, u32[]{:S(2)}, u32[]{:S(2)}) collective-permute-start(bf16[4,2,24,1536]{3,2,1,0:T(8,128)(2,1)S(1)} %collective-permute-done.10.refs_1_), channel_id=1, source_target_pairs={{0,16},{1,17},{2,18},{3,19},{4,20},{5,21},{6,22},{7,23},{8,9},{9,8... | collective-permute-start | bytes 1769480 | tf_op jit(solution)/shard_map/ppermute | solution.py:706
  65.3 15.8 %collective-permute-start.18 = (bf16[2,24,3072]{2,1,0:T(8,128)(2,1)S(1)}, bf16[2,24,3072]{2,1,0:T(8,128)(2,1)S(1)}, u32[]{:S(2)}, u32[]{:S(2)}) collective-permute-start(bf16[2,24,3072]{2,1,0:T(8,128)(2,1)S(1)} %get-tuple-element.253), channel_id=1, source_target_pairs={{0,2},{1,3},{2,4},{3,5},{4,6},{5,7},{6,0},{7,1},{8,10},{9,11},{10,... | collective-permute-start | bytes 884744 | tf_op jit(solution)/shard_map/ppermute | solution.py:706
  66.5 26.1 %collective-permute-start.19 = (bf16[2,24,3072]{2,1,0:T(8,128)(2,1)S(1)}, bf16[2,24,3072]{2,1,0:T(8,128)(2,1)S(1)}, u32[]{:S(2)}, u32[]{:S(2)}) collective-permute-start(bf16[2,24,3072]{2,1,0:T(8,128)(2,1)S(1)} %get-tuple-element.253), channel_id=1, source_target_pairs={{0,6},{1,7},{2,0},{3,1},{4,2},{5,3},{6,4},{7,5},{8,14},{9,15},{10,... | collective-permute-start | bytes 884744 | tf_op jit(solution)/shard_map/ppermute | solution.py:706
  69.9 33.8 %collective-permute-start.13 = (bf16[4,2,24,1536]{3,2,1,0:T(8,128)(2,1)S(1)}, bf16[4,2,24,1536]{3,2,1,0:T(8,128)(2,1)S(1)}, u32[]{:S(2)}, u32[]{:S(2)}) collective-permute-start(bf16[4,2,24,1536]{3,2,1,0:T(8,128)(2,1)S(1)} %pad_maximum_fusion.refs_0_), channel_id=1, source_target_pairs={{0,8},{1,9},{2,10},{3,11},{4,12},{5,13},{6,14},{7,15},{8,0},{9,1},... | collective-permute-start | bytes 1769480 | tf_op jit(solution)/shard_map/ppermute | solution.py:706
  81.0 32.7 %collective-permute-start.20 = (bf16[2,24,3072]{2,1,0:T(8,128)(2,1)S(1)}, bf16[2,24,3072]{2,1,0:T(8,128)(2,1)S(1)}, u32[]{:S(2)}, u32[]{:S(2)}) collective-permute-start(bf16[2,24,3072]{2,1,0:T(8,128)(2,1)S(1)} %get-tuple-element.253), channel_id=1, source_target_pairs={{0,4},{1,5},{2,6},{3,7},{4,0},{5,1},{6,2},{7,3},{8,12},{9,13},{10,... | collective-permute-start | bytes 884744 | tf_op jit(solution)/shard_map/ppermute | solution.py:706
  92.7 11.1 %collective-permute-start.14 = (bf16[4,2,24,1536]{3,2,1,0:T(8,128)(2,1)S(1)}, bf16[4,2,24,1536]{3,2,1,0:T(8,128)(2,1)S(1)}, u32[]{:S(2)}, u32[]{:S(2)}) collective-permute-start(bf16[4,2,24,1536]{3,2,1,0:T(8,128)(2,1)S(1)} %collective-permute-done.10.refs_1_), channel_id=1, source_target_pairs={{0,8},{1,9},{2,10},{3,11},{4,12},{5,13},{6,14},{7,15},{8,0},{9,1},... | collective-permute-start | bytes 1769480 | tf_op jit(solution)/shard_map/ppermute | solution.py:706
  114.0 33.1 %collective-permute-start.21 = (bf16[4,2,24,3072]{3,2,1,0:T(8,128)(2,1)S(1)}, bf16[4,2,24,3072]{3,2,1,0:T(8,128)(2,1)}, u32[]{:S(2)}, u32[]{:S(2)}) collective-permute-start(bf16[4,2,24,3072]{3,2,1,0:T(8,128)(2,1)S(1)} %maximum_add_fusion.refs_0_), channel_id=1, source_target_pairs={{0,1},{1,0},{2,3},{3,2},{4,5},{5,4},{6,7},{7,6},{8,24},{9,25},{10,... | collective-permute-start | bytes 3538952 | tf_op jit(solution)/shard_map/ppermute | solution.py:706
  115.6 34.9 %collective-permute-start.22 = (bf16[4,2,24,3072]{3,2,1,0:T(8,128)(2,1)S(1)}, bf16[4,2,24,3072]{3,2,1,0:T(8,128)(2,1)}, u32[]{:S(2)}, u32[]{:S(2)}) collective-permute-start(bf16[4,2,24,3072]{3,2,1,0:T(8,128)(2,1)S(1)} %maximum_add_fusion.refs_0_), channel_id=1, source_target_pairs={{0,16},{1,17},{2,18},{3,19},{4,20},{5,21},{6,22},{7,23},{8,9},{9,8... | collective-permute-start | bytes 3538952 | tf_op jit(solution)/shard_map/ppermute | solution.py:706
  148.4 16.4 %collective-permute-start.23 = (bf16[4,2,24,3072]{3,2,1,0:T(8,128)(2,1)S(1)}, bf16[4,2,24,3072]{3,2,1,0:T(8,128)(2,1)}, u32[]{:S(2)}, u32[]{:S(2)}) collective-permute-start(bf16[4,2,24,3072]{3,2,1,0:T(8,128)(2,1)S(1)} %broadcast_add_fusion), channel_id=1, source_target_pairs={{0,16},{1,17},{2,18},{3,19},{4,20},{5,21},{6,22},{7,23},{8,9},{9,8... | collective-permute-start | bytes 3538952 | tf_op jit(solution)/shard_map/ppermute | solution.py:706
  150.0 16.5 %collective-permute-start.24 = (bf16[4,2,24,3072]{3,2,1,0:T(8,128)(2,1)S(1)}, bf16[4,2,24,3072]{3,2,1,0:T(8,128)(2,1)}, u32[]{:S(2)}, u32[]{:S(2)}) collective-permute-start(bf16[4,2,24,3072]{3,2,1,0:T(8,128)(2,1)S(1)} %maximum_add_fusion.refs_0_), channel_id=1, source_target_pairs={{0,8},{1,9},{2,10},{3,11},{4,12},{5,13},{6,14},{7,15},{8,0},{9,1},... | collective-permute-start | bytes 3538952 | tf_op jit(solution)/shard_map/ppermute | solution.py:706
  150.0 16.5 %collective-permute-start.25 = (bf16[4,2,24,3072]{3,2,1,0:T(8,128)(2,1)}, bf16[4,2,24,3072]{3,2,1,0:T(8,128)(2,1)}, u32[]{:S(2)}, u32[]{:S(2)}) collective-permute-start(bf16[4,2,24,3072]{3,2,1,0:T(8,128)(2,1)} %collective-permute-done.21.refs_1_), channel_id=1, source_target_pairs={{0,8},{1,9},{2,10},{3,11},{4,12},{5,13},{6,14},{7,15},{8,0},{9,1},... | collective-permute-start | bytes 3538952 | tf_op jit(solution)/shard_map/ppermute | solution.py:706
  150.5 16.0 %collective-permute-start.26 = (bf16[4,2,24,3072]{3,2,1,0:T(8,128)(2,1)}, bf16[4,2,24,3072]{3,2,1,0:T(8,128)(2,1)}, u32[]{:S(2)}, u32[]{:S(2)}) collective-permute-start(bf16[4,2,24,3072]{3,2,1,0:T(8,128)(2,1)} %collective-permute-done.22.refs_2_), channel_id=1, source_target_pairs={{0,8},{1,9},{2,10},{3,11},{4,12},{5,13},{6,14},{7,15},{8,0},{9,1},... | collective-permute-start | bytes 3538952 | tf_op jit(solution)/shard_map/ppermute | solution.py:706
  246.6 14.2 %collective-permute-start.28 = (bf16[768,3456]{1,0:T(8,128)(2,1)}, bf16[768,3456]{1,0:T(8,128)(2,1)}, u32[]{:S(2)}, u32[]{:S(2)}) collective-permute-start(bf16[768,3456]{1,0:T(8,128)(2,1)} %get-tuple-element.100), channel_id=1, source_target_pairs={{0,8},{1,9},{2,10},{3,11},{4,12},{5,13},{6,14},{7,15},{8,0},{9,1},... | collective-permute-start | bytes 15925256 | tf_op jit(solution)/shard_map/ppermute | solution.py:706
  267.1 18.0 %collective-permute-start.29 = (bf16[4,2,24,3456]{3,2,1,0:T(8,128)(2,1)S(1)}, bf16[4,2,24,3456]{3,2,1,0:T(8,128)(2,1)}, u32[]{:S(2)}, u32[]{:S(2)}) collective-permute-start(bf16[4,2,24,3456]{3,2,1,0:T(8,128)(2,1)S(1)} %fusion.4), channel_id=1, source_target_pairs={{0,16},{1,17},{2,18},{3,19},{4,20},{5,21},{6,22},{7,23},{8,9},{9,8... | collective-permute-start | bytes 3981320 | tf_op jit(solution)/shard_map/ppermute | solution.py:706
  269.0 51.5 %collective-permute-start.30 = (bf16[4,2,24,3456]{3,2,1,0:T(8,128)(2,1)S(1)}, bf16[4,2,24,3456]{3,2,1,0:T(8,128)(2,1)}, u32[]{:S(2)}, u32[]{:S(2)}) collective-permute-start(bf16[4,2,24,3456]{3,2,1,0:T(8,128)(2,1)S(1)} %fusion.5), channel_id=1, source_target_pairs={{0,16},{1,17},{2,18},{3,19},{4,20},{5,21},{6,22},{7,23},{8,9},{9,8... | collective-permute-start | bytes 3981320 | tf_op jit(solution)/shard_map/ppermute | solution.py:706
  281.0 26.9 %collective-permute-start.31 = (bf16[768,1152]{1,0:T(8,128)(2,1)}, bf16[768,1152]{1,0:T(8,128)(2,1)S(1)}, u32[]{:S(2)}, u32[]{:S(2)}) collective-permute-start(bf16[768,1152]{1,0:T(8,128)(2,1)} %get-tuple-element.112), channel_id=1, source_target_pairs={{0,8},{1,9},{2,10},{3,11},{4,12},{5,13},{6,14},{7,15},{8,0},{9,1},... | collective-permute-start | bytes 5308424 | tf_op jit(solution)/shard_map/ppermute | solution.py:706
  286.9 46.0 %collective-permute-start.32 = (bf16[4,2,24,3456]{3,2,1,0:T(8,128)(2,1)S(1)}, bf16[4,2,24,3456]{3,2,1,0:T(8,128)(2,1)S(1)}, u32[]{:S(2)}, u32[]{:S(2)}) collective-permute-start(bf16[4,2,24,3456]{3,2,1,0:T(8,128)(2,1)S(1)} %fusion.3), channel_id=1, source_target_pairs={{0,1},{1,0},{2,3},{3,2},{4,5},{5,4},{6,7},{7,6},{8,24},{9,25},{10,... | collective-permute-start | bytes 3981320 | tf_op jit(solution)/shard_map/ppermute | solution.py:706
  307.6 28.9 %collective-permute-start.34 = (bf16[768,3456]{1,0:T(8,128)(2,1)}, bf16[768,3456]{1,0:T(8,128)(2,1)}, u32[]{:S(2)}, u32[]{:S(2)}) collective-permute-start(bf16[768,3456]{1,0:T(8,128)(2,1)} %get-tuple-element.120), channel_id=1, source_target_pairs={{0,8},{1,9},{2,10},{3,11},{4,12},{5,13},{6,14},{7,15},{8,0},{9,1},... | collective-permute-start | bytes 15925256 | tf_op jit(solution)/shard_map/ppermute | solution.py:706
  312.0 20.1 %collective-permute-start.52 = (bf16[4,2,24,1152]{3,2,1,0:T(8,128)(2,1)S(1)}, bf16[4,2,24,1152]{3,2,1,0:T(8,128)(2,1)S(1)}, u32[]{:S(2)}, u32[]{:S(2)}) collective-permute-start(bf16[4,2,24,1152]{3,2,1,0:T(8,128)(2,1)S(1)} %fusion.19), channel_id=1, source_target_pairs={{0,16},{1,17},{2,18},{3,19},{4,20},{5,21},{6,22},{7,23},{8,9},{9,8... | collective-permute-start | bytes 1327112 | tf_op jit(solution)/shard_map/ppermute | solution.py:706
  318.8 13.3 %collective-permute-start.40 = (bf16[4,2,24,1152]{3,2,1,0:T(8,128)(2,1)S(1)}, bf16[4,2,24,1152]{3,2,1,0:T(8,128)(2,1)S(1)}, u32[]{:S(2)}, u32[]{:S(2)}) collective-permute-start(bf16[4,2,24,1152]{3,2,1,0:T(8,128)(2,1)S(1)} %fusion.11), channel_id=1, source_target_pairs={{0,1},{1,0},{2,3},{3,2},{4,5},{5,4},{6,7},{7,6},{8,24},{9,25},{10,... | collective-permute-start | bytes 1327112 | tf_op jit(solution)/shard_map/ppermute | solution.py:706
  340.4 17.8 %collective-permute-start.35 = (bf16[4,2,24,3456]{3,2,1,0:T(8,128)(2,1)S(1)}, bf16[4,2,24,3456]{3,2,1,0:T(8,128)(2,1)S(1)}, u32[]{:S(2)}, u32[]{:S(2)}) collective-permute-start(bf16[4,2,24,3456]{3,2,1,0:T(8,128)(2,1)S(1)} %fusion.6), channel_id=1, source_target_pairs={{0,16},{1,17},{2,18},{3,19},{4,20},{5,21},{6,22},{7,23},{8,9},{9,8... | collective-permute-start | bytes 3981320 | tf_op jit(solution)/shard_map/ppermute | solution.py:706
  342.8 28.8 %collective-permute-start.36 = (bf16[2,24,3456]{2,1,0:T(8,128)(2,1)S(1)}, bf16[2,24,3456]{2,1,0:T(8,128)(2,1)}, u32[]{:S(2)}, u32[]{:S(2)}) collective-permute-start(bf16[2,24,3456]{2,1,0:T(8,128)(2,1)S(1)} %get-tuple-element.213), channel_id=1, source_target_pairs={{0,2},{1,3},{2,4},{3,5},{4,6},{5,7},{6,0},{7,1},{8,10},{9,11},{10,... | collective-permute-start | bytes 995336 | tf_op jit(solution)/shard_map/ppermute | solution.py:706
  344.1 27.5 %collective-permute-start.37 = (bf16[2,24,3456]{2,1,0:T(8,128)(2,1)}, bf16[2,24,3456]{2,1,0:T(8,128)(2,1)}, u32[]{:S(2)}, u32[]{:S(2)}) collective-permute-start(bf16[2,24,3456]{2,1,0:T(8,128)(2,1)} %get-tuple-element.212), channel_id=1, source_target_pairs={{0,4},{1,5},{2,6},{3,7},{4,0},{5,1},{6,2},{7,3},{8,12},{9,13},{10,... | collective-permute-start | bytes 995336 | tf_op jit(solution)/shard_map/ppermute | solution.py:706
  346.7 25.0 %collective-permute-start.38 = (bf16[2,24,3456]{2,1,0:T(8,128)(2,1)S(1)}, bf16[2,24,3456]{2,1,0:T(8,128)(2,1)}, u32[]{:S(2)}, u32[]{:S(2)}) collective-permute-start(bf16[2,24,3456]{2,1,0:T(8,128)(2,1)S(1)} %get-tuple-element.211), channel_id=1, source_target_pairs={{0,6},{1,7},{2,0},{3,1},{4,2},{5,3},{6,4},{7,5},{8,14},{9,15},{10,... | collective-permute-start | bytes 995336 | tf_op jit(solution)/shard_map/ppermute | solution.py:706
  349.7 34.1 %collective-permute-start.44 = (bf16[4,2,24,3456]{3,2,1,0:T(8,128)(2,1)}, bf16[4,2,24,3456]{3,2,1,0:T(8,128)(2,1)}, u32[]{:S(2)}, u32[]{:S(2)}) collective-permute-start(bf16[4,2,24,3456]{3,2,1,0:T(8,128)(2,1)} %fusion.7), channel_id=1, source_target_pairs={{0,16},{1,17},{2,18},{3,19},{4,20},{5,21},{6,22},{7,23},{8,9},{9,8... | collective-permute-start | bytes 3981320 | tf_op jit(solution)/shard_map/ppermute | solution.py:706
  359.9 25.2 %collective-permute-start.39 = (bf16[4,2,24,3456]{3,2,1,0:T(8,128)(2,1)}, bf16[4,2,24,3456]{3,2,1,0:T(8,128)(2,1)}, u32[]{:S(2)}, u32[]{:S(2)}) collective-permute-start(bf16[4,2,24,3456]{3,2,1,0:T(8,128)(2,1)} %fusion.1), channel_id=1, source_target_pairs={{0,1},{1,0},{2,3},{3,2},{4,5},{5,4},{6,7},{7,6},{8,24},{9,25},{10,... | collective-permute-start | bytes 3981320 | tf_op jit(solution)/shard_map/ppermute | solution.py:706
  371.6 30.2 %collective-permute-start.41 = (bf16[768,1152]{1,0:T(8,128)(2,1)}, bf16[768,1152]{1,0:T(8,128)(2,1)S(1)}, u32[]{:S(2)}, u32[]{:S(2)}) collective-permute-start(bf16[768,1152]{1,0:T(8,128)(2,1)} %get-tuple-element.131), channel_id=1, source_target_pairs={{0,8},{1,9},{2,10},{3,11},{4,12},{5,13},{6,14},{7,15},{8,0},{9,1},... | collective-permute-start | bytes 5308424 | tf_op jit(solution)/shard_map/ppermute | solution.py:706
  390.0 24.0 %collective-permute-start.45 = (bf16[2,24,3456]{2,1,0:T(8,128)(2,1)S(1)}, bf16[2,24,3456]{2,1,0:T(8,128)(2,1)}, u32[]{:S(2)}, u32[]{:S(2)}) collective-permute-start(bf16[2,24,3456]{2,1,0:T(8,128)(2,1)S(1)} %get-tuple-element.210), channel_id=1, source_target_pairs={{0,2},{1,3},{2,4},{3,5},{4,6},{5,7},{6,0},{7,1},{8,10},{9,11},{10,... | collective-permute-start | bytes 995336 | tf_op jit(solution)/shard_map/ppermute | solution.py:706
  391.2 35.2 %collective-permute-start.48 = (bf16[2,24,3456]{2,1,0:T(8,128)(2,1)}, bf16[2,24,3456]{2,1,0:T(8,128)(2,1)}, u32[]{:S(2)}, u32[]{:S(2)}) collective-permute-start(bf16[2,24,3456]{2,1,0:T(8,128)(2,1)} %get-tuple-element.209), channel_id=1, source_target_pairs={{0,4},{1,5},{2,6},{3,7},{4,0},{5,1},{6,2},{7,3},{8,12},{9,13},{10,... | collective-permute-start | bytes 995336 | tf_op jit(solution)/shard_map/ppermute | solution.py:706
  393.8 34.6 %collective-permute-start.49 = (bf16[2,24,3456]{2,1,0:T(8,128)(2,1)}, bf16[2,24,3456]{2,1,0:T(8,128)(2,1)}, u32[]{:S(2)}, u32[]{:S(2)}) collective-permute-start(bf16[2,24,3456]{2,1,0:T(8,128)(2,1)} %get-tuple-element.208), channel_id=1, source_target_pairs={{0,6},{1,7},{2,0},{3,1},{4,2},{5,3},{6,4},{7,5},{8,14},{9,15},{10,... | collective-permute-start | bytes 995336 | tf_op jit(solution)/shard_map/ppermute | solution.py:706
  404.2 13.0 %collective-permute-start.43 = (bf16[4,2,24,1152]{3,2,1,0:T(8,128)(2,1)S(1)}, bf16[4,2,24,1152]{3,2,1,0:T(8,128)(2,1)S(1)}, u32[]{:S(2)}, u32[]{:S(2)}) collective-permute-start(bf16[4,2,24,1152]{3,2,1,0:T(8,128)(2,1)S(1)} %fusion.18), channel_id=1, source_target_pairs={{0,16},{1,17},{2,18},{3,19},{4,20},{5,21},{6,22},{7,23},{8,9},{9,8... | collective-permute-start | bytes 1327112 | tf_op jit(solution)/shard_map/ppermute | solution.py:706
  412.4 21.7 %collective-permute-start.51 = (bf16[4,2,24,1152]{3,2,1,0:T(8,128)(2,1)}, bf16[4,2,24,1152]{3,2,1,0:T(8,128)(2,1)}, u32[]{:S(2)}, u32[]{:S(2)}) collective-permute-start(bf16[4,2,24,1152]{3,2,1,0:T(8,128)(2,1)} %fusion.10), channel_id=1, source_target_pairs={{0,1},{1,0},{2,3},{3,2},{4,5},{5,4},{6,7},{7,6},{8,24},{9,25},{10,... | collective-permute-start | bytes 1327112 | tf_op jit(solution)/shard_map/ppermute | solution.py:706
  420.4 37.6 %collective-permute-start.53 = (bf16[2,24,1152]{2,1,0:T(8,128)(2,1)}, bf16[2,24,1152]{2,1,0:T(8,128)(2,1)}, u32[]{:S(2)}, u32[]{:S(2)}) collective-permute-start(bf16[2,24,1152]{2,1,0:T(8,128)(2,1)} %get-tuple-element.239), channel_id=1, source_target_pairs={{0,2},{1,3},{2,4},{3,5},{4,6},{5,7},{6,0},{7,1},{8,10},{9,11},{10,... | collective-permute-start | bytes 331784 | tf_op jit(solution)/shard_map/ppermute | solution.py:706
  426.4 31.6 %collective-permute-start.54 = (bf16[2,24,1152]{2,1,0:T(8,128)(2,1)}, bf16[2,24,1152]{2,1,0:T(8,128)(2,1)}, u32[]{:S(2)}, u32[]{:S(2)}) collective-permute-start(bf16[2,24,1152]{2,1,0:T(8,128)(2,1)} %get-tuple-element.238), channel_id=1, source_target_pairs={{0,4},{1,5},{2,6},{3,7},{4,0},{5,1},{6,2},{7,3},{8,12},{9,13},{10,... | collective-permute-start | bytes 331784 | tf_op jit(solution)/shard_map/ppermute | solution.py:706
  438.8 12.9 %collective-permute-start.60 = (bf16[2,24,1152]{2,1,0:T(8,128)(2,1)S(1)}, bf16[2,24,1152]{2,1,0:T(8,128)(2,1)S(1)}, u32[]{:S(2)}, u32[]{:S(2)}) collective-permute-start(bf16[2,24,1152]{2,1,0:T(8,128)(2,1)S(1)} %get-tuple-element.236), channel_id=1, source_target_pairs={{0,4},{1,5},{2,6},{3,7},{4,0},{5,1},{6,2},{7,3},{8,12},{9,13},{10,... | collective-permute-start | bytes 331784 | tf_op jit(solution)/shard_map/ppermute | solution.py:706
  442.6 15.4 %collective-permute-start.55 = (bf16[2,24,1152]{2,1,0:T(8,128)(2,1)S(1)}, bf16[2,24,1152]{2,1,0:T(8,128)(2,1)S(1)}, u32[]{:S(2)}, u32[]{:S(2)}) collective-permute-start(bf16[2,24,1152]{2,1,0:T(8,128)(2,1)S(1)} %copy-done.31), channel_id=1, source_target_pairs={{0,6},{1,7},{2,0},{3,1},{4,2},{5,3},{6,4},{7,5},{8,14},{9,15},{10,... | collective-permute-start | bytes 331784 | tf_op jit(solution)/shard_map/ppermute | solution.py:706
  453.1 18.9 %collective-permute-start.62 = (f32[24,1152]{1,0:T(8,128)}, f32[24,1152]{1,0:T(8,128)}, u32[]{:S(2)}, u32[]{:S(2)}) collective-permute-start(f32[24,1152]{1,0:T(8,128)} %dynamic-slice_bitcast_fusion.3), channel_id=1, source_target_pairs={{0,8},{1,9},{2,10},{3,11},{4,12},{5,13},{6,14},{7,15},{8,0},{9,1},... | collective-permute-start | bytes 331784 | tf_op jit(solution)/shard_map/ppermute | solution.py:706
  (72 other events, 552.5 us)
Sparse Core Ops, SparseCore 0:
  16.9 130.0 all-gather.1

commit v5 on v4

--- a/solution.py
+++ b/solution.py
@@ -69,9 +69,9 @@
     return out
 
 
-def bias_kernel(heads, small_ref, rows_ref, lanes_ref, *refs):
+def bias_kernel(small_ref, rows_ref, lanes_ref, *refs):
     out_ref, wide_ref = refs[-2:]
-    first = lax.rem(pl.program_id(0) * GROUP, heads)
+    first = pl.program_id(0) * GROUP
     for i in range(GROUP):
         table = small_ref[0, pl.ds(TABLE + first + i, 1), :]
         one_bias(table, rows_ref, lanes_ref, out_ref.at[i], wide_ref.at[i])
@@ -94,14 +94,13 @@
     out_ref[...] = jnp.where(row >= IMG_ROWS, NEG, val)
 
 
-def build_bias(small, heads, after=()):
-    layers = small.shape[0]
+def build_bias(small, layer, heads, after=()):
     return pl.pallas_call(
-        functools.partial(bias_kernel, heads),
-        grid=(layers * heads // GROUP,),
-        out_shape=jax.ShapeDtypeStruct((layers * heads, PAD_ROWS, LANES), F32),
+        bias_kernel,
+        grid=(heads // GROUP,),
+        out_shape=jax.ShapeDtypeStruct((heads, PAD_ROWS, LANES), F32),
         in_specs=[
-            pl.BlockSpec((1, SMALL_ROWS, TILE), lambda h: (h * GROUP // heads, 0, 0)),
+            pl.BlockSpec((1, SMALL_ROWS, TILE), lambda h: (layer, 0, 0)),
             pl.BlockSpec((PAD_ROWS, BLOCK * GRID), lambda h: (0, 0)),
             pl.BlockSpec((WIDE, LANES), lambda h: (0, 0)),
         ]
@@ -109,7 +108,7 @@
         out_specs=pl.BlockSpec((GROUP, PAD_ROWS, LANES), lambda h: (h, 0, 0)),
         scratch_shapes=[pltpu.VMEM((GROUP, BLOCK * GRID, WIDE), B16)],
         compiler_params=params(),
-        cost_estimate=cost(10),
+        cost_estimate=cost(5),
         name="bias_expand",
     )(small, jnp.asarray(row_onehot(False), B16), jnp.asarray(lane_onehot(), B16), *after)
 
@@ -196,7 +195,7 @@
         out_ref[0, :, at : at + PAIR] = jnp.concatenate(parts, axis=0).T.astype(B16)
 
 
-def attention_forward(qkv, bias, layer):
+def attention_forward(qkv, bias):
     images = qkv.shape[0]
     width = qkv.shape[2] // 3
     heads = width // HEAD
@@ -209,7 +208,7 @@
         ),
         in_specs=[
             pl.BlockSpec((1, PAD_ROWS, 3 * width), lambda i: (i, 0, 0)),
-            pl.BlockSpec((heads, PAD_ROWS, LANES), lambda i: (layer, 0, 0)),
+            pl.BlockSpec((heads, PAD_ROWS, LANES), lambda i: (0, 0, 0)),
         ],
         out_specs=(
             pl.BlockSpec((1, PAD_ROWS, width), lambda i: (i, 0, 0)),
@@ -262,7 +261,7 @@
         out_ref[0, :, 2 * width + at : 2 * width + at + PAIR] = dv.astype(B16)
 
 
-def attention_backward(qkv, bias, lse, grad, layer, after=()):
+def attention_backward(qkv, bias, lse, grad, after=()):
     images = qkv.shape[0]
     width = qkv.shape[2] // 3
     heads = width // HEAD
@@ -275,7 +274,7 @@
         ),
         in_specs=[
             pl.BlockSpec((1, PAD_ROWS, 3 * width), lambda i: (i, 0, 0)),
-            pl.BlockSpec((heads, PAD_ROWS, LANES), lambda i: (layer, 0, 0)),
+            pl.BlockSpec((heads, PAD_ROWS, LANES), lambda i: (0, 0, 0)),
             pl.BlockSpec((1, 16, LANES), lambda i: (i, 0, 0)),
             pl.BlockSpec((1, PAD_ROWS, width), lambda i: (i, 0, 0)),
         ]
@@ -868,7 +867,7 @@
 
 
 def unpack_kernel(first, src_ref, *refs):
-    out_ref, sem = refs[-2:]
+    out_ref, ready_ref, sem = refs[-3:]
     shards, ratio, _, width = out_ref.shape
     copies = []
     for d in range(shards):
@@ -878,6 +877,7 @@
             )
             copy.start()
             copies.append(copy)
+    ready_ref[...] = jnp.zeros_like(ready_ref)
     for copy in copies:
         copy.wait()
 
@@ -886,9 +886,12 @@
     shards, rows, _ = packed.shape
     return pl.pallas_call(
         functools.partial(unpack_kernel, first),
-        out_shape=jax.ShapeDtypeStruct((shards, ratio, rows, width), B16),
+        out_shape=(
+            jax.ShapeDtypeStruct((shards, ratio, rows, width), B16),
+            jax.ShapeDtypeStruct((8, 128), F32),
+        ),
         in_specs=[ANY] * (1 + len(after)),
-        out_specs=pl.BlockSpec(memory_space=pltpu.VMEM),
+        out_specs=(pl.BlockSpec(memory_space=pltpu.VMEM), pl.BlockSpec(memory_space=pltpu.VMEM)),
         scratch_shapes=[pltpu.SemaphoreType.DMA],
         compiler_params=params(),
         cost_estimate=cost(5),
@@ -1072,7 +1075,7 @@
 
     if not fast:
         packed_weights = [fetch_packed(layer) for layer in range(LAYERS)]
-        bias = build_bias(small, heads)
+        bias = [build_bias(small, layer, heads) for layer in range(LAYERS)]
     else:
         first = Gathering([qkv_weight[0][None], proj_weight[0][None]])
         second = Gathering([fc1_weight[0][None], two_blocks(0)])
@@ -1080,7 +1083,7 @@
         first.plane()
         first.far()
         moved = second.along(moved)
-        bias = build_bias(small, heads, [moved[0], moved[2]])
+        bias = [build_bias(small, 0, heads, [moved[0], moved[2]])]
         packed_weights = [None, fetch_packed(1)]
     weights = []
     x = pad_rows(tokens)
@@ -1088,22 +1091,25 @@
     for layer in range(LAYERS):
         full = packed_weights[layer]
         if full is None:
-            w_qkv, w_proj = first.finish([bias])
+            w_qkv, w_proj = first.finish([bias[0]])
             w_qkv = (w_qkv.reshape(width, 3 * width), 0)
             w_proj = (w_proj.reshape(width, width), 0)
         else:
             w_qkv, w_proj, w_one = (full, 0), (full, 3), (full, 4)
         qkv, h = qkv_forward(x, small, layer, w_qkv)
         qkv = qkv.reshape(images, PAD_ROWS, 3 * width)
-        att, lse = attention_forward(qkv, bias, layer)
+        att, lse = attention_forward(qkv, bias[layer])
         att = att.reshape(images * PAD_ROWS, width)
         if full is None:
             second.plane([w_qkv[0]])
             second.far([att])
-            w_one, w_two = second.finish()
+            bias.append(build_bias(small, 1, heads, [lse]))
+            later = packed_weights[1].reshape(shards, own, -1)
+            later, ready = unpack_two(later, 4 * width + hidden, ratio, width, [lse])
+            w_one, w_two = second.finish([ready])
             w_one = (w_one.reshape(width, hidden), 0)
         elif fast:
-            w_two = unpack_two(full.reshape(shards, own, -1), 4 * width + hidden, ratio, width)
+            w_two = later
         else:
             w_two = full[:, 4 * width + hidden :].reshape(shards, own, ratio, width)
             w_two = w_two.transpose(0, 2, 1, 3)
@@ -1140,7 +1146,7 @@
         )
         main = (theirs, mine)
         d_qkv, d_bias = attention_backward(
-            qkv, bias, lse, d_att.reshape(images, PAD_ROWS, width), layer, hooks[1](main)
+            qkv, bias[layer], lse, d_att.reshape(images, PAD_ROWS, width), hooks[1](main)
         )
         tables[layer] = d_bias
         theirs, mine, grad, qkv_sums = qkv_backward(
@@ -1200,7 +1206,7 @@
     for (qkv_sums, mlp_sums), table in zip(small_grads, tables):
         parts += [qkv_sums, mlp_sums, table]
     totals = pack_small(parts, [b0.r3, b0.r2, a0.rz[0]] if fast else ())
-    totals = sum_plane(totals, a0.rz) if fast else lax.psum(totals, AXES)
+    totals = sum_plane(totals, a0.rz[1:2]) if fast else lax.psum(totals, AXES)
     late = ()
     if fast:
         late = b0.near() + b1.rz

time: 488 us -> 488 us (level)
  waiting for transfers between devices: 113 us -> 108 us
    ppermute x66, waiting for transfers between devices: 113 us -> 108 us  [send(): return lax.ppermute(v, AXES, pairs)]
    unnamed x122, local copies, waits for them, and re-layouts: 13.9 us -> 18.8 us
    pallas_call x2 -> x3, Pallas kernels: 14.8 us -> 16.6 us  [the longest x2 12.1 us: build_bias(): pl.pallas_call(bias_kernel, grid=(heads // GROUP,), out_shape=jax.ShapeDt...]
  transfers between devices with their start and end apart: 67 -> 67, of which waited for: 18 -> 17; matrix products, arithmetic and copies ran while one was open for 10% -> 9% of each run, Pallas kernels for 29% -> 25%
where the time goes in v5:
time: 488 us; the launch traced here: 484 us
  Pallas kernels  196 us (40%)
  waiting for transfers between devices  108 us (22%)
  starting transfers between devices  82.5 us (17%)
  local copies, waits for them, and re-layouts  46.8 us (10%)
  other arithmetic  30.1 us (6%)
  between operations  20.3 us (4%)
    ppermute x66, waiting for transfers between devices, send(): return lax.ppermute(v, AXES, pairs)  108 us
    ppermute x66, starting transfers between devices, send(): return lax.ppermute(v, AXES, pairs)  82.5 us
    pallas_call x2, Pallas kernels, mlp_backward(): pl.pallas_call(mlp_grad_kernel, grid=(hidden // TILE,), out_shape=(jax.Sh...  40.8 us
    pallas_call x2, Pallas kernels, mlp_forward(): pl.pallas_call(mlp_kernel, grid=(hidden // TILE,), out_shape=(full, full,...  31.1 us
    pallas_call x2, Pallas kernels, attention_backward(): pl.pallas_call(functools.partial(attention_grad_kernel, width), grid=(ima...  23.7 us
    pallas_call x2, Pallas kernels, qkv_backward(): pl.pallas_call(qkv_grad_kernel, grid=(3,), out_shape=(jax.ShapeDtypeStruc...  22.5 us
    unnamed x122, local copies, waits for them, and re-layouts  18.8 us
    pallas_call x2, Pallas kernels, attention_forward(): pl.pallas_call(functools.partial(attention_kernel, width), grid=(images,)...  16.8 us
  transfers between devices with their start and end apart: 67, of which 17 were waited for; matrix products, arithmetic and copies ran while one was open for 9% of the time, Pallas kernels for 25%

profile of v5, /device:TPU:0, one launch (start us, length us, event | category | flops | bytes accessed | tf_op | source)
XLA Modules:
  0.0 483.7 jit_solution(15747582058363275042)
XLA Ops:
  15.8 3.1 collective-permute-start
  18.9 2.6 collective-permute-start.1
  26.2 4.9 %collective-permute-done.9 = bf16[2,24,1536]{2,1,0:T(8,128)(2,1)S(1)} collective-permute-done((bf16[2,24,1536]{2,1,0:T(8,128)(2,1)S(1)}, bf16[2,24,1536]{2,1,0:T(8,128)(2,1)S(1)}, u32[]{:S(2)}, u32[]{:S(2)}) %collective-permute-start.9) | collective-permute-done | bytes 147488 | tf_op jit(solution)/shard_map/ppermute | solution.py:705
  31.2 4.3 collective-permute-start.2
  35.4 10.9 %collective-permute-done.8 = bf16[2,24,1536]{2,1,0:T(8,128)(2,1)S(1)} collective-permute-done((bf16[2,24,1536]{2,1,0:T(8,128)(2,1)S(1)}, bf16[2,24,1536]{2,1,0:T(8,128)(2,1)S(1)}, u32[]{:S(2)}, u32[]{:S(2)}) %collective-permute-start.8) | collective-permute-done | bytes 147488 | tf_op jit(solution)/shard_map/ppermute | solution.py:705
  56.6 8.3 %collective-permute-done.4 = bf16[2,32,768]{2,1,0:T(8,128)(2,1)S(1)} collective-permute-done((bf16[2,32,768]{2,1,0:T(8,128)(2,1)S(1)}, bf16[2,32,768]{2,1,0:T(8,128)(2,1)S(1)}, u32[]{:S(2)}, u32[]{:S(2)}) %collective-permute-start.4) | collective-permute-done | bytes 98336 | tf_op jit(solution)/shard_map/ppermute | solution.py:705
  71.8 4.0 collective-permute-start.19
  77.1 11.3 %collective-permute-done.18.refs_0_ = bf16[2,24,3072]{2,1,0:T(8,128)(2,1)S(1)} collective-permute-done((bf16[2,24,3072]{2,1,0:T(8,128)(2,1)S(1)}, bf16[2,24,3072]{2,1,0:T(8,128)(2,1)S(1)}, u32[]{:S(2)}, u32[]{:S(2)}) %collective-permute-start.18) | collective-permute-done | bytes 294944 | tf_op jit(solution)/shard_map/ppermute | solution.py:705
  88.4 10.9 %collective-permute-start.20 = (bf16[2,24,3072]{2,1,0:T(8,128)(2,1)S(1)}, bf16[2,24,3072]{2,1,0:T(8,128)(2,1)S(1)}, u32[]{:S(2)}, u32[]{:S(2)}) collective-permute-start(bf16[2,24,3072]{2,1,0:T(8,128)(2,1)S(1)} %get-tuple-element.257), channel_id=1, source_target_pairs={{0,4},{1,5},{2,6},{3,7},{4,0},{5,1},{6,2},{7,3},{8,12},{9,13},{10,... | collective-permute-start | bytes 884744 | tf_op jit(solution)/shard_map/ppermute | solution.py:705
  100.0 6.1 %bias_expand.2.refs_8_.bias_ref = f32[12,208,256]{2,1,0:T(8,128)} custom-call(f32[2,32,768]{2,1,0:T(8,128)} %add_convert_fusion.8.small_ref, bf16[208,224]{1,0:T(8,128)(2,1)} %constant.390.clone.rows_ref, bf16[384,256]{1,0:T(8,128)(2,1)} %constant.391.clone.lanes_ref, bf16[2,24,3072]{2,1,0:T(8,128)(2,1)} %copy-done.23, bf16[2,24,3072]{2,1,0:T(8,128)(2,1)} %copy-done.25), custom_call_target="tpu_custom_call" | custom-call | flops 22000001024 | bytes 70000000 | tf_op jit(solution)/shard_map/bias_expand/pallas_call | solution.py:98
  108.1 5.3 %assemble.2 = (bf16[32,1,24,2304]{3,2,1,0:T(8,128)(2,1)}, bf16[32,1,24,768]{3,2,1,0:T(8,128)(2,1)}) custom-call(s32[4]{0:T(128)} %pad_add_fusion.1.pos_ref, bf16[4,2,24,1536]{3,2,1,0:T(8,128)(2,1)} %copy-done.18, bf16[4,2,24,1536]{3,2,1,0:T(8,128)(2,1)} %copy-done.35, bf16[4,2,24,1536]{3,2,1,0:T(8,128)(2,1)} %copy-done.36, ...), custom_call_target="tpu_custom_call" | custom-call | flops 30799998976 | bytes 98000000 | tf_op jit(solution)/shard_map/assemble/pallas_call | solution.py:789
  115.2 5.1 %collective-permute-done.20 = bf16[2,24,3072]{2,1,0:T(8,128)(2,1)S(1)} collective-permute-done((bf16[2,24,3072]{2,1,0:T(8,128)(2,1)S(1)}, bf16[2,24,3072]{2,1,0:T(8,128)(2,1)S(1)}, u32[]{:S(2)}, u32[]{:S(2)}) %collective-permute-start.20) | collective-permute-done | bytes 294944 | tf_op jit(solution)/shard_map/ppermute | solution.py:705
  123.4 5.8 %qkv.2 = (bf16[416,2304]{1,0:T(8,128)(2,1)}, bf16[416,768]{1,0:T(8,128)(2,1)}) custom-call(f32[416,768]{1,0:T(8,128)} %bitcast_convert_fusion.x_ref, f32[2,32,768]{2,1,0:T(8,128)} %add_convert_fusion.8.small_ref, bf16[768,2304]{1,0:T(8,128)(2,1)} %bitcast.332), custom_call_target="tpu_custom_call" | custom-call | flops 26400000000 | bytes 84000000 | tf_op jit(solution)/shard_map/qkv/pallas_call | solution.py:349
  129.3 8.3 %attention.2 = (bf16[2,208,768]{2,1,0:T(8,128)(2,1)}, f32[2,16,256]{2,1,0:T(8,128)}) custom-call(bf16[2,208,2304]{2,1,0:T(8,128)(2,1)} %bitcast.343, f32[12,208,256]{2,1,0:T(8,128)} %bias_expand.2.refs_8_.bias_ref), custom_call_target="tpu_custom_call" | custom-call | flops 35200000000 | bytes 112000000 | tf_op jit(solution)/shard_map/attention/pallas_call | solution.py:202
  139.4 14.1 %collective-permute-done.21.refs_1_ = bf16[4,2,24,3072]{3,2,1,0:T(8,128)(2,1)S(1)} collective-permute-done((bf16[4,2,24,3072]{3,2,1,0:T(8,128)(2,1)S(1)}, bf16[4,2,24,3072]{3,2,1,0:T(8,128)(2,1)S(1)}, u32[]{:S(2)}, u32[]{:S(2)}) %collective-permute-start.21) | collective-permute-done | bytes 1179680 | tf_op jit(solution)/shard_map/ppermute | solution.py:705
  155.3 6.0 %bias_expand.3.bias_ref = f32[12,208,256]{2,1,0:T(8,128)} custom-call(f32[2,32,768]{2,1,0:T(8,128)} %add_convert_fusion.8.small_ref, bf16[208,224]{1,0:T(8,128)(2,1)} %constant.390.clone.rows_ref, bf16[384,256]{1,0:T(8,128)(2,1)} %constant.391.clone.lanes_ref, f32[2,16,256]{2,1,0:T(8,128)} %get-tuple-element.84.refs_0_.lse_ref), custom_call_target="tpu_custom_call" | custom-call | flops 22000001024 | bytes 70000000 | tf_op jit(solution)/shard_map/bias_expand/pallas_call | solution.py:98
  161.8 8.2 %collective-permute-done.23.refs_3_ = bf16[4,2,24,3072]{3,2,1,0:T(8,128)(2,1)} collective-permute-done((bf16[4,2,24,3072]{3,2,1,0:T(8,128)(2,1)S(1)}, bf16[4,2,24,3072]{3,2,1,0:T(8,128)(2,1)}, u32[]{:S(2)}, u32[]{:S(2)}) %collective-permute-start.23) | collective-permute-done | bytes 1179680 | tf_op jit(solution)/shard_map/ppermute | solution.py:705
  170.0 4.5 unpack.1
  174.6 8.2 %assemble.3 = (bf16[32,1,24,3072]{3,2,1,0:T(8,128)(2,1)}, bf16[32,4,24,768]{3,2,1,0:T(8,128)(2,1)}) custom-call(s32[4]{0:T(128)} %pad_add_fusion.1.pos_ref, bf16[4,2,24,3072]{3,2,1,0:T(8,128)(2,1)} %copy-done.11, bf16[4,2,24,3072]{3,2,1,0:T(8,128)(2,1)} %copy-done.12, bf16[4,2,24,3072]{3,2,1,0:T(8,128)(2,1)} %copy-done.34, ...), custom_call_target="tpu_custom_call" | custom-call | flops 30799998976 | bytes 98000000 | tf_op jit(solution)/shard_map/assemble/pallas_call | solution.py:789
  182.8 15.6 %mlp.2 = (f32[416,768]{1,0:T(8,128)}, f32[416,768]{1,0:T(8,128)}, f32[416,768]{1,0:T(8,128)}, f32[416,768]{1,0:T(8,128)}, bf16[416,768]{1,0:T(8,128)(2,1)}, /*in...) custom-call(f32[416,768]{1,0:T(8,128)} %bitcast_convert_fusion.x_ref, bf16[416,768]{1,0:T(8,128)(2,1)} %bitcast.341, ...), custom_call_target="tpu_custom_call" | custom-call | flops 65999998976 | bytes 210000000 | tf_op jit(solution)/shard_map/mlp/pallas_call | solution.py:486
  198.5 5.9 %qkv.3 = (bf16[416,2304]{1,0:T(8,128)(2,1)}, bf16[416,768]{1,0:T(8,128)(2,1)}) custom-call(f32[416,768]{1,0:T(8,128)} %get-tuple-element.88.x_ref, f32[2,32,768]{2,1,0:T(8,128)} %add_convert_fusion.8.small_ref, bf16[768,9216]{1,0:T(8,128)(2,1)} %all-gather.2.cloned.1.call-done.w_ref.wp_ref.w1_ref), custom_call_target="tpu_custom_call" | custom-call | flops 26400000000 | bytes 84000000 | tf_op jit(solution)/shard_map/qkv/pallas_call | solution.py:349
  204.3 8.5 %attention.3 = (bf16[2,208,768]{2,1,0:T(8,128)(2,1)}, f32[2,16,256]{2,1,0:T(8,128)}) custom-call(bf16[2,208,2304]{2,1,0:T(8,128)(2,1)} %bitcast.345, f32[12,208,256]{2,1,0:T(8,128)} %bias_expand.3.bias_ref), custom_call_target="tpu_custom_call" | custom-call | flops 35200000000 | bytes 112000000 | tf_op jit(solution)/shard_map/attention/pallas_call | solution.py:202
  212.8 15.5 %mlp.3 = (f32[416,768]{1,0:T(8,128)}, f32[416,768]{1,0:T(8,128)}, f32[416,768]{1,0:T(8,128)}, f32[416,768]{1,0:T(8,128)}, bf16[416,768]{1,0:T(8,128)(2,1)}, /*in...) custom-call(f32[416,768]{1,0:T(8,128)} %get-tuple-element.88.x_ref, bf16[416,768]{1,0:T(8,128)(2,1)} %bitcast.353, ...), custom_call_target="tpu_custom_call" | custom-call | flops 65999998976 | bytes 210000000 | tf_op jit(solution)/shard_map/mlp/pallas_call | solution.py:486
  228.3 20.3 %mlp_grad.2 = (bf16[768,3456]{1,0:T(8,128)(2,1)}, bf16[768,3456]{1,0:T(8,128)(2,1)}, f32[416,768]{1,0:T(8,128)}, bf16[416,768]{1,0:T(8,128)(2,1)}, f32[16,768]{1,0:T(8,128)}) custom-call(s32[1]{0:T(128)} %bitcast.7.core_ref, f32[416,768]{1,0:T(8,128)} %convert_select_fusion.g_ref, f32[416,768]{1,0:T(8,128)} %get-tuple-element.94.mid_ref, ...), custom_call_target="tpu_custom_call" | custom-call | flops 88000004096 | bytes 280000000 | tf_op jit(solution)/shard_map/mlp_grad/pallas_call | solution.py:646
  250.9 12.2 %attention_grad.2 = (bf16[2,208,2304]{2,1,0:T(8,128)(2,1)}, f32[12,208,256]{2,1,0:T(8,128)}) custom-call(bf16[2,208,2304]{2,1,0:T(8,128)(2,1)} %bitcast.346, f32[12,208,256]{2,1,0:T(8,128)} %bias_expand.3.bias_ref, f32[2,16,256]{2,1,0:T(8,128)} %get-tuple-element.93.lse_ref, bf16[2,208,768]{2,1,0:T(8,128)(2,1)} %bitcast.351), custom_call_target="tpu_custom_call" | custom-call | flops 52800000000 | bytes 168000000 | tf_op jit(solution)/shard_map/attention_grad/pallas_call | solution.py:268
  263.0 4.0 constant_dynamic-slice_fusion.20
  271.8 11.3 %qkv_grad.2 = (bf16[768,1152]{1,0:T(8,128)(2,1)}, bf16[768,1152]{1,0:T(8,128)(2,1)}, f32[416,768]{1,0:T(8,128)}, f32[8,768]{1,0:T(8,128)}) custom-call(s32[1]{0:T(128)} %bitcast.7.core_ref, bf16[416,2304]{1,0:T(8,128)(2,1)} %bitcast.348, bf16[416,768]{1,0:T(8,128)(2,1)} %get-tuple-element.102.h_ref, f32[416,768]{1,0:T(8,128)} %get-tuple-element.88.x_ref, ...), custom_call_target="tpu_custom_call" | custom-call | flops 48399998976 | bytes 154000000 | tf_op jit(solution)/shard_map/qkv_grad/pallas_call | solution.py:417
  283.2 4.1 collective-permute-done.29.refs_0_
  289.4 20.4 %mlp_grad.3 = (bf16[768,3456]{1,0:T(8,128)(2,1)}, bf16[768,3456]{1,0:T(8,128)(2,1)}, f32[416,768]{1,0:T(8,128)}, bf16[416,768]{1,0:T(8,128)(2,1)}, f32[16,768]{1,0:T(8,128)}) custom-call(s32[1]{0:T(128)} %bitcast.7.core_ref, f32[416,768]{1,0:T(8,128)} %get-tuple-element.105.g_ref, f32[416,768]{1,0:T(8,128)} %get-tuple-element.106.mid_ref, ...), custom_call_target="tpu_custom_call" | custom-call | flops 88000004096 | bytes 280000000 | tf_op jit(solution)/shard_map/mlp_grad/pallas_call | solution.py:646
  315.1 6.1 %collective-permute-done.33.refs_1_ = bf16[4,2,24,1152]{3,2,1,0:T(8,128)(2,1)S(1)} collective-permute-done((bf16[4,2,24,1152]{3,2,1,0:T(8,128)(2,1)S(1)}, bf16[4,2,24,1152]{3,2,1,0:T(8,128)(2,1)S(1)}, u32[]{:S(2)}, u32[]{:S(2)}) %collective-permute-start.33) | collective-permute-done | bytes 442400 | tf_op jit(solution)/shard_map/ppermute | solution.py:705
  322.8 11.5 %attention_grad.3 = (bf16[2,208,2304]{2,1,0:T(8,128)(2,1)}, f32[12,208,256]{2,1,0:T(8,128)}) custom-call(bf16[2,208,2304]{2,1,0:T(8,128)(2,1)} %bitcast.344, f32[12,208,256]{2,1,0:T(8,128)} %bias_expand.2.refs_8_.bias_ref, f32[2,16,256]{2,1,0:T(8,128)} %get-tuple-element.84.refs_0_.lse_ref, bf16[2,208,768]{2,1,0:T(8,128)(2,1)} %bitcast.352, ...), custom_call_target="tpu_custom_call" | custom-call | flops 52800000000 | bytes 168000000 | tf_op jit(solution)/shard_map/attention_grad/pallas_call | solution.py:268
  338.8 3.0 constant_dynamic-slice_fusion.10
  346.5 2.3 collective-permute-start.37
  352.4 8.0 %collective-permute-done.35.refs_2_ = bf16[4,2,24,3456]{3,2,1,0:T(8,128)(2,1)S(1)} collective-permute-done((bf16[4,2,24,3456]{3,2,1,0:T(8,128)(2,1)S(1)}, bf16[4,2,24,3456]{3,2,1,0:T(8,128)(2,1)S(1)}, u32[]{:S(2)}, u32[]{:S(2)}) %collective-permute-start.35) | collective-permute-done | bytes 1327136 | tf_op jit(solution)/shard_map/ppermute | solution.py:705
  362.9 11.2 %qkv_grad.3 = (bf16[768,1152]{1,0:T(8,128)(2,1)}, bf16[768,1152]{1,0:T(8,128)(2,1)}, f32[416,768]{1,0:T(8,128)}, f32[8,768]{1,0:T(8,128)}) custom-call(s32[1]{0:T(128)} %bitcast.7.core_ref, bf16[416,2304]{1,0:T(8,128)(2,1)} %bitcast.347, bf16[416,768]{1,0:T(8,128)(2,1)} %get-tuple-element.118.h_ref, f32[416,768]{1,0:T(8,128)} %bitcast_convert_fusion.x_ref, ...), custom_call_target="tpu_custom_call" | custom-call | flops 48399998976 | bytes 154000000 | tf_op jit(solution)/shard_map/qkv_grad/pallas_call | solution.py:417
  374.2 6.4 %bias_reduce.2.refs_0_.refs_5_ = f32[12,1,768]{2,1,0:T(1,128)} custom-call(f32[12,208,256]{2,1,0:T(8,128)} %get-tuple-element.131.g_ref, bf16[224,208]{1,0:T(8,128)(2,1)} %constant.392.clone.rows_ref, bf16[256,384]{1,0:T(8,128)(2,1)} %constant.393.clone.lanes_ref, f32[8,768]{1,0:T(8,128)} %get-tuple-element.128.refs_0_, ...), custom_call_target="tpu_custom_call" | custom-call | flops 26400000000 | bytes 84000000 | tf_op jit(solution)/shard_map/bias_reduce/pallas_call | solution.py:151
  380.5 5.6 %collective-permute-done.44 = bf16[4,2,24,3456]{3,2,1,0:T(8,128)(2,1)} collective-permute-done((bf16[4,2,24,3456]{3,2,1,0:T(8,128)(2,1)}, bf16[4,2,24,3456]{3,2,1,0:T(8,128)(2,1)}, u32[]{:S(2)}, u32[]{:S(2)}) %collective-permute-start.44) | collective-permute-done | bytes 1327136 | tf_op jit(solution)/shard_map/ppermute | solution.py:705
  387.4 2.3 fusion
  393.7 2.4 collective-permute-start.48
  396.1 6.5 %bias_reduce.3.refs_2_ = f32[12,1,768]{2,1,0:T(1,128)} custom-call(f32[12,208,256]{2,1,0:T(8,128)} %get-tuple-element.130.g_ref, bf16[224,208]{1,0:T(8,128)(2,1)} %constant.392.clone.rows_ref, bf16[256,384]{1,0:T(8,128)(2,1)} %constant.393.clone.lanes_ref, f32[12,1,768]{2,1,0:T(1,128)} %bias_reduce.2.refs_0_.refs_5_, ...), custom_call_target="tpu_custom_call" | custom-call | flops 26400000000 | bytes 84000000 | tf_op jit(solution)/shard_map/bias_reduce/pallas_call | solution.py:151
  406.2 6.1 %collective-permute-done.42.refs_6_ = bf16[4,2,24,1152]{3,2,1,0:T(8,128)(2,1)S(1)} collective-permute-done((bf16[4,2,24,1152]{3,2,1,0:T(8,128)(2,1)S(1)}, bf16[4,2,24,1152]{3,2,1,0:T(8,128)(2,1)S(1)}, u32[]{:S(2)}, u32[]{:S(2)}) %collective-permute-start.42) | collective-permute-done | bytes 442400 | tf_op jit(solution)/shard_map/ppermute | solution.py:705
  414.6 3.2 collective-permute-done.43.refs_7_
  424.1 2.4 reshape.300
  429.5 2.5 collective-permute-start.47
  439.2 3.9 collective-permute-start.54
  443.1 5.1 %collective-permute-done.59 = bf16[2,24,1152]{2,1,0:T(8,128)(2,1)S(1)} collective-permute-done((bf16[2,24,1152]{2,1,0:T(8,128)(2,1)S(1)}, bf16[2,24,1152]{2,1,0:T(8,128)(2,1)S(1)}, u32[]{:S(2)}, u32[]{:S(2)}) %collective-permute-start.59) | collective-permute-done | bytes 110624 | tf_op jit(solution)/shard_map/ppermute | solution.py:705
  449.6 4.2 collective-permute-done.49
  458.3 2.4 collective-permute-start.56
  (348 shorter events, 118.6 us)
Async XLA Ops:
  7.2 162.8 %all-gather.2.cloned.1.call-start = ((), (), s32[]{:S(2)}) async-start(), calls=%async_computation | async-start | bytes 14598144 | tf_op jit(solution)/shard_map/all_gather | solution.py:1074
  15.8 32.6 %collective-permute-start = (bf16[2,32,128]{2,1,0:T(8,128)(2,1)}, bf16[2,32,128]{2,1,0:T(8,128)(2,1)S(1)}, u32[]{:S(2)}, u32[]{:S(2)}) collective-permute-start(bf16[2,32,128]{2,1,0:T(8,128)(2,1)} %small_own.1.refs_0_), channel_id=1, source_target_pairs={{0,2},{1,3},{2,4},{3,5},{4,6},{5,7},{6,0},{7,1},{8,10},{9,11},{10,... | collective-permute-start | bytes 49160 | tf_op jit(solution)/shard_map/ppermute | solution.py:705
  18.9 29.6 %collective-permute-start.1 = (bf16[2,32,128]{2,1,0:T(8,128)(2,1)}, bf16[2,32,128]{2,1,0:T(8,128)(2,1)S(1)}, u32[]{:S(2)}, u32[]{:S(2)}) collective-permute-start(bf16[2,32,128]{2,1,0:T(8,128)(2,1)} %small_own.1.refs_0_), channel_id=1, source_target_pairs={{0,4},{1,5},{2,6},{3,7},{4,0},{5,1},{6,2},{7,3},{8,12},{9,13},{10,... | collective-permute-start | bytes 49160 | tf_op jit(solution)/shard_map/ppermute | solution.py:705
  24.3 22.0 %collective-permute-start.8 = (bf16[2,24,1536]{2,1,0:T(8,128)(2,1)S(1)}, bf16[2,24,1536]{2,1,0:T(8,128)(2,1)S(1)}, u32[]{:S(2)}, u32[]{:S(2)}) collective-permute-start(bf16[2,24,1536]{2,1,0:T(8,128)(2,1)S(1)} %get-tuple-element.267), channel_id=1, source_target_pairs={{0,4},{1,5},{2,6},{3,7},{4,0},{5,1},{6,2},{7,3},{8,12},{9,13},{10,... | collective-permute-start | bytes 442376 | tf_op jit(solution)/shard_map/ppermute | solution.py:705
  24.5 21.8 %collective-permute-start.7 = (bf16[2,24,1536]{2,1,0:T(8,128)(2,1)S(1)}, bf16[2,24,1536]{2,1,0:T(8,128)(2,1)S(1)}, u32[]{:S(2)}, u32[]{:S(2)}) collective-permute-start(bf16[2,24,1536]{2,1,0:T(8,128)(2,1)S(1)} %get-tuple-element.267), channel_id=1, source_target_pairs={{0,2},{1,3},{2,4},{3,5},{4,6},{5,7},{6,0},{7,1},{8,10},{9,11},{10,... | collective-permute-start | bytes 442376 | tf_op jit(solution)/shard_map/ppermute | solution.py:705
  31.2 17.3 %collective-permute-start.2 = (bf16[2,32,128]{2,1,0:T(8,128)(2,1)S(1)}, bf16[2,32,128]{2,1,0:T(8,128)(2,1)S(1)}, u32[]{:S(2)}, u32[]{:S(2)}) collective-permute-start(bf16[2,32,128]{2,1,0:T(8,128)(2,1)S(1)} %copy-done.42), channel_id=1, source_target_pairs={{0,6},{1,7},{2,0},{3,1},{4,2},{5,3},{6,4},{7,5},{8,14},{9,15},{10,... | collective-permute-start | bytes 49160 | tf_op jit(solution)/shard_map/ppermute | solution.py:705
  46.4 25.4 %collective-permute-start.17 = (bf16[24,3072]{1,0:T(8,128)(2,1)S(1)}, bf16[24,3072]{1,0:T(8,128)(2,1)S(1)}, u32[]{:S(2)}, u32[]{:S(2)}) collective-permute-start(bf16[24,3072]{1,0:T(8,128)(2,1)S(1)} %constant_dynamic-update-slice_fusion.4), channel_id=1, source_target_pairs={{0,8},{1,9},{2,10},{3,11},{4,12},{5,13},{6,14},{7,15},{8,0},{9,1},... | collective-permute-start | bytes 442376 | tf_op jit(solution)/shard_map/ppermute | solution.py:705
  46.5 24.2 %collective-permute-start.10 = (bf16[4,2,24,1536]{3,2,1,0:T(8,128)(2,1)S(1)}, bf16[4,2,24,1536]{3,2,1,0:T(8,128)(2,1)S(1)}, u32[]{:S(2)}, u32[]{:S(2)}) collective-permute-start(bf16[4,2,24,1536]{3,2,1,0:T(8,128)(2,1)S(1)} %pad_maximum_fusion.refs_0_), channel_id=1, source_target_pairs={{0,1},{1,0},{2,3},{3,2},{4,5},{5,4},{6,7},{7,6},{8,24},{9,25},{10,... | collective-permute-start | bytes 1769480 | tf_op jit(solution)/shard_map/ppermute | solution.py:705
  53.9 11.1 %collective-permute-start.4 = (bf16[2,32,768]{2,1,0:T(8,128)(2,1)S(1)}, bf16[2,32,768]{2,1,0:T(8,128)(2,1)S(1)}, u32[]{:S(2)}, u32[]{:S(2)}) collective-permute-start(bf16[2,32,768]{2,1,0:T(8,128)(2,1)S(1)} %add.715), channel_id=1, source_target_pairs={{0,1},{1,0},{2,3},{3,2},{4,5},{5,4},{6,7},{7,6},{8,9},{9,8},{10,11... | collective-permute-start | bytes 294920 | tf_op jit(solution)/shard_map/ppermute | solution.py:705
  65.0 11.4 %collective-permute-start.5 = (bf16[2,32,768]{2,1,0:T(8,128)(2,1)S(1)}, bf16[2,32,768]{2,1,0:T(8,128)(2,1)S(1)}, u32[]{:S(2)}, u32[]{:S(2)}) collective-permute-start(bf16[2,32,768]{2,1,0:T(8,128)(2,1)S(1)} %add.716), channel_id=1, source_target_pairs={{0,16},{1,17},{2,18},{3,19},{4,20},{5,21},{6,22},{7,23},{8,24},{9,... | collective-permute-start | bytes 294920 | tf_op jit(solution)/shard_map/ppermute | solution.py:705
  66.0 33.2 %collective-permute-start.11 = (bf16[4,2,24,1536]{3,2,1,0:T(8,128)(2,1)S(1)}, bf16[4,2,24,1536]{3,2,1,0:T(8,128)(2,1)S(1)}, u32[]{:S(2)}, u32[]{:S(2)}) collective-permute-start(bf16[4,2,24,1536]{3,2,1,0:T(8,128)(2,1)S(1)} %pad_maximum_fusion.refs_0_), channel_id=1, source_target_pairs={{0,16},{1,17},{2,18},{3,19},{4,20},{5,21},{6,22},{7,23},{8,9},{9,8... | collective-permute-start | bytes 1769480 | tf_op jit(solution)/shard_map/ppermute | solution.py:705
  70.7 29.1 %collective-permute-start.12 = (bf16[4,2,24,1536]{3,2,1,0:T(8,128)(2,1)S(1)}, bf16[4,2,24,1536]{3,2,1,0:T(8,128)(2,1)S(1)}, u32[]{:S(2)}, u32[]{:S(2)}) collective-permute-start(bf16[4,2,24,1536]{3,2,1,0:T(8,128)(2,1)S(1)} %collective-permute-done.10.refs_1_), channel_id=1, source_target_pairs={{0,16},{1,17},{2,18},{3,19},{4,20},{5,21},{6,22},{7,23},{8,9},{9,8... | collective-permute-start | bytes 1769480 | tf_op jit(solution)/shard_map/ppermute | solution.py:705
  71.8 16.6 %collective-permute-start.18 = (bf16[2,24,3072]{2,1,0:T(8,128)(2,1)S(1)}, bf16[2,24,3072]{2,1,0:T(8,128)(2,1)S(1)}, u32[]{:S(2)}, u32[]{:S(2)}) collective-permute-start(bf16[2,24,3072]{2,1,0:T(8,128)(2,1)S(1)} %get-tuple-element.257), channel_id=1, source_target_pairs={{0,2},{1,3},{2,4},{3,5},{4,6},{5,7},{6,0},{7,1},{8,10},{9,11},{10,... | collective-permute-start | bytes 884744 | tf_op jit(solution)/shard_map/ppermute | solution.py:705
  71.8 27.4 %collective-permute-start.19 = (bf16[2,24,3072]{2,1,0:T(8,128)(2,1)S(1)}, bf16[2,24,3072]{2,1,0:T(8,128)(2,1)S(1)}, u32[]{:S(2)}, u32[]{:S(2)}) collective-permute-start(bf16[2,24,3072]{2,1,0:T(8,128)(2,1)S(1)} %get-tuple-element.257), channel_id=1, source_target_pairs={{0,6},{1,7},{2,0},{3,1},{4,2},{5,3},{6,4},{7,5},{8,14},{9,15},{10,... | collective-permute-start | bytes 884744 | tf_op jit(solution)/shard_map/ppermute | solution.py:705
  76.4 29.7 %collective-permute-start.13 = (bf16[4,2,24,1536]{3,2,1,0:T(8,128)(2,1)S(1)}, bf16[4,2,24,1536]{3,2,1,0:T(8,128)(2,1)S(1)}, u32[]{:S(2)}, u32[]{:S(2)}) collective-permute-start(bf16[4,2,24,1536]{3,2,1,0:T(8,128)(2,1)S(1)} %pad_maximum_fusion.refs_0_), channel_id=1, source_target_pairs={{0,8},{1,9},{2,10},{3,11},{4,12},{5,13},{6,14},{7,15},{8,0},{9,1},... | collective-permute-start | bytes 1769480 | tf_op jit(solution)/shard_map/ppermute | solution.py:705
  88.4 32.0 %collective-permute-start.20 = (bf16[2,24,3072]{2,1,0:T(8,128)(2,1)S(1)}, bf16[2,24,3072]{2,1,0:T(8,128)(2,1)S(1)}, u32[]{:S(2)}, u32[]{:S(2)}) collective-permute-start(bf16[2,24,3072]{2,1,0:T(8,128)(2,1)S(1)} %get-tuple-element.257), channel_id=1, source_target_pairs={{0,4},{1,5},{2,6},{3,7},{4,0},{5,1},{6,2},{7,3},{8,12},{9,13},{10,... | collective-permute-start | bytes 884744 | tf_op jit(solution)/shard_map/ppermute | solution.py:705
  120.5 33.0 %collective-permute-start.21 = (bf16[4,2,24,3072]{3,2,1,0:T(8,128)(2,1)S(1)}, bf16[4,2,24,3072]{3,2,1,0:T(8,128)(2,1)S(1)}, u32[]{:S(2)}, u32[]{:S(2)}) collective-permute-start(bf16[4,2,24,3072]{3,2,1,0:T(8,128)(2,1)S(1)} %maximum_add_fusion.refs_0_), channel_id=1, source_target_pairs={{0,1},{1,0},{2,3},{3,2},{4,5},{5,4},{6,7},{7,6},{8,24},{9,25},{10,... | collective-permute-start | bytes 3538952 | tf_op jit(solution)/shard_map/ppermute | solution.py:705
  121.7 39.6 %collective-permute-start.22 = (bf16[4,2,24,3072]{3,2,1,0:T(8,128)(2,1)S(1)}, bf16[4,2,24,3072]{3,2,1,0:T(8,128)(2,1)S(1)}, u32[]{:S(2)}, u32[]{:S(2)}) collective-permute-start(bf16[4,2,24,3072]{3,2,1,0:T(8,128)(2,1)S(1)} %maximum_add_fusion.refs_0_), channel_id=1, source_target_pairs={{0,16},{1,17},{2,18},{3,19},{4,20},{5,21},{6,22},{7,23},{8,9},{9,8... | collective-permute-start | bytes 3538952 | tf_op jit(solution)/shard_map/ppermute | solution.py:705
  123.4 51.1 %collective-permute-start.24 = (bf16[4,2,24,3072]{3,2,1,0:T(8,128)(2,1)S(1)}, bf16[4,2,24,3072]{3,2,1,0:T(8,128)(2,1)}, u32[]{:S(2)}, u32[]{:S(2)}) collective-permute-start(bf16[4,2,24,3072]{3,2,1,0:T(8,128)(2,1)S(1)} %maximum_add_fusion.refs_0_), channel_id=1, source_target_pairs={{0,8},{1,9},{2,10},{3,11},{4,12},{5,13},{6,14},{7,15},{8,0},{9,1},... | collective-permute-start | bytes 3538952 | tf_op jit(solution)/shard_map/ppermute | solution.py:705
  153.6 16.4 %collective-permute-start.23 = (bf16[4,2,24,3072]{3,2,1,0:T(8,128)(2,1)S(1)}, bf16[4,2,24,3072]{3,2,1,0:T(8,128)(2,1)}, u32[]{:S(2)}, u32[]{:S(2)}) collective-permute-start(bf16[4,2,24,3072]{3,2,1,0:T(8,128)(2,1)S(1)} %broadcast_add_fusion), channel_id=1, source_target_pairs={{0,16},{1,17},{2,18},{3,19},{4,20},{5,21},{6,22},{7,23},{8,9},{9,8... | collective-permute-start | bytes 3538952 | tf_op jit(solution)/shard_map/ppermute | solution.py:705
  161.3 13.3 %collective-permute-start.25 = (bf16[4,2,24,3072]{3,2,1,0:T(8,128)(2,1)S(1)}, bf16[4,2,24,3072]{3,2,1,0:T(8,128)(2,1)}, u32[]{:S(2)}, u32[]{:S(2)}) collective-permute-start(bf16[4,2,24,3072]{3,2,1,0:T(8,128)(2,1)S(1)} %collective-permute-done.21.refs_1_), channel_id=1, source_target_pairs={{0,8},{1,9},{2,10},{3,11},{4,12},{5,13},{6,14},{7,15},{8,0},{9,1},... | collective-permute-start | bytes 3538952 | tf_op jit(solution)/shard_map/ppermute | solution.py:705
  161.3 13.3 %collective-permute-start.26 = (bf16[4,2,24,3072]{3,2,1,0:T(8,128)(2,1)S(1)}, bf16[4,2,24,3072]{3,2,1,0:T(8,128)(2,1)}, u32[]{:S(2)}, u32[]{:S(2)}) collective-permute-start(bf16[4,2,24,3072]{3,2,1,0:T(8,128)(2,1)S(1)} %collective-permute-done.22.refs_2_), channel_id=1, source_target_pairs={{0,8},{1,9},{2,10},{3,11},{4,12},{5,13},{6,14},{7,15},{8,0},{9,1},... | collective-permute-start | bytes 3538952 | tf_op jit(solution)/shard_map/ppermute | solution.py:705
  248.6 14.4 %collective-permute-start.28 = (bf16[768,3456]{1,0:T(8,128)(2,1)}, bf16[768,3456]{1,0:T(8,128)(2,1)}, u32[]{:S(2)}, u32[]{:S(2)}) collective-permute-start(bf16[768,3456]{1,0:T(8,128)(2,1)} %get-tuple-element.104), channel_id=1, source_target_pairs={{0,8},{1,9},{2,10},{3,11},{4,12},{5,13},{6,14},{7,15},{8,0},{9,1},... | collective-permute-start | bytes 15925256 | tf_op jit(solution)/shard_map/ppermute | solution.py:705
  269.3 18.0 %collective-permute-start.29 = (bf16[4,2,24,3456]{3,2,1,0:T(8,128)(2,1)S(1)}, bf16[4,2,24,3456]{3,2,1,0:T(8,128)(2,1)}, u32[]{:S(2)}, u32[]{:S(2)}) collective-permute-start(bf16[4,2,24,3456]{3,2,1,0:T(8,128)(2,1)S(1)} %fusion.4), channel_id=1, source_target_pairs={{0,16},{1,17},{2,18},{3,19},{4,20},{5,21},{6,22},{7,23},{8,9},{9,8... | collective-permute-start | bytes 3981320 | tf_op jit(solution)/shard_map/ppermute | solution.py:705
  271.3 51.5 %collective-permute-start.30 = (bf16[4,2,24,3456]{3,2,1,0:T(8,128)(2,1)S(1)}, bf16[4,2,24,3456]{3,2,1,0:T(8,128)(2,1)}, u32[]{:S(2)}, u32[]{:S(2)}) collective-permute-start(bf16[4,2,24,3456]{3,2,1,0:T(8,128)(2,1)S(1)} %fusion.5), channel_id=1, source_target_pairs={{0,16},{1,17},{2,18},{3,19},{4,20},{5,21},{6,22},{7,23},{8,9},{9,8... | collective-permute-start | bytes 3981320 | tf_op jit(solution)/shard_map/ppermute | solution.py:705
  283.1 27.3 %collective-permute-start.31 = (bf16[768,1152]{1,0:T(8,128)(2,1)}, bf16[768,1152]{1,0:T(8,128)(2,1)S(1)}, u32[]{:S(2)}, u32[]{:S(2)}) collective-permute-start(bf16[768,1152]{1,0:T(8,128)(2,1)} %get-tuple-element.116), channel_id=1, source_target_pairs={{0,8},{1,9},{2,10},{3,11},{4,12},{5,13},{6,14},{7,15},{8,0},{9,1},... | collective-permute-start | bytes 5308424 | tf_op jit(solution)/shard_map/ppermute | solution.py:705
  289.1 46.0 %collective-permute-start.32 = (bf16[4,2,24,3456]{3,2,1,0:T(8,128)(2,1)S(1)}, bf16[4,2,24,3456]{3,2,1,0:T(8,128)(2,1)S(1)}, u32[]{:S(2)}, u32[]{:S(2)}) collective-permute-start(bf16[4,2,24,3456]{3,2,1,0:T(8,128)(2,1)S(1)} %fusion.3), channel_id=1, source_target_pairs={{0,1},{1,0},{2,3},{3,2},{4,5},{5,4},{6,7},{7,6},{8,24},{9,25},{10,... | collective-permute-start | bytes 3981320 | tf_op jit(solution)/shard_map/ppermute | solution.py:705
  309.9 28.9 %collective-permute-start.34 = (bf16[768,3456]{1,0:T(8,128)(2,1)}, bf16[768,3456]{1,0:T(8,128)(2,1)}, u32[]{:S(2)}, u32[]{:S(2)}) collective-permute-start(bf16[768,3456]{1,0:T(8,128)(2,1)} %get-tuple-element.124), channel_id=1, source_target_pairs={{0,8},{1,9},{2,10},{3,11},{4,12},{5,13},{6,14},{7,15},{8,0},{9,1},... | collective-permute-start | bytes 15925256 | tf_op jit(solution)/shard_map/ppermute | solution.py:705
  314.3 20.0 %collective-permute-start.51 = (bf16[4,2,24,1152]{3,2,1,0:T(8,128)(2,1)S(1)}, bf16[4,2,24,1152]{3,2,1,0:T(8,128)(2,1)S(1)}, u32[]{:S(2)}, u32[]{:S(2)}) collective-permute-start(bf16[4,2,24,1152]{3,2,1,0:T(8,128)(2,1)S(1)} %fusion.19), channel_id=1, source_target_pairs={{0,16},{1,17},{2,18},{3,19},{4,20},{5,21},{6,22},{7,23},{8,9},{9,8... | collective-permute-start | bytes 1327112 | tf_op jit(solution)/shard_map/ppermute | solution.py:705
  321.3 13.0 %collective-permute-start.40 = (bf16[4,2,24,1152]{3,2,1,0:T(8,128)(2,1)S(1)}, bf16[4,2,24,1152]{3,2,1,0:T(8,128)(2,1)S(1)}, u32[]{:S(2)}, u32[]{:S(2)}) collective-permute-start(bf16[4,2,24,1152]{3,2,1,0:T(8,128)(2,1)S(1)} %fusion.11), channel_id=1, source_target_pairs={{0,1},{1,0},{2,3},{3,2},{4,5},{5,4},{6,7},{7,6},{8,24},{9,25},{10,... | collective-permute-start | bytes 1327112 | tf_op jit(solution)/shard_map/ppermute | solution.py:705
  342.6 17.8 %collective-permute-start.35 = (bf16[4,2,24,3456]{3,2,1,0:T(8,128)(2,1)S(1)}, bf16[4,2,24,3456]{3,2,1,0:T(8,128)(2,1)S(1)}, u32[]{:S(2)}, u32[]{:S(2)}) collective-permute-start(bf16[4,2,24,3456]{3,2,1,0:T(8,128)(2,1)S(1)} %fusion.6), channel_id=1, source_target_pairs={{0,16},{1,17},{2,18},{3,19},{4,20},{5,21},{6,22},{7,23},{8,9},{9,8... | collective-permute-start | bytes 3981320 | tf_op jit(solution)/shard_map/ppermute | solution.py:705
  345.1 29.0 %collective-permute-start.36 = (bf16[2,24,3456]{2,1,0:T(8,128)(2,1)S(1)}, bf16[2,24,3456]{2,1,0:T(8,128)(2,1)}, u32[]{:S(2)}, u32[]{:S(2)}) collective-permute-start(bf16[2,24,3456]{2,1,0:T(8,128)(2,1)S(1)} %get-tuple-element.217), channel_id=1, source_target_pairs={{0,2},{1,3},{2,4},{3,5},{4,6},{5,7},{6,0},{7,1},{8,10},{9,11},{10,... | collective-permute-start | bytes 995336 | tf_op jit(solution)/shard_map/ppermute | solution.py:705
  346.5 27.7 %collective-permute-start.37 = (bf16[2,24,3456]{2,1,0:T(8,128)(2,1)}, bf16[2,24,3456]{2,1,0:T(8,128)(2,1)}, u32[]{:S(2)}, u32[]{:S(2)}) collective-permute-start(bf16[2,24,3456]{2,1,0:T(8,128)(2,1)} %get-tuple-element.216), channel_id=1, source_target_pairs={{0,4},{1,5},{2,6},{3,7},{4,0},{5,1},{6,2},{7,3},{8,12},{9,13},{10,... | collective-permute-start | bytes 995336 | tf_op jit(solution)/shard_map/ppermute | solution.py:705
  348.8 25.4 %collective-permute-start.38 = (bf16[2,24,3456]{2,1,0:T(8,128)(2,1)S(1)}, bf16[2,24,3456]{2,1,0:T(8,128)(2,1)}, u32[]{:S(2)}, u32[]{:S(2)}) collective-permute-start(bf16[2,24,3456]{2,1,0:T(8,128)(2,1)S(1)} %get-tuple-element.215), channel_id=1, source_target_pairs={{0,6},{1,7},{2,0},{3,1},{4,2},{5,3},{6,4},{7,5},{8,14},{9,15},{10,... | collective-permute-start | bytes 995336 | tf_op jit(solution)/shard_map/ppermute | solution.py:705
  351.9 34.2 %collective-permute-start.44 = (bf16[4,2,24,3456]{3,2,1,0:T(8,128)(2,1)}, bf16[4,2,24,3456]{3,2,1,0:T(8,128)(2,1)}, u32[]{:S(2)}, u32[]{:S(2)}) collective-permute-start(bf16[4,2,24,3456]{3,2,1,0:T(8,128)(2,1)} %fusion.7), channel_id=1, source_target_pairs={{0,16},{1,17},{2,18},{3,19},{4,20},{5,21},{6,22},{7,23},{8,9},{9,8... | collective-permute-start | bytes 3981320 | tf_op jit(solution)/shard_map/ppermute | solution.py:705
  362.2 25.2 %collective-permute-start.39 = (bf16[4,2,24,3456]{3,2,1,0:T(8,128)(2,1)}, bf16[4,2,24,3456]{3,2,1,0:T(8,128)(2,1)}, u32[]{:S(2)}, u32[]{:S(2)}) collective-permute-start(bf16[4,2,24,3456]{3,2,1,0:T(8,128)(2,1)} %fusion.1), channel_id=1, source_target_pairs={{0,1},{1,0},{2,3},{3,2},{4,5},{5,4},{6,7},{7,6},{8,24},{9,25},{10,... | collective-permute-start | bytes 3981320 | tf_op jit(solution)/shard_map/ppermute | solution.py:705
  374.1 28.5 %collective-permute-start.41 = (bf16[768,1152]{1,0:T(8,128)(2,1)}, bf16[768,1152]{1,0:T(8,128)(2,1)S(1)}, u32[]{:S(2)}, u32[]{:S(2)}) collective-permute-start(bf16[768,1152]{1,0:T(8,128)(2,1)} %get-tuple-element.135), channel_id=1, source_target_pairs={{0,8},{1,9},{2,10},{3,11},{4,12},{5,13},{6,14},{7,15},{8,0},{9,1},... | collective-permute-start | bytes 5308424 | tf_op jit(solution)/shard_map/ppermute | solution.py:705
  392.2 22.4 %collective-permute-start.45 = (bf16[2,24,3456]{2,1,0:T(8,128)(2,1)S(1)}, bf16[2,24,3456]{2,1,0:T(8,128)(2,1)}, u32[]{:S(2)}, u32[]{:S(2)}) collective-permute-start(bf16[2,24,3456]{2,1,0:T(8,128)(2,1)S(1)} %get-tuple-element.214), channel_id=1, source_target_pairs={{0,2},{1,3},{2,4},{3,5},{4,6},{5,7},{6,0},{7,1},{8,10},{9,11},{10,... | collective-permute-start | bytes 995336 | tf_op jit(solution)/shard_map/ppermute | solution.py:705
  393.7 32.8 %collective-permute-start.48 = (bf16[2,24,3456]{2,1,0:T(8,128)(2,1)}, bf16[2,24,3456]{2,1,0:T(8,128)(2,1)}, u32[]{:S(2)}, u32[]{:S(2)}) collective-permute-start(bf16[2,24,3456]{2,1,0:T(8,128)(2,1)} %get-tuple-element.213), channel_id=1, source_target_pairs={{0,4},{1,5},{2,6},{3,7},{4,0},{5,1},{6,2},{7,3},{8,12},{9,13},{10,... | collective-permute-start | bytes 995336 | tf_op jit(solution)/shard_map/ppermute | solution.py:705
  405.0 12.8 %collective-permute-start.43 = (bf16[4,2,24,1152]{3,2,1,0:T(8,128)(2,1)S(1)}, bf16[4,2,24,1152]{3,2,1,0:T(8,128)(2,1)S(1)}, u32[]{:S(2)}, u32[]{:S(2)}) collective-permute-start(bf16[4,2,24,1152]{3,2,1,0:T(8,128)(2,1)S(1)} %fusion.18), channel_id=1, source_target_pairs={{0,16},{1,17},{2,18},{3,19},{4,20},{5,21},{6,22},{7,23},{8,9},{9,8... | collective-permute-start | bytes 1327112 | tf_op jit(solution)/shard_map/ppermute | solution.py:705
  413.2 18.7 %collective-permute-start.50 = (bf16[4,2,24,1152]{3,2,1,0:T(8,128)(2,1)}, bf16[4,2,24,1152]{3,2,1,0:T(8,128)(2,1)}, u32[]{:S(2)}, u32[]{:S(2)}) collective-permute-start(bf16[4,2,24,1152]{3,2,1,0:T(8,128)(2,1)} %fusion.10), channel_id=1, source_target_pairs={{0,1},{1,0},{2,3},{3,2},{4,5},{5,4},{6,7},{7,6},{8,24},{9,25},{10,... | collective-permute-start | bytes 1327112 | tf_op jit(solution)/shard_map/ppermute | solution.py:705
  421.0 33.6 %collective-permute-start.52 = (bf16[2,24,1152]{2,1,0:T(8,128)(2,1)}, bf16[2,24,1152]{2,1,0:T(8,128)(2,1)}, u32[]{:S(2)}, u32[]{:S(2)}) collective-permute-start(bf16[2,24,1152]{2,1,0:T(8,128)(2,1)} %get-tuple-element.243), channel_id=1, source_target_pairs={{0,2},{1,3},{2,4},{3,5},{4,6},{5,7},{6,0},{7,1},{8,10},{9,11},{10,... | collective-permute-start | bytes 331784 | tf_op jit(solution)/shard_map/ppermute | solution.py:705
  421.6 33.0 %collective-permute-start.53 = (bf16[2,24,1152]{2,1,0:T(8,128)(2,1)}, bf16[2,24,1152]{2,1,0:T(8,128)(2,1)}, u32[]{:S(2)}, u32[]{:S(2)}) collective-permute-start(bf16[2,24,1152]{2,1,0:T(8,128)(2,1)} %get-tuple-element.242), channel_id=1, source_target_pairs={{0,4},{1,5},{2,6},{3,7},{4,0},{5,1},{6,2},{7,3},{8,12},{9,13},{10,... | collective-permute-start | bytes 331784 | tf_op jit(solution)/shard_map/ppermute | solution.py:705
  435.3 12.9 %collective-permute-start.59 = (bf16[2,24,1152]{2,1,0:T(8,128)(2,1)S(1)}, bf16[2,24,1152]{2,1,0:T(8,128)(2,1)S(1)}, u32[]{:S(2)}, u32[]{:S(2)}) collective-permute-start(bf16[2,24,1152]{2,1,0:T(8,128)(2,1)S(1)} %get-tuple-element.240), channel_id=1, source_target_pairs={{0,4},{1,5},{2,6},{3,7},{4,0},{5,1},{6,2},{7,3},{8,12},{9,13},{10,... | collective-permute-start | bytes 331784 | tf_op jit(solution)/shard_map/ppermute | solution.py:705
  439.2 15.4 %collective-permute-start.54 = (bf16[2,24,1152]{2,1,0:T(8,128)(2,1)S(1)}, bf16[2,24,1152]{2,1,0:T(8,128)(2,1)S(1)}, u32[]{:S(2)}, u32[]{:S(2)}) collective-permute-start(bf16[2,24,1152]{2,1,0:T(8,128)(2,1)S(1)} %copy-done.29), channel_id=1, source_target_pairs={{0,6},{1,7},{2,0},{3,1},{4,2},{5,3},{6,4},{7,5},{8,14},{9,15},{10,... | collective-permute-start | bytes 331784 | tf_op jit(solution)/shard_map/ppermute | solution.py:705
  448.2 18.5 %collective-permute-start.63 = (bf16[2,24,3456]{2,1,0:T(8,128)(2,1)}, bf16[2,24,3456]{2,1,0:T(8,128)(2,1)}, u32[]{:S(2)}, u32[]{:S(2)}) collective-permute-start(bf16[2,24,3456]{2,1,0:T(8,128)(2,1)} %get-tuple-element.212), channel_id=1, source_target_pairs={{0,6},{1,7},{2,0},{3,1},{4,2},{5,3},{6,4},{7,5},{8,14},{9,15},{10,... | collective-permute-start | bytes 995336 | tf_op jit(solution)/shard_map/ppermute | solution.py:705
  453.9 17.7 %collective-permute-start.61 = (f32[24,1152]{1,0:T(8,128)}, f32[24,1152]{1,0:T(8,128)}, u32[]{:S(2)}, u32[]{:S(2)}) collective-permute-start(f32[24,1152]{1,0:T(8,128)} %dynamic-slice_bitcast_fusion.3), channel_id=1, source_target_pairs={{0,8},{1,9},{2,10},{3,11},{4,12},{5,13},{6,14},{7,15},{8,0},{9,1},... | collective-permute-start | bytes 331784 | tf_op jit(solution)/shard_map/ppermute | solution.py:705
  457.2 11.2 %collective-permute-start.57 = (f32[2,32,128]{2,1,0:T(8,128)}, f32[2,32,128]{2,1,0:T(8,128)}, u32[]{:S(2)}, u32[]{:S(2)}) collective-permute-start(f32[2,32,128]{2,1,0:T(8,128)} %get-tuple-element.141), channel_id=1, source_target_pairs={{0,6},{1,7},{2,0},{3,1},{4,2},{5,3},{6,4},{7,5},{8,14},{9,15},{10,... | collective-permute-start | bytes 98312 | tf_op jit(solution)/shard_map/ppermute | solution.py:705
  (72 other events, 475.7 us)
Sparse Core Ops, SparseCore 0:
  13.8 143.6 all-gather.1
